TPU v7x, 32 devices: a whole 2x2x4 slice. The times are simulated.
32 devices in a mesh: req: 4 (over z), blk: 8 (over y, x, core).
Axes of the slice: x: 2, y: 2, z: 4, core: 2. Of those that a mesh axis runs over, the one named last changes fastest.
Arguments:
- tree_input: bfloat16 [1536, 1280], P(('req', 'blk')), may hold values from -6 to 6
- cache: bfloat16 [4, 2, 16384, 1280], P('req', None, 'blk'), may hold values from -1200 to 1200, as said below
- page_table: int32 [4, 128], P('req'), may hold values from 0 to 127, each once within a row
- lengths: int32 [4, 8], P('req'), may hold values from 1 to 13440, 14336 in all within a row
- parents: int32 [32, 48], P(('req', 'blk')), may hold values from 0 to 29, as said below
- accept_leaf: int32 [4, 8], P('req'), may hold values from 0 to 47
- w_qkv: bfloat16 [1280, 3840], P(None, 'blk'), may hold values from -0.15625 to 0.15625
- w_out: bfloat16 [1280, 1280], P(None, 'blk'), may hold values from -0.15625 to 0.15625
- w_up: bfloat16 [1280, 1280], P(None, 'blk'), may hold values from -0.15625 to 0.15625
- w_down: bfloat16 [1280, 1280], P('blk'), may hold values from -0.15625 to 0.15625
- w_draft: bfloat16 [4, 1280, 1280], P(None, None, 'blk'), may hold values from -0.15625 to 0.15625
- w_patch: bfloat16 [1280, 1280], P(None, 'req'), may hold values from -0.15625 to 0.15625
Outputs:
- layer_out: bfloat16 [1536, 1280], P(('req', 'blk'))
- drafts: bfloat16 [4, 1536, 1280], P(None, ('req', 'blk'))
- cache_new: bfloat16 [4, 2, 16384, 1280], P('req', None, 'blk')
Inputs may be any that keep to these rules, and one draw needn't show every extreme that they name: `cache`: keys of the pool may hold a few rows of far larger size. `parents`: node 0 is its own parent. The nodes form 5 levels of sizes 1, 4, 10, 15, 18 in index order, and every other node's parent lies in the level before its own. `page_table`: row g holds the pool pages of group g; request r's pages are the npages_r entries after those of requests before it (see the steps), and page p is held by index p // 16 of blk.
All inputs are finite; a program needn't handle non-finite values.
Results may differ from a plain program's by a relative error of at most 0.018.
The roundings to bfloat16 on the way count: a program that leaves them out, or rounds other values in their place, can miss the bound.
Values may be sent and summed in bfloat16 or wider, within the bound.
No kernel may reach another device: no remote copies, remote signals or barrier semaphores. Data moves between devices by JAX's collectives and lax.ppermute only.
A program may use at most 192 MiB of HBM per device.

v0:
```python
import math

import jax
import jax.numpy as jnp
from jax import lax
from jax.sharding import PartitionSpec as P

H = 16
HD = 80
TREE = 48
DEPTH = 5
PAGE = 128


EPS = 1e-06
NEG = -1e30
LEVEL_START = (0, 1, 5, 15, 30, 48)


def rms_rows(values):
    wide = values.astype(jnp.float32)
    return (wide * lax.rsqrt(jnp.mean(wide * wide, axis=-1, keepdims=True) + EPS)).astype(
        jnp.bfloat16
    )


def ancestors(parent_rows):
    nodes = jnp.arange(TREE, dtype=jnp.int32)
    current = jnp.broadcast_to(nodes, parent_rows.shape)
    marks = current[:, :, None] == nodes[None, None, :]
    for level in range(DEPTH - 1):
        current = jnp.take_along_axis(parent_rows, current, axis=1)
        marks = marks | (current[:, :, None] == nodes[None, None, :])
    return marks


def row_blocks(values, mapper):
    return mapper(lax.all_gather(values, "blk", axis=0, tiled=True), jnp.int32(0))


def column_blocks(values):
    return lax.all_to_all(values, "blk", split_axis=0, concat_axis=1, tiled=True)


def on_device(
    tree_input,
    cache,
    page_table,
    lengths,
    parents,
    accept_leaf,
    w_qkv,
    w_out,
    w_up,
    w_down,
    w_draft,
    w_patch,
):
    blocks = lax.axis_size("blk")
    myself = lax.axis_index("blk")
    tree_rows = tree_input.shape[0]
    width = tree_input.shape[1]
    requests = lengths.shape[1]
    pool_pages = cache.shape[2] // PAGE
    scale = 1.0 / math.sqrt(HD)
    normed = rms_rows(tree_input)

    def project_qkv(piece, start):
        return jnp.dot(piece, w_qkv, preferred_element_type=jnp.float32).astype(jnp.bfloat16)

    projected_part = row_blocks(normed, project_qkv)
    projected = column_blocks(projected_part)
    key_own = projected[:, width : 2 * width]
    value_own = projected[:, 2 * width :]
    query_all = lax.all_gather(projected[:, :width], "blk", axis=0, tiled=True)
    page_row = page_table[0]
    length_row = lengths[0]
    leaf_row = accept_leaf[0]
    total_pages = page_row.shape[0]
    npages = (length_row + DEPTH + PAGE - 1) // PAGE
    page_ends = jnp.cumsum(npages)
    offsets = page_ends - npages
    local_ids = myself * pool_pages + jnp.arange(pool_pages, dtype=jnp.int32)
    located = page_row[None, :] == local_ids[:, None]
    where_at = jnp.sum(
        jnp.where(located, jnp.arange(total_pages, dtype=jnp.int32)[None, :], 0), axis=1
    )
    owner = jnp.sum((page_ends[None, :] <= where_at[:, None]).astype(jnp.int32), axis=1)
    owner_hot = owner[:, None] == jnp.arange(requests, dtype=jnp.int32)[None, :]
    safe_owner = jnp.minimum(owner, requests - 1)
    page_len = jnp.sum(jnp.where(owner_hot, length_row[None, :], 0), axis=1)
    page_offset = jnp.sum(jnp.where(owner_hot, offsets[None, :], 0), axis=1)
    positions = (where_at - page_offset)[:, None] * PAGE + jnp.arange(PAGE, dtype=jnp.int32)[
        None, :
    ]
    valid = positions < page_len[:, None]
    query4 = query_all.reshape(requests, tree_rows, H, HD)
    query_page = jnp.take(query4, safe_owner, axis=0)
    keys = cache[0, 0].reshape(pool_pages, PAGE, H, HD)
    values = cache[0, 1].reshape(pool_pages, PAGE, H, HD)
    scores = (
        jnp.einsum("pqhd,pthd->pqht", query_page, keys, preferred_element_type=jnp.float32) * scale
    )
    masked = jnp.where(valid[:, None, None, :], scores, NEG)
    page_max = jnp.max(masked, axis=-1)
    request_max = jnp.max(jnp.where(owner_hot.T[:, :, None, None], page_max[None], NEG), axis=1)
    page_top = jnp.take(request_max, safe_owner, axis=0)
    weights = jnp.where(valid[:, None, None, :], jnp.exp(masked - page_top[..., None]), 0.0)
    page_den = jnp.sum(weights, axis=-1)
    page_num = jnp.einsum(
        "pqht,pthd->pqhd", weights.astype(jnp.bfloat16), values, preferred_element_type=jnp.float32
    )
    hot = owner_hot.astype(jnp.float32)
    den_part = jnp.einsum("pr,pqh->rqh", hot, page_den, precision=lax.Precision.HIGHEST)
    num_part = jnp.einsum("pr,pqhd->rqhd", hot, page_num, precision=lax.Precision.HIGHEST).reshape(
        requests, tree_rows, width
    )
    max_all = lax.pmax(request_max, "blk")
    factor = jnp.exp(request_max - max_all)
    den_scaled = den_part * factor
    num_scaled = (num_part.reshape(requests, tree_rows, H, HD) * factor[..., None]).reshape(
        requests, tree_rows, width
    )
    den_own, num_own = (
        lax.psum_scatter(den_scaled, "blk", scatter_dimension=0, tiled=True),
        lax.psum_scatter(num_scaled, "blk", scatter_dimension=0, tiled=True),
    )
    cache_top = lax.dynamic_slice_in_dim(max_all, myself, 1, 0)[0]
    cache_den = den_own[0]
    cache_num = num_own[0]
    marks = ancestors(parents)[0]
    query_own = lax.dynamic_slice_in_dim(query_all, myself * tree_rows, tree_rows, 0).reshape(
        tree_rows, H, HD
    )
    key_tree = key_own.reshape(tree_rows, H, HD)
    value_tree = value_own.reshape(tree_rows, H, HD)
    tree_scores = (
        jnp.einsum("qhd,khd->qhk", query_own, key_tree, preferred_element_type=jnp.float32) * scale
    )
    tree_masked = jnp.where(marks[:, None, :], tree_scores, NEG)
    row_top = jnp.maximum(cache_top, jnp.max(tree_masked, axis=-1))
    tree_weights = jnp.where(marks[:, None, :], jnp.exp(tree_masked - row_top[..., None]), 0.0)
    carried = jnp.exp(cache_top - row_top)
    denom = cache_den * carried + jnp.sum(tree_weights, axis=-1)
    numer = cache_num.reshape(tree_rows, H, HD) * carried[..., None] + jnp.einsum(
        "qhk,khd->qhd",
        tree_weights.astype(jnp.bfloat16),
        value_tree,
        preferred_element_type=jnp.float32,
    )
    attended = (numer / denom[..., None]).reshape(tree_rows, width).astype(jnp.bfloat16)

    def project_out(piece, start):
        return jnp.dot(piece, w_out, preferred_element_type=jnp.float32).astype(jnp.bfloat16)

    proj = column_blocks(row_blocks(attended, project_out))
    mid = (tree_input.astype(jnp.float32) + proj.astype(jnp.float32)).astype(jnp.bfloat16)

    def project_up(piece, start):
        return jax.nn.gelu(jnp.dot(piece, w_up, preferred_element_type=jnp.float32)).astype(
            jnp.bfloat16
        )

    hidden_all = row_blocks(rms_rows(mid), project_up)
    feedforward = lax.psum_scatter(
        jnp.dot(hidden_all, w_down, preferred_element_type=jnp.float32),
        "blk",
        scatter_dimension=0,
        tiled=True,
    )
    layer_out = (mid.astype(jnp.float32) + feedforward).astype(jnp.bfloat16)
    head_count = w_draft.shape[0]
    head_cols = w_draft.shape[2]

    def project_draft(piece, start):
        grown = jnp.einsum("nd,kdc->nkc", piece, w_draft, preferred_element_type=jnp.float32)
        return (
            jax.nn.silu(grown).astype(jnp.bfloat16).reshape(piece.shape[0], head_count * head_cols)
        )

    branch = column_blocks(row_blocks(rms_rows(layer_out), project_draft))
    branch = (
        branch.reshape(tree_rows, blocks, head_count, head_cols)
        .transpose(2, 0, 1, 3)
        .reshape(head_count, tree_rows, width)
    )
    drafted = (layer_out.astype(jnp.float32)[None] + branch.astype(jnp.float32)).astype(
        jnp.bfloat16
    )
    drafts = jnp.einsum(
        "krd,do->kro",
        drafted,
        lax.all_gather(w_patch, "req", axis=1, tiled=True),
        preferred_element_type=jnp.float32,
    ).astype(jnp.bfloat16)
    my_leaf = lax.dynamic_slice_in_dim(leaf_row, myself, 1, 0)
    chosen = jnp.take(marks, my_leaf, axis=0)[0]
    ranks = jnp.cumsum(chosen.astype(jnp.int32)) - 1
    picker = chosen[None, :] & (ranks[None, :] == jnp.arange(DEPTH, dtype=jnp.int32)[:, None])
    both_rows = jnp.concatenate([key_own, value_own], axis=1)
    send_rows = jnp.dot(
        picker.astype(jnp.bfloat16), both_rows, preferred_element_type=jnp.float32
    ).astype(jnp.bfloat16)
    received = lax.all_gather(send_rows, "blk", axis=0, tiled=True)
    level_marks = jnp.asarray(LEVEL_START[1:-1], jnp.int32)
    accepted_count = 1 + jnp.sum(
        (leaf_row[:, None] >= level_marks[None, :]).astype(jnp.int32), axis=1
    )
    steps_ahead = jnp.arange(DEPTH, dtype=jnp.int32)
    written = length_row[:, None] + steps_ahead[None, :]
    page_index = jnp.take(
        page_row, jnp.clip(offsets[:, None] + written // PAGE, 0, total_pages - 1)
    )
    keeper = (steps_ahead[None, :] < accepted_count[:, None]) & (page_index // pool_pages == myself)
    target = jnp.where(
        keeper, page_index % pool_pages * PAGE + written % PAGE, pool_pages * PAGE
    ).reshape(-1)
    new_keys = cache[0, 0].at[target].set(received[:, :width], mode="drop")
    new_values = cache[0, 1].at[target].set(received[:, width:], mode="drop")
    cache_new = jnp.stack([new_keys, new_values])[None]
    return (layer_out, drafts, cache_new)


def solution(mesh):
    in_specs = (
        P(("req", "blk"), None),
        P("req", None, "blk", None),
        P("req", None),
        P("req", None),
        P(("req", "blk"), None),
        P("req", None),
        P(None, "blk"),
        P(None, "blk"),
        P(None, "blk"),
        P("blk", None),
        P(None, None, "blk"),
        P(None, "req"),
    )
    out_specs = (
        P(("req", "blk"), None),
        P(None, ("req", "blk"), None),
        P("req", None, "blk", None),
    )
    return jax.shard_map(
        on_device, mesh=mesh, in_specs=in_specs, out_specs=out_specs, check_vma=False
    )
```

profile of v0, /device:TPU:0, one launch (start us, length us, event | category | flops | bytes accessed | tf_op | source)
XLA Modules:
  0.0 339.3 jit_solution(18099997209600794324)
XLA Ops:
  10.2 12.3 %all_gather.21 = bf16[384,1280]{1,0:T(8,128)(2,1)S(1)} all-gather(bf16[48,1280]{1,0:T(8,128)(2,1)S(1)} %fusion.41), channel_id=1, replica_groups=mesh['req'=4,'blk'=8] {'blk'}, dimensions={0}, use_global_device_ids=true | all-gather | bytes 1105920 | tf_op jit(solution)/shard_map/all_gather | solution.py:38
  22.5 2.1 convolution_convert_fusion.1
  25.5 3.5 %all-to-all-start = ((bf16[8,48,480]{2,1,0:T(8,128)(2,1)}), bf16[8,48,480]{2,1,0:T(8,128)(2,1)S(1)}, u32[]{:S(2)}, u32[]{:S(2)}) async-start(bf16[8,48,480]{2,1,0:T(8,128)(2,1)} %bitcast.8), calls=%async_computation | async-start | bytes 786432 | tf_op jit(solution)/shard_map/all_to_all | solution.py:42
  29.7 10.3 %slice_bitcast_fusion.1 = (bf16[2048,1280]{1,0:T(8,128)(2,1)}, bf16[2048,1280]{1,0:T(8,128)(2,1)}, bf16[1,1,2048,1280]{3,2,1,0:T(8,128)(2,1)}, bf16[1,1,2048,1280]{3,2,1,0:T(8,128)(2,1)}) fusion(bf16[1,2,2048,1280]{3,2,1,0:T(8,128)(2,1)} %param.16), kind=kLoop, calls=%fused_computation.220 | loop fusion | bytes 31457280 | tf_op jit(solution)/shard_map/squeeze | solution.py:218
  39.9 15.7 %reshape.1047 = bf16[16,128,16,80]{3,2,1,0:T(8,128)(2,1)} reshape(bf16[1,1,2048,1280]{3,2,1,0:T(8,128)(2,1)} %get-tuple-element.30) | data formatting | bytes 10485760 | tf_op jit(solution)/shard_map/reshape;squeeze | solution.py:99
  55.7 15.7 %reshape.1048 = bf16[16,128,16,80]{3,2,1,0:T(8,128)(2,1)} reshape(bf16[1,1,2048,1280]{3,2,1,0:T(8,128)(2,1)} %get-tuple-element.29) | data formatting | bytes 10485760 | tf_op jit(solution)/shard_map/reshape;squeeze | solution.py:100
  73.0 12.9 %all_gather.22 = bf16[384,1280]{1,0:T(8,128)(2,1)} all-gather(bf16[48,1280]{1,0:T(8,128)(2,1)S(1)} %get-tuple-element.33), channel_id=1, replica_groups=mesh['req'=4,'blk'=8] {'blk'}, dimensions={0}, use_global_device_ids=true | all-gather | bytes 1105920 | tf_op jit(solution)/shard_map/all_gather | solution.py:75
  85.9 3.3 reshape.896
  89.2 2.7 gather_fusion
  91.9 2.2 broadcast_select_fusion
  94.2 10.6 %bitcast_reduce_fusion = (f32[16,48,16]{1,2,0:T(8,128)S(1)}, f32[16,16,48,128]{3,2,1,0:T(8,128)}) fusion(pred[16,128]{1,0:T(8,128)(4,1)S(1)} %add_compare_fusion, bf16[16,128,16,80]{3,2,1,0:T(8,128)(2,1)} %reshape.1047, bf16[16,48,16,80]{3,2,1,0:T(8,128)(2,1)S(1)} %broadcast_select_fusion), kind=kOutput, calls=%fused_computation.15 | convolution fusion | flops 256364544 | bytes 13551616 | tf_op jit(solution)/shard_map/pqhd,pthd->pqht/dot_general | solution.py:102
  105.6 24.0 %pmax.7 = f32[8,48,16]{1,0,2:T(8,128)S(1)} all-reduce(f32[8,48,16]{1,0,2:T(8,128)S(1)} %copy.79), channel_id=1, replica_groups=mesh['req'=4,'blk'=8] {'blk'}, use_global_device_ids=true, to_apply=%region_8.9 | all-reduce | flops 6144 | bytes 49152 | tf_op jit(solution)/shard_map/pmax | solution.py:118
  129.9 5.7 %fusion.8 = f32[16,48,16]{1,2,0:T(8,128)S(1)} fusion(f32[16,16,48,128]{3,2,1,0:T(8,128)} %get-tuple-element.38, f32[16,48,16]{1,2,0:T(8,128)S(1)} %broadcast_select_fusion.1, pred[16,128]{1,0:T(8,128)(4,1)S(1)} %add_compare_fusion), kind=kLoop, calls=%fused_computation.21 | loop fusion | flops 7852032 | bytes 6391808 | tf_op jit(solution)/shard_map/reduce_sum | solution.py:109
  137.1 7.6 %fusion.21 = f32[16,48,16,80]{3,1,2,0:T(8,128)S(1)} fusion(bf16[16,128,16,80]{3,2,1,0:T(8,128)(2,1)} %reshape.1048, f32[16,16,48,128]{3,2,1,0:T(8,128)} %get-tuple-element.38, f32[16,48,16]{1,2,0:T(8,128)S(1)} %broadcast_select_fusion.1, pred[16,128]{1,0:T(8,128)(4,1)S(1)} %add_compare_fusion), kind=kOutput, calls=%fused_computation.35 | convolution fusion | flops 259522560 | bytes 15517696 | tf_op jit(solution)/shard_map/pqht,pthd->pqhd/dot_general | solution.py:110
  144.7 6.7 %fusion.29 = f32[8,48,16,80]{3,0,2,1:T(8,128)S(1)} fusion(f32[16,48,16,80]{3,1,2,0:T(8,128)S(1)} %fusion.21, f32[8,48,16]{0,2,1:T(8,128)S(1)} %copy.80, s32[16]{0:T(128)S(1)} %convert_reduce_fusion), kind=kOutput, calls=%fused_computation.37 | convolution fusion | flops 94863488 | bytes 5922880 | tf_op jit(solution)/shard_map/pr,pqhd->rqhd/dot_general | solution.py:115
  151.4 2.2 copy.81
  153.7 4.2 %reshape.897 = f32[8,48,1280]{2,1,0:T(8,128)} reshape(f32[8,48,16,80]{3,2,1,0:T(8,128)} %copy.81) | data formatting | bytes 3932160 | tf_op jit(solution)/shard_map/reshape | solution.py:121
  164.4 5.3 %reduce-scatter.6.cloned.1.call-done = f32[1,48,16]{1,2,0:T(8,128)} async-done(((f32[8,48,16]{1,2,0:T(8,128)}), f32[1,48,16]{1,2,0:T(8,128)}) %reduce-scatter.6.cloned.1.call-update) | async-done | bytes 3088 | tf_op jit(solution)/shard_map/reduce_scatter | solution.py:125
  170.4 43.4 %reduce-scatter.4.cloned.1.call-done = f32[1,48,1280]{2,1,0:T(8,128)} async-done(((f32[8,48,1280]{2,1,0:T(8,128)}), f32[1,48,1280]{2,1,0:T(8,128)}) %reduce-scatter.4.cloned.1.call-update) | async-done | bytes 245776 | tf_op jit(solution)/shard_map/reduce_scatter | solution.py:126
  216.7 10.7 %all_gather.23 = bf16[384,1280]{1,0:T(8,128)(2,1)S(1)} all-gather(bf16[48,1280]{1,0:T(8,128)(2,1)S(1)} %convert_element_type.114), channel_id=1, replica_groups=mesh['req'=4,'blk'=8] {'blk'}, dimensions={0}, use_global_device_ids=true | all-gather | bytes 1105920 | tf_op jit(solution)/shard_map/all_gather | solution.py:38
  228.0 8.8 %all_to_all.45 = bf16[8,48,160]{2,1,0:T(8,128)(2,1)S(1)} all-to-all(bf16[8,48,160]{2,1,0:T(8,128)(2,1)S(1)} %bitcast.181), channel_id=1, replica_groups=mesh['req'=4,'blk'=8] {'blk'}, dimensions={0} | all-to-all | bytes 245760 | tf_op jit(solution)/shard_map/all_to_all | solution.py:42
  237.5 9.9 %all_gather.24 = bf16[384,1280]{1,0:T(8,128)(2,1)S(1)} all-gather(bf16[48,1280]{1,0:T(8,128)(2,1)S(1)} %fusion.44), channel_id=1, replica_groups=mesh['req'=4,'blk'=8] {'blk'}, dimensions={0}, use_global_device_ids=true | all-gather | bytes 1105920 | tf_op jit(solution)/shard_map/all_gather | solution.py:38
  247.4 3.4 fusion.63
  256.1 9.4 %all-gather = bf16[8,5,2560]{2,1,0:T(8,128)(2,1)S(1)} all-gather(bf16[1,5,2560]{2,1,0:T(8,128)(2,1)S(1)} %fusion.10), channel_id=1, replica_groups=mesh['req'=4,'blk'=8] {'blk'}, dimensions={0}, use_global_device_ids=true | all-gather | bytes 230400 | tf_op jit(solution)/shard_map/all_gather | solution.py:204
  265.6 6.7 %scatter_custom_fusion = bf16[2048,1280]{1,0:T(8,128)(2,1)} fusion(bf16[2048,1280]{1,0:T(8,128)(2,1)} %get-tuple-element.27, s32[40]{0:T(128)S(1)} %fusion.97, bf16[40,2560]{1,0:T(8,128)(2,1)S(1)} %reshape.1021), kind=kCustom, calls=%fused_computation.96 | custom fusion | bytes 5345280 | tf_op jit(solution)/shard_map/scatter | solution.py:218
  272.3 6.9 %scatter_custom_fusion.1 = bf16[2048,1280]{1,0:T(8,128)(2,1)} fusion(bf16[2048,1280]{1,0:T(8,128)(2,1)} %get-tuple-element.28, s32[40]{0:T(128)S(1)} %fusion.97, bf16[40,2560]{1,0:T(8,128)(2,1)S(1)} %reshape.1021), kind=kCustom, calls=%fused_computation.94 | custom fusion | bytes 5345280 | tf_op jit(solution)/shard_map/scatter | solution.py:219
  279.2 12.1 %reduce-scatter.8.cloned.1.call-done = f32[48,1280]{1,0:T(8,128)} async-done(((f32[384,1280]{1,0:T(8,128)}), f32[48,1280]{1,0:T(8,128)}) %reduce-scatter.8.cloned.1.call-update) | async-done | bytes 245776 | tf_op jit(solution)/shard_map/reduce_scatter | solution.py:165
  293.2 10.7 %all_gather.25 = bf16[384,1280]{1,0:T(8,128)(2,1)S(1)} all-gather(bf16[48,1280]{1,0:T(8,128)(2,1)S(1)} %multiply_convert_fusion.1), channel_id=1, replica_groups=mesh['req'=4,'blk'=8] {'blk'}, dimensions={0}, use_global_device_ids=true | all-gather | bytes 1105920 | tf_op jit(solution)/shard_map/all_gather | solution.py:38
  307.5 3.5 %all-to-all-start.2 = ((bf16[8,48,640]{2,1,0:T(8,128)(2,1)}), bf16[8,48,640]{2,1,0:T(8,128)(2,1)S(1)}, u32[]{:S(2)}, u32[]{:S(2)}) async-start(bf16[8,48,640]{2,1,0:T(8,128)(2,1)} %all_to_all.40), calls=%async_computation.5 | async-start | bytes 983040 | tf_op jit(solution)/shard_map/all_to_all | solution.py:42
  311.0 9.1 %maximum_bitcast_fusion = bf16[1,2,2048,1280]{3,2,1,0:T(8,128)(2,1)} fusion(bf16[1,2048,1280]{2,1,0:T(8,128)(2,1)} %bitcast.176, bf16[1,2048,1280]{2,1,0:T(8,128)(2,1)} %bitcast.177), kind=kLoop, calls=%fused_computation.9 | loop fusion | flops 5242880 | bytes 20971520 | tf_op jit(solution)/shard_map/broadcast_in_dim | solution.py:220
  321.3 2.4 reshape.932
  328.0 3.9 %fusion.26 = bf16[4,48,1280]{2,1,0:T(8,128)(2,1)} fusion(bf16[1280,1280]{0,1:T(8,128)(2,1)} %all-gather.3.cloned.1.call-done, f32[4,48,1280]{2,1,0:T(8,128)S(1)} %reshape.924, f32[48,1280]{1,0:T(8,128)S(1)} %copy-done.7), kind=kOutput, calls=%fused_computation.36 | convolution fusion | flops 629882880 | bytes 4997120 | tf_op jit(solution)/shard_map/krd,do->kro/dot_general | solution.py:190
  (137 shorter events, 33.4 us)
Async XLA Ops:
  8.0 296.0 %copy-start = (bf16[4,1280,160]{1,2,0:T(8,128)(2,1)S(1)}, bf16[4,1280,160]{1,2,0:T(8,128)(2,1)}, u32[]{:S(2)}) copy-start(bf16[4,1280,160]{1,2,0:T(8,128)(2,1)} %param.25) | copy-start | bytes 4915204
  8.0 21.0 %copy-start.10 = (s32[1,8]{1,0:T(1,128)S(1)}, s32[1,8]{1,0:T(1,128)}, u32[]{:S(2)}) copy-start(s32[1,8]{1,0:T(1,128)} %param.18) | copy-start | bytes 100
  8.0 21.2 %copy-start.1 = (s32[1,128]{1,0:T(1,128)S(1)}, s32[1,128]{1,0:T(1,128)}, u32[]{:S(2)}) copy-start(s32[1,128]{1,0:T(1,128)} %param.17) | copy-start | bytes 1540
  25.5 45.9 %all-to-all-start = ((bf16[8,48,480]{2,1,0:T(8,128)(2,1)}), bf16[8,48,480]{2,1,0:T(8,128)(2,1)S(1)}, u32[]{:S(2)}, u32[]{:S(2)}) async-start(bf16[8,48,480]{2,1,0:T(8,128)(2,1)} %bitcast.8), calls=%async_computation | async-start | bytes 786432 | tf_op jit(solution)/shard_map/all_to_all | solution.py:42
  29.0 140.7 %reduce-scatter.6.cloned.1.call-start = ((), (), s32[]{:S(2)}) async-start(), calls=%async_computation.7 | async-start | bytes 73728 | tf_op jit(solution)/shard_map/reduce_scatter | solution.py:125
  72.3 0.7 copy-start.3
  136.5 77.4 %reduce-scatter.4.cloned.1.call-start = ((), (), s32[]{:S(2)}) async-start(), calls=%async_computation.6 | async-start | bytes 2211840 | tf_op jit(solution)/shard_map/reduce_scatter | solution.py:126
  151.4 6.7 %copy-start.2 = (s32[1,48]{1,0:T(1,128)S(1)}, s32[1,48]{1,0:T(1,128)}, u32[]{:S(2)}) copy-start(s32[1,48]{1,0:T(1,128)} %param.19) | copy-start | bytes 580
  157.9 69.5 %copy-start.9 = (bf16[1280,160]{0,1:T(8,128)(2,1)S(1)}, bf16[1280,160]{0,1:T(8,128)(2,1)}, u32[]{:S(2)}) copy-start(bf16[1280,160]{0,1:T(8,128)(2,1)} %param.22) | copy-start | bytes 1228804
  157.9 133.4 %reduce-scatter.8.cloned.1.call-start = ((), (), s32[]{:S(2)}) async-start(), calls=%async_computation.8 | async-start | bytes 2211840 | tf_op jit(solution)/shard_map/reduce_scatter | solution.py:165
  164.1 73.2 %copy-start.5 = (bf16[48,1280]{1,0:T(8,128)(2,1)S(1)}, bf16[48,1280]{1,0:T(8,128)(2,1)}, u32[]{:S(2)}) copy-start(bf16[48,1280]{1,0:T(8,128)(2,1)} %param.15) | copy-start | bytes 368644
  215.0 32.4 %copy-start.8 = (bf16[160,1280]{1,0:T(8,128)(2,1)S(1)}, bf16[160,1280]{1,0:T(8,128)(2,1)}, u32[]{:S(2)}) copy-start(bf16[160,1280]{1,0:T(8,128)(2,1)} %param.24) | copy-start | bytes 1228804
  236.8 14.6 %copy-start.11 = (s32[1,8]{1,0:T(1,128)S(1)}, s32[1,8]{1,0:T(1,128)}, u32[]{:S(2)}) copy-start(s32[1,8]{1,0:T(1,128)} %param.20) | copy-start | bytes 100
  247.4 8.0 %copy-start.12 = (s32[4]{0:T(128)S(1)}, s32[4]{0:T(128)}, u32[]{:S(2)}) copy-start(s32[4]{0:T(128)} %constant.187.clone) | copy-start | bytes 52
  247.4 8.6 %copy-start.4 = (bf16[48,3840]{1,0:T(8,128)(2,1)S(1)}, bf16[48,3840]{1,0:T(8,128)(2,1)}, u32[]{:S(2)}) copy-start(bf16[48,3840]{1,0:T(8,128)(2,1)} %copy-done.3) | copy-start | bytes 1105924
  250.8 77.1 %all-gather.3.cloned.1.call-start = ((), (), s32[]{:S(2)}) async-start(), calls=%async_computation.9 | async-start | bytes 4096000 | tf_op jit(solution)/shard_map/all_gather | solution.py:193
  293.0 14.5 %copy-start.6 = (bf16[48,1280]{1,0:T(8,128)(2,1)}, bf16[48,1280]{1,0:T(8,128)(2,1)S(1)}, u32[]{:S(2)}) copy-start(bf16[48,1280]{1,0:T(8,128)(2,1)S(1)} %get-tuple-element.18) | copy-start | bytes 368644
  307.5 12.8 %all-to-all-start.2 = ((bf16[8,48,640]{2,1,0:T(8,128)(2,1)}), bf16[8,48,640]{2,1,0:T(8,128)(2,1)S(1)}, u32[]{:S(2)}, u32[]{:S(2)}) async-start(bf16[8,48,640]{2,1,0:T(8,128)(2,1)} %all_to_all.40), calls=%async_computation.5 | async-start | bytes 983040 | tf_op jit(solution)/shard_map/all_to_all | solution.py:42
  320.1 7.9 %copy-start.7 = (f32[48,1280]{1,0:T(8,128)S(1)}, f32[48,1280]{1,0:T(8,128)}, u32[]{:S(2)}) copy-start(f32[48,1280]{1,0:T(8,128)} %get-tuple-element.17) | copy-start | bytes 737284
Sparse Core Ops, SparseCore 0:
  136.6 33.0 reduce-scatter.5
  173.5 40.2 reduce-scatter.3
  250.9 40.3 reduce-scatter.7
Sparse Core Ops, SparseCore 1:
  252.9 65.5 all-gather.2
where the time goes:
time: 346 us; the launch traced here: 339 us
  blocking collectives  98.7 us (29%)
  local copies, waits for them, and re-layouts  90.3 us (26%)
  waiting for transfers between devices  61.7 us (18%)
  matrix products  37.7 us (11%)
  other arithmetic  25.1 us (7%)
  between operations  17.9 us (5%)
  starting transfers between devices  7.8 us (2%)
    all_gather x4, blocking collectives, row_blocks(): lax.all_gather(values, 'blk', axis=0, tiled=True)  43.6 us
    reduce_scatter x1, waiting for transfers between devices, on_device(): lax.psum_scatter(num_scaled, 'blk', scatter_dimension=0, tiled=True)  43.4 us
    pmax x1, blocking collectives, on_device(): max_all = lax.pmax(request_max, 'blk')  24 us
    another operation x1, local copies, waits for them, and re-layouts, on_device(): keys = cache[0, 0].reshape(pool_pages, PAGE, H, HD)  15.7 us
    another operation x1, local copies, waits for them, and re-layouts, on_device(): values = cache[0, 1].reshape(pool_pages, PAGE, H, HD)  15.7 us
    all_gather x1, blocking collectives, on_device(): query_all = lax.all_gather(projected[:, :width], 'blk', axis=0, tiled=True)  12.9 us
    reduce_scatter x1, waiting for transfers between devices, on_device(): lax.psum_scatter(jnp.dot(hidden_all, w_down, preferred_element_type=jnp.f...  12.1 us
    dot_general x1, matrix products, on_device(): jnp.einsum('pqhd,pthd->pqht', query_page, keys, preferred_element_type=jn...  10.6 us
  transfers between devices with their start and end apart: 6, of which 4 were waited for; matrix products, arithmetic and copies ran while one was open for 32% of the time, Pallas kernels for 0%

commit v1 on v0

v1 whole, which is shorter than its diff:
```python
import functools
import math

import jax
import jax.numpy as jnp
from jax import lax
from jax.experimental import pallas as pl
from jax.experimental.pallas import tpu as pltpu
from jax.sharding import PartitionSpec as P

H = 16
HD = 80
TREE = 48
DEPTH = 5
PAGE = 128
EPS = 1e-06
NEG = -1e30
LEVEL_START = (0, 1, 5, 15, 30, 48)
SCALE = 1.0 / math.sqrt(HD)

WIN = 256
WINDOWS = H * HD // WIN
SLOTS = 4
LOW = 16
SIDE = 128
SHARDS_AT = (0, 2, 4, 6, 1, 3, 5, 7)
LIGHT = pl.CostEstimate(flops=0, bytes_accessed=0, transcendentals=0)
HBM = pl.BlockSpec(memory_space=pltpu.HBM)


def rms_rows(values):
    wide = values.astype(jnp.float32)
    return (wide * lax.rsqrt(jnp.mean(wide * wide, axis=-1, keepdims=True) + EPS)).astype(
        jnp.bfloat16
    )


def dot_t(left, right):
    return lax.dot_general(
        left, right, (((1,), (1,)), ((), ())), preferred_element_type=jnp.float32
    )


def dot_n(left, right):
    return lax.dot_general(
        left, right, (((1,), (0,)), ((), ())), preferred_element_type=jnp.float32
    )


def in_head(window, slot, rows):
    lane = lax.broadcasted_iota(jnp.int32, (rows, WIN), 1)
    first = (3 * window + slot) * HD - window * WIN
    return (lane >= first) & (lane < first + HD)


def masked_queries(rows, window):
    part = rows[:, window * WIN : (window + 1) * WIN].astype(jnp.float32)
    slots = [
        jnp.where(in_head(window, slot, TREE), part, 0.0).astype(jnp.bfloat16)
        for slot in range(SLOTS)
    ]
    return jnp.concatenate(slots, axis=0)


def by_head(products):
    pieces = [None] * H
    for window, product in enumerate(products):
        for slot in range(SLOTS):
            piece = product[slot * TREE : (slot + 1) * TREE]
            head = 3 * window + slot
            pieces[head] = piece if pieces[head] is None else pieces[head] + piece
    return pieces


def own_lanes(product, window):
    total = None
    for slot in range(SLOTS):
        piece = jnp.where(
            in_head(window, slot, TREE), product[slot * TREE : (slot + 1) * TREE], 0.0
        )
        total = piece if total is None else total + piece
    return total


def heads_to_lanes(column):
    lane = lax.broadcasted_iota(jnp.int32, (TREE, SIDE), 1) & (H - 1)
    total = jnp.zeros((TREE, SIDE), jnp.float32)
    for head in range(H):
        total = jnp.where(lane == head, column[head * TREE : (head + 1) * TREE], total)
    return total


def three_parts(wide):
    lane = lax.broadcasted_iota(jnp.int32, wide.shape, 1)
    high = wide.astype(jnp.bfloat16).astype(jnp.float32)
    rest = wide - high
    middle = rest.astype(jnp.bfloat16).astype(jnp.float32)
    low = rest - middle
    return jnp.where(
        lane < 32, high, jnp.where(lane < 64, middle, jnp.where(lane < 96, low, 0.0))
    ).astype(jnp.bfloat16)


def attend_body(
    pages,
    requests,
    info,
    q_ref,
    cache_ref,
    part_ref,
    copy_ref,
    held,
    scores,
    queries,
    top,
    total,
    numer,
    load_sem,
    save_sem,
):
    width = q_ref.shape[1]

    def place(page):
        return pl.ds(pl.multiple_of(info[page] * PAGE, PAGE), PAGE)

    def load(side, page):
        return pltpu.make_async_copy(
            cache_ref.at[side, place(page)], held.at[side, page], load_sem.at[side, page]
        )

    def save(side, page):
        return pltpu.make_async_copy(
            held.at[side, page], copy_ref.at[side, place(page)], save_sem.at[side, page]
        )

    for side in range(2):
        for page in range(pages):
            load(side, page).start()

    def request(r, carry):
        begin = info[2 * pages + r]
        count = info[2 * pages + requests + r]

        @pl.when(count == 0)
        def _():
            part_ref[r, :, :width] = jnp.zeros((TREE, width), jnp.bfloat16)
            part_ref[r, :, width:] = three_parts(jnp.full((TREE, SIDE), NEG, jnp.float32))

        @pl.when(count > 0)
        def _():
            rows = q_ref[pl.ds(pl.multiple_of(r * TREE, 16), TREE), :]
            for window in range(WINDOWS):
                queries[window] = masked_queries(rows, window)
            top[...] = jnp.full(top.shape, NEG, jnp.float32)

            def score(i, carry):
                page = begin + i
                load(0, page).wait()
                save(0, page).start()
                keep = lax.broadcasted_iota(jnp.int32, (TREE, PAGE), 1) < info[pages + page]
                products = [
                    dot_t(
                        queries[window], held[0, page, :, window * WIN : (window + 1) * WIN]
                    )
                    for window in range(WINDOWS)
                ]
                for head, piece in enumerate(by_head(products)):
                    span = pl.ds(head * TREE, TREE)
                    masked = jnp.where(keep, piece * SCALE, NEG)
                    scores[page, span] = masked
                    top[span] = jnp.maximum(top[span], masked)
                return carry

            lax.fori_loop(0, count, score, 0)
            largest = jnp.max(top[...], axis=1, keepdims=True)
            top[...] = jnp.broadcast_to(largest, top.shape)
            total[...] = jnp.zeros(total.shape, jnp.float32)
            numer[...] = jnp.zeros(numer.shape, jnp.float32)

            def weigh(i, carry):
                page = begin + i
                load(1, page).wait()
                save(1, page).start()
                weights = jnp.exp(scores[page] - top[...])
                total[...] += weights
                low = weights.astype(jnp.bfloat16)
                for window in range(WINDOWS):
                    first = 3 * window * TREE
                    numer[window] += dot_n(
                        low[first : first + SLOTS * TREE],
                        held[1, page, :, window * WIN : (window + 1) * WIN],
                    )
                return carry

            lax.fori_loop(0, count, weigh, 0)
            denom = jnp.sum(total[...], axis=1, keepdims=True)
            inverse = 1.0 / denom
            for window in range(WINDOWS):
                first = 3 * window * TREE
                scaled = numer[window] * inverse[first : first + SLOTS * TREE]
                part_ref[r, :, window * WIN : (window + 1) * WIN] = own_lanes(
                    scaled, window
                ).astype(jnp.bfloat16)
            part_ref[r, :, width:] = three_parts(
                heads_to_lanes(top[:, :1] + jnp.log(denom))
            )

        return carry

    lax.fori_loop(0, requests, request, 0)
    used = info[2 * pages + requests - 1] + info[2 * pages + 2 * requests - 1]

    def untouched(page, carry):
        for side in range(2):
            load(side, page).wait()
            save(side, page).start()
        return carry

    lax.fori_loop(used, pages, untouched, 0)

    def settle(page, carry):
        for side in range(2):
            save(side, page).wait()
        return carry

    lax.fori_loop(0, pages, settle, 0)


def attend(info, query_all, cache, requests):
    pages = cache.shape[1] // PAGE
    width = query_all.shape[1]
    return pl.pallas_call(
        functools.partial(attend_body, pages, requests),
        out_shape=(
            jax.ShapeDtypeStruct((requests, TREE, width + SIDE), jnp.bfloat16),
            jax.ShapeDtypeStruct(cache.shape, cache.dtype),
        ),
        in_specs=[
            pl.BlockSpec(memory_space=pltpu.SMEM),
            pl.BlockSpec(memory_space=pltpu.VMEM),
            HBM,
        ],
        out_specs=(
            pl.BlockSpec(memory_space=pltpu.VMEM),
            HBM,
        ),
        scratch_shapes=[
            pltpu.VMEM((2, pages, PAGE, width), jnp.bfloat16),
            pltpu.VMEM((pages, H * TREE, PAGE), jnp.float32),
            pltpu.VMEM((WINDOWS, SLOTS * TREE, WIN), jnp.bfloat16),
            pltpu.VMEM((H * TREE, PAGE), jnp.float32),
            pltpu.VMEM((H * TREE, PAGE), jnp.float32),
            pltpu.VMEM((WINDOWS, SLOTS * TREE, WIN), jnp.float32),
            pltpu.SemaphoreType.DMA((2, pages)),
            pltpu.SemaphoreType.DMA((2, pages)),
        ],
        compiler_params=pltpu.CompilerParams(vmem_limit_bytes=60 * 1024 * 1024),
        cost_estimate=pl.CostEstimate(
            flops=4 * pages * PAGE * H * TREE * WIN,
            bytes_accessed=5 * cache.size,
            transcendentals=pages * PAGE * H * TREE,
        ),
        name="attend",
    )(info, query_all, cache)


def project_body(tree_ref, w_ref, out_ref):
    blocks = out_ref.shape[0]
    product = dot_t(rms_rows(tree_ref[...]), w_ref[...]).astype(jnp.bfloat16)
    for block in range(blocks):
        out_ref[block] = product[block * TREE : (block + 1) * TREE]


def project(tree_all, w_rows):
    rows, width = tree_all.shape
    columns = w_rows.shape[0]
    return pl.pallas_call(
        project_body,
        out_shape=jax.ShapeDtypeStruct((rows // TREE, TREE, columns), jnp.bfloat16),
        in_specs=[pl.BlockSpec(memory_space=pltpu.VMEM)] * 2,
        out_specs=pl.BlockSpec(memory_space=pltpu.VMEM),
        compiler_params=pltpu.CompilerParams(vmem_limit_bytes=24 * 1024 * 1024),
        cost_estimate=LIGHT,
        name="project",
    )(tree_all, w_rows)


def tree_body(info, qkv_ref, parent_ref, part_ref, send_ref):
    width = qkv_ref.shape[1] // 3
    node_row = lax.broadcasted_iota(jnp.int32, (TREE, TREE), 0)
    node_col = lax.broadcasted_iota(jnp.int32, (TREE, TREE), 1)
    steps = jnp.minimum(parent_ref[...] + jnp.where(node_row == node_col, 1.0, 0.0), 1.0)
    for _ in range(2):
        low = steps.astype(jnp.bfloat16)
        steps = jnp.minimum(dot_n(low, low), 1.0)
    marks = steps > 0.5

    query = qkv_ref[:, :width]
    key = qkv_ref[:, width : 2 * width]
    value = qkv_ref[:, 2 * width :]
    products = [
        dot_t(masked_queries(query, window), key[:, window * WIN : (window + 1) * WIN])
        for window in range(WINDOWS)
    ]
    scores = jnp.concatenate(
        [jnp.where(marks, piece * SCALE, NEG) for piece in by_head(products)], axis=0
    )
    top = jnp.max(scores, axis=1, keepdims=True)
    weights = jnp.exp(scores - top)
    denom = jnp.sum(weights, axis=1, keepdims=True)
    inverse = 1.0 / denom
    low = weights.astype(jnp.bfloat16)
    for window in range(WINDOWS):
        span = slice(window * WIN, (window + 1) * WIN)
        first = 3 * window * TREE
        numer = dot_n(low[first : first + SLOTS * TREE], value[:, span])
        part_ref[:, span] = own_lanes(numer * inverse[first : first + SLOTS * TREE], window)
    part_ref[:, width:] = heads_to_lanes(top + jnp.log(denom))

    leaf = jnp.where(
        lax.broadcasted_iota(jnp.int32, (LOW, TREE), 1) == info[0], 1.0, 0.0
    ).astype(jnp.bfloat16)
    chosen = dot_n(leaf, steps.astype(jnp.bfloat16))
    earlier = jnp.where(node_row <= node_col, 1.0, 0.0).astype(jnp.bfloat16)
    rank = dot_n(chosen.astype(jnp.bfloat16), earlier) - 1.0
    wanted = lax.broadcasted_iota(jnp.int32, (LOW, TREE), 0).astype(jnp.float32)
    is_key = (chosen > 0.5) & (rank == wanted) & (wanted < DEPTH)
    is_value = (chosen > 0.5) & (rank == wanted - DEPTH) & (rank < DEPTH)
    send_ref[...] = (
        dot_n(jnp.where(is_key, 1.0, 0.0).astype(jnp.bfloat16), key)
        + dot_n(jnp.where(is_value, 1.0, 0.0).astype(jnp.bfloat16), value)
    ).astype(jnp.bfloat16)


def tree(info, qkv, parent_hot):
    width = qkv.shape[1] // 3
    return pl.pallas_call(
        tree_body,
        out_shape=(
            jax.ShapeDtypeStruct((TREE, width + SIDE), jnp.float32),
            jax.ShapeDtypeStruct((LOW, width), jnp.bfloat16),
        ),
        in_specs=[pl.BlockSpec(memory_space=pltpu.SMEM)]
        + [pl.BlockSpec(memory_space=pltpu.VMEM)] * 2,
        out_specs=(pl.BlockSpec(memory_space=pltpu.VMEM),) * 2,
        compiler_params=pltpu.CompilerParams(vmem_limit_bytes=12 * 1024 * 1024),
        cost_estimate=LIGHT,
        name="tree",
    )(info, qkv, parent_hot)


def mix_body(spots, info, part_ref, own_ref, tree_ref, *rest):
    count = 1 + max(buffer for buffer, _ in spots)
    buffers = rest[:count]
    mid_ref, normed_ref, weights, sems = rest[count:]
    blocks = part_ref.shape[0]
    width = tree_ref.shape[1]
    rows = width // len(spots)
    copies = []
    for index, (buffer, row) in enumerate(spots):
        first = pl.multiple_of(info[index] * rows, 16)
        copies.append(
            pltpu.make_async_copy(
                buffers[buffer].at[pl.ds(row, rows)],
                weights.at[pl.ds(first, rows)],
                sems.at[index],
            )
        )
    for copy in copies:
        copy.start()

    lane = lax.broadcasted_iota(jnp.int32, (TREE, SIDE), 1)
    logs = []
    for block in range(blocks):
        packed = part_ref[block, :, width:].astype(jnp.float32)
        logs.append(
            packed + (pltpu.roll(packed, SIDE - 32, 1) + pltpu.roll(packed, SIDE - 64, 1))
        )
    logs.append(own_ref[:, width:])
    largest = functools.reduce(jnp.maximum, logs)
    shares = [jnp.exp(one - largest) for one in logs]
    whole = functools.reduce(jnp.add, shares)
    spread_rows = []
    for share in shares:
        share = share / whole
        high = share.astype(jnp.bfloat16).astype(jnp.float32)
        spread_rows.append(
            jnp.where(
                lane < LOW, high, jnp.where(lane < 2 * LOW, share - high, 0.0)
            ).astype(jnp.bfloat16)
        )
    spread_rows = jnp.concatenate(spread_rows, axis=0)
    for window in range(WINDOWS):
        span = slice(window * WIN, (window + 1) * WIN)
        head = lax.broadcasted_iota(jnp.int32, (SIDE, WIN), 0)
        column = lax.broadcasted_iota(jnp.int32, (SIDE, WIN), 1) + window * WIN
        first = (head & (H - 1)) * HD
        expand = jnp.where(
            (head < 2 * LOW) & (column >= first) & (column < first + HD), 1.0, 0.0
        ).astype(jnp.bfloat16)
        spread = dot_n(spread_rows, expand)
        mixed = spread[blocks * TREE :] * own_ref[:, span]
        for block in range(blocks):
            mixed = mixed + spread[block * TREE : (block + 1) * TREE] * part_ref[
                block, :, span
            ].astype(jnp.float32)
        mid_ref[:, span] = mixed.astype(jnp.bfloat16)

    attended = mid_ref[...]
    for copy in copies:
        copy.wait()
    proj = dot_t(attended, weights[...]).astype(jnp.bfloat16)
    mid = (tree_ref[...].astype(jnp.float32) + proj.astype(jnp.float32)).astype(jnp.bfloat16)
    mid_ref[...] = mid
    normed_ref[...] = rms_rows(mid)


def mix(info, parts, own, tree_input, buffers, spots):
    width = tree_input.shape[1]
    return pl.pallas_call(
        functools.partial(mix_body, spots),
        out_shape=(jax.ShapeDtypeStruct((TREE, width), jnp.bfloat16),) * 2,
        in_specs=[pl.BlockSpec(memory_space=pltpu.SMEM)]
        + [pl.BlockSpec(memory_space=pltpu.VMEM)] * 3
        + [HBM] * len(buffers),
        out_specs=(pl.BlockSpec(memory_space=pltpu.VMEM),) * 2,
        scratch_shapes=[
            pltpu.VMEM((width, width), jnp.bfloat16),
            pltpu.SemaphoreType.DMA((len(spots),)),
        ],
        compiler_params=pltpu.CompilerParams(vmem_limit_bytes=40 * 1024 * 1024),
        cost_estimate=LIGHT,
        name="mix",
    )(info, parts, own, tree_input, *buffers)


def feed_body(count, normed_ref, *rest):
    buffers, out_ref = rest[:count], rest[count]
    half = buffers[0].shape[0] // 2
    up = jnp.concatenate([buffer[:half] for buffer in buffers], axis=0)
    down = jnp.concatenate([buffer[half:] for buffer in buffers], axis=0)
    hidden = jax.nn.gelu(dot_t(normed_ref[...], up)).astype(jnp.bfloat16)
    out_ref[...] = dot_n(hidden, down).astype(out_ref.dtype)


def feed(normed, buffers, kind):
    return pl.pallas_call(
        functools.partial(feed_body, len(buffers)),
        out_shape=jax.ShapeDtypeStruct(normed.shape, kind),
        in_specs=[pl.BlockSpec(memory_space=pltpu.VMEM)] * (1 + len(buffers)),
        out_specs=pl.BlockSpec(memory_space=pltpu.VMEM),
        compiler_params=pltpu.CompilerParams(vmem_limit_bytes=24 * 1024 * 1024),
        cost_estimate=LIGHT,
        name="feed",
    )(normed, *buffers)


def finish_body(mid_ref, *rest):
    *parts, layer_ref, normed_ref = rest
    total = mid_ref[...].astype(jnp.float32)
    total = total + functools.reduce(
        jnp.add, [part[...].astype(jnp.float32) for part in parts]
    )
    layer = total.astype(jnp.bfloat16)
    layer_ref[...] = layer
    normed_ref[...] = rms_rows(layer)


def finish(mid, parts):
    return pl.pallas_call(
        finish_body,
        out_shape=(jax.ShapeDtypeStruct(mid.shape, jnp.bfloat16),) * 2,
        in_specs=[pl.BlockSpec(memory_space=pltpu.VMEM)] * (1 + len(parts)),
        out_specs=(pl.BlockSpec(memory_space=pltpu.VMEM),) * 2,
        cost_estimate=LIGHT,
        name="finish",
    )(mid, *parts)


def draft_body(rows_ref, w_ref, branch_ref):
    blocks = rows_ref.shape[0]
    rows = rows_ref[...].reshape(-1, rows_ref.shape[2])
    grown = jax.nn.silu(dot_t(rows, w_ref[...])).astype(jnp.bfloat16)
    for block in range(blocks):
        branch_ref[block] = grown[block * TREE : (block + 1) * TREE]


def draft(rows, w_draft_rows):
    blocks = rows.shape[0]
    columns, width = w_draft_rows.shape
    return pl.pallas_call(
        draft_body,
        out_shape=jax.ShapeDtypeStruct((blocks, TREE, columns), jnp.bfloat16),
        in_specs=[pl.BlockSpec(memory_space=pltpu.VMEM)] * 2,
        out_specs=pl.BlockSpec(memory_space=pltpu.VMEM),
        compiler_params=pltpu.CompilerParams(vmem_limit_bytes=12 * 1024 * 1024),
        cost_estimate=LIGHT,
        name="draft",
    )(rows, w_draft_rows)


def patch_body(heads, count, info, branch_ref, layer_ref, *rest):
    buffers = rest[:count]
    out_ref, weights, sems = rest[count:]
    blocks, _, columns = branch_ref.shape
    piece = columns // heads
    copies = []
    for index, buffer in enumerate(buffers):
        rows = buffer.shape[0]
        first = pl.multiple_of(info[index] * rows, 16)
        copies.append(
            pltpu.make_async_copy(buffer, weights.at[pl.ds(first, rows)], sems.at[index])
        )
    for copy in copies:
        copy.start()
    layer = layer_ref[...].astype(jnp.float32)
    drafted = []
    for head in range(heads):
        branch = jnp.concatenate(
            [
                branch_ref[block, :, head * piece : (head + 1) * piece].astype(jnp.float32)
                for block in range(blocks)
            ],
            axis=1,
        )
        drafted.append((layer + branch).astype(jnp.bfloat16))
    for copy in copies:
        copy.wait()
    product = dot_t(jnp.concatenate(drafted, axis=0), weights[...]).astype(jnp.bfloat16)
    for head in range(heads):
        out_ref[head] = product[head * TREE : (head + 1) * TREE]


def patch(info, branches, layer_out, buffers, heads):
    count = len(buffers)
    width = layer_out.shape[1]
    outputs = sum(buffer.shape[0] for buffer in buffers)
    return pl.pallas_call(
        functools.partial(patch_body, heads, count),
        out_shape=jax.ShapeDtypeStruct((heads, TREE, outputs), jnp.bfloat16),
        in_specs=[pl.BlockSpec(memory_space=pltpu.SMEM)]
        + [pl.BlockSpec(memory_space=pltpu.VMEM)] * 2
        + [HBM] * count,
        out_specs=pl.BlockSpec(memory_space=pltpu.VMEM),
        scratch_shapes=[
            pltpu.VMEM((outputs, width), jnp.bfloat16),
            pltpu.SemaphoreType.DMA((count,)),
        ],
        compiler_params=pltpu.CompilerParams(vmem_limit_bytes=16 * 1024 * 1024),
        cost_estimate=LIGHT,
        name="patch",
    )(info, branches, layer_out, *buffers)


def append_body(requests, count, info, *rest):
    sent = rest[:count]
    _, cache_ref, rows, blocks, load_sem, save_sem = rest[count:]

    def where(index, side):
        return cache_ref.at[side, pl.ds(pl.multiple_of(info[index], LOW), LOW)]

    def load(index, side):
        return pltpu.make_async_copy(
            where(index, side), blocks.at[index, side], load_sem.at[index, side]
        )

    def save(index, side):
        return pltpu.make_async_copy(
            blocks.at[index, side], where(index, side), save_sem.at[index, side]
        )

    def fetch(index, carry):
        @pl.when(info[index] >= 0)
        def _():
            for side in range(2):
                load(index, side).start()

        return carry

    def merge(index, carry):
        entry = index // 2
        request = info[5 * requests + entry]
        index = 2 * request + index % 2

        @pl.when(info[index] >= 0)
        def _():
            fresh = rows[entry].astype(jnp.float32)
            step = (
                lax.broadcasted_iota(jnp.int32, (LOW, fresh.shape[1]), 0)
                + info[2 * requests + index]
            )
            count = info[4 * requests + request]
            for side in range(2):
                load(index, side).wait()
                merged = blocks[index, side].astype(jnp.float32)
                for a in range(DEPTH):
                    row = fresh[side * DEPTH + a : side * DEPTH + a + 1]
                    merged = jnp.where((step == a) & (a < count), row, merged)
                blocks[index, side] = merged.astype(jnp.bfloat16)
                save(index, side).start()

        return carry

    def settle(index, carry):
        @pl.when(info[index] >= 0)
        def _():
            for side in range(2):
                save(index, side).wait()

        return carry

    lax.fori_loop(0, 2 * requests, fetch, 0)
    each = requests // count
    for index in range(count):
        for entry in range(each):
            rows[index * each + entry] = sent[index][entry * LOW : (entry + 1) * LOW]
    lax.fori_loop(0, 2 * requests, merge, 0)
    lax.fori_loop(0, 2 * requests, settle, 0)


def append(info, sent, cache, requests):
    width = cache.shape[2]
    count = len(sent)
    return pl.pallas_call(
        functools.partial(append_body, requests, count),
        out_shape=jax.ShapeDtypeStruct(cache.shape, cache.dtype),
        in_specs=[pl.BlockSpec(memory_space=pltpu.SMEM)]
        + [pl.BlockSpec(memory_space=pltpu.VMEM)] * count
        + [HBM],
        out_specs=HBM,
        input_output_aliases={1 + count: 0},
        scratch_shapes=[
            pltpu.VMEM((requests, LOW, width), jnp.bfloat16),
            pltpu.VMEM((2 * requests, 2, LOW, width), jnp.bfloat16),
            pltpu.SemaphoreType.DMA((2 * requests, 2)),
            pltpu.SemaphoreType.DMA((2 * requests, 2)),
        ],
        compiler_params=pltpu.CompilerParams(vmem_limit_bytes=24 * 1024 * 1024),
        cost_estimate=LIGHT,
        name="append",
    )(info, *sent, cache)


def after(values, earlier):
    return lax.optimization_barrier((values, earlier))[0]


def to_chips(shard):
    if lax.axis_size("blk") != 8:
        return [lax.all_gather(shard, "blk", axis=0, tiled=True)]
    return [shard] + [swap(shard, "blk", bits) for bits in (2, 4, 6)]


def to_cores(shards):
    if lax.axis_size("blk") != 8:
        return shards
    return shards + [swap(shard, "blk", 1) for shard in shards]


def pass_on(values, axis):
    size = lax.axis_size(axis)
    return lax.ppermute(values, axis, [(i, (i + 1) % size) for i in range(size)])


def swap(values, axis, bits):
    size = lax.axis_size(axis)
    return lax.ppermute(values, axis, [(i, i ^ bits) for i in range(size)])


def on_device(
    tree_input,
    cache,
    page_table,
    lengths,
    parents,
    accept_leaf,
    w_qkv,
    w_out,
    w_up,
    w_down,
    w_draft,
    w_patch,
):
    blocks = lax.axis_size("blk")
    myself = lax.axis_index("blk")
    lines = lax.axis_size("req")
    my_line = lax.axis_index("req")
    width = tree_input.shape[1]
    requests = lengths.shape[1]
    pool_pages = cache.shape[2] // PAGE
    heads = w_draft.shape[0]
    int32 = jnp.int32

    tree_all = lax.all_gather(tree_input, "blk", axis=0, tiled=True)
    projected = project(tree_all, w_qkv.T)
    out_rows = w_out.T
    feed_rows = jnp.concatenate([w_up.T, w_down])
    if blocks == 8:
        out_y = swap(after(out_rows, projected), "blk", 4)
    ring = [after(w_patch.T, projected)]
    ring.append(pass_on(ring[-1], "req"))
    projected = lax.all_to_all(projected, "blk", split_axis=0, concat_axis=0, tiled=True)
    projected = projected.transpose(1, 0, 2).reshape(tree_input.shape[0], -1)
    query_all = lax.all_gather(projected[:, :width], "blk", axis=0, tiled=True)
    if blocks == 8:
        query_all, out_y = lax.optimization_barrier((query_all, out_y))
        out_x = swap(jnp.concatenate([out_rows, out_y]), "blk", 2)
        feed_y = swap(after(feed_rows, query_all), "blk", 4)

    page_row, length_row, leaf_row = page_table[0], lengths[0], accept_leaf[0]
    total_pages = page_row.shape[0]
    npages = (length_row + DEPTH + PAGE - 1) // PAGE
    each = jnp.arange(requests, dtype=int32)
    page_ends = jnp.sum(
        jnp.where(each[None, :] <= each[:, None], npages[None, :], 0), axis=1
    )
    offsets = page_ends - npages
    local = jnp.arange(pool_pages, dtype=int32)
    places = jnp.arange(total_pages, dtype=int32)
    where_at = jnp.sum(
        jnp.where(page_row[None, :] == (myself * pool_pages + local)[:, None], places[None, :], 0),
        axis=1,
    )
    owner_hot = (offsets[None, :] <= where_at[:, None]) & (page_ends[None, :] > where_at[:, None])
    left = jnp.where(
        owner_hot, length_row[None, :] - (where_at[:, None] - offsets[None, :]) * PAGE, 0
    )
    limit = jnp.clip(jnp.sum(left, axis=1), 0, PAGE)
    used = limit > 0
    ranking = jnp.where(used, where_at, total_pages + local)
    rank = jnp.sum((ranking[None, :] < ranking[:, None]).astype(int32), axis=1)
    put = rank[None, :] == local[:, None]
    order = jnp.sum(jnp.where(put, local[None, :], 0), axis=1)
    limit_at = jnp.sum(jnp.where(put, limit[None, :], 0), axis=1)
    holds = (owner_hot & used[:, None]).astype(int32)
    count = jnp.sum(holds, axis=0)
    begin = jnp.sum(jnp.where(each[None, :] < each[:, None], count[None, :], 0), axis=1)
    page_info = jnp.concatenate([order, limit_at, begin, count])

    parts, cache_copy = attend(page_info, query_all, cache[0], requests)
    ring.append(pass_on(after(ring[-1], parts), "req"))
    projected = after(projected, parts)
    parts = lax.all_to_all(parts, "blk", split_axis=0, concat_axis=0, tiled=True)

    nodes = jnp.arange(TREE, dtype=int32)
    parent_hot = (parents[0][:, None] == nodes[None, :]).astype(jnp.float32)
    my_leaf = jnp.sum(jnp.where(each == myself, leaf_row, 0))
    own, sent = tree(my_leaf.astype(int32).reshape(1), projected, parent_hot)
    if blocks == 8:
        buffers = [out_rows, *after((out_y, out_x), own)]
        buffers += [swap(buffer, "blk", 1) for buffer in buffers]
        spots = ((0, 0), (1, 0), (2, 0), (2, out_rows.shape[0]))
        spots += tuple((buffer + 3, row) for buffer, row in spots)
        shards_at = [myself ^ bits for bits in (0, 4, 2, 6, 1, 5, 3, 7)]
        feeds = [feed_rows, after(feed_y, own)]
        feeds += [swap(buffer, "blk", 1) for buffer in feeds]
    else:
        buffers = [lax.all_gather(out_rows, "blk", axis=0, tiled=True)]
        spots = ((0, 0),)
        shards_at = [jnp.zeros((), int32)]
        halves = [lax.all_gather(one, "blk", axis=0, tiled=True) for one in (w_up.T, w_down)]
        feeds = [jnp.concatenate(halves)]
    mid, mid_normed = mix(
        jnp.stack([at.astype(int32) for at in shards_at]), parts, own, tree_input, buffers, spots
    )
    if blocks == 8:
        other = swap(mid_normed, "blk", 2)
        sums = [feed(mid_normed, feeds, jnp.float32)]
        sums.append(swap(feed(other, feeds, jnp.bfloat16), "blk", 2))
    else:
        sums = [feed(mid_normed, feeds, jnp.float32)]
    layer_out, draft_rows = finish(mid, sums)
    ring.append(pass_on(after(ring[-1], layer_out), "req"))
    if blocks == 8:
        draft_rows, *sent_near = lax.optimization_barrier((draft_rows, *to_chips(sent)))
    rows_all = lax.all_gather(draft_rows, "blk", axis=0, tiled=False)

    branch = draft(rows_all, w_draft.transpose(0, 2, 1).reshape(-1, width))
    branch = lax.all_to_all(branch, "blk", split_axis=0, concat_axis=0, tiled=True)
    patch_info = jnp.stack([(my_line + lines - step) % lines for step in range(lines)])
    drafts = patch(patch_info.astype(int32), branch, layer_out, ring, heads)

    if blocks == 8:
        sent_all = to_cores(sent_near)
        sent_by = myself ^ jnp.asarray(SHARDS_AT, int32)
    else:
        sent_all = [lax.all_gather(sent, "blk", axis=0, tiled=True)]
        sent_by = each
    level_marks = jnp.asarray(LEVEL_START[1:-1], int32)
    accepted = 1 + jnp.sum((leaf_row[:, None] >= level_marks[None, :]).astype(int32), axis=1)
    block_at = (length_row // LOW * LOW)[:, None] + jnp.arange(2, dtype=int32)[None, :] * LOW
    slot = jnp.minimum(offsets[:, None] + block_at // PAGE, total_pages - 1)
    page = jnp.sum(
        jnp.where(slot[:, :, None] == places[None, None, :], page_row[None, None, :], 0), axis=2
    )
    needed = (length_row + accepted)[:, None] > block_at
    row = jnp.where(
        needed & (page // pool_pages == myself),
        page % pool_pages * PAGE + block_at % PAGE,
        -1,
    )
    shift = block_at - length_row[:, None]
    append_info = jnp.concatenate([row.reshape(-1), shift.reshape(-1), accepted, sent_by])
    cache_new = append(append_info, sent_all, cache_copy, requests)[None]
    return (layer_out, drafts, cache_new)


def solution(mesh):
    in_specs = (
        P(("req", "blk"), None),
        P("req", None, "blk", None),
        P("req", None),
        P("req", None),
        P(("req", "blk"), None),
        P("req", None),
        P(None, "blk"),
        P(None, "blk"),
        P(None, "blk"),
        P("blk", None),
        P(None, None, "blk"),
        P(None, "req"),
    )
    out_specs = (
        P(("req", "blk"), None),
        P(None, ("req", "blk"), None),
        P("req", None, "blk", None),
    )
    return jax.shard_map(
        on_device, mesh=mesh, in_specs=in_specs, out_specs=out_specs, check_vma=False
    )
```

time: 346 us -> 145 us (0.42); the launches traced: 339 us -> 144 us
  local copies, waits for them, and re-layouts: 90.3 us -> 10.2 us
  blocking collectives: 98.7 us -> 38.6 us
  Pallas kernels: 0 us -> 39 us
  matrix products: 37.7 us -> 0 us
  waiting for transfers between devices: 61.7 us -> 24 us
  other arithmetic: 25.1 us -> 6.27 us
  between operations: 17.9 us -> 0.94 us
  starting transfers between devices: 7.8 us -> 24.7 us
    reduce_scatter x3 -> x0, waiting for transfers between devices: 60.8 us -> none  [the longest x1 43.4 us: on_device(): lax.psum_scatter(num_scaled, 'blk', scatter_dimension=0, tiled=True)]
    pallas_call x0 -> x10, Pallas kernels: none -> 39 us  [the longest x1 16.9 us: attend(): pl.pallas_call(functools.partial(attend_body, pages, requests), out_shape...]
    dot_general x11 -> x0, matrix products: 36.7 us -> none  [the longest x1 10.6 us: on_device(): jnp.einsum('pqhd,pthd->pqht', query_page, keys, preferred_element_type=jn...]
    another operation x3 -> x1, local copies, waits for them, and re-layouts: 32.6 us -> 0.08 us  [on_device(): jnp.stack([at.astype(int32) for at in shards_at])]
    all_gather x5 -> x2, blocking collectives: 53 us -> 23.7 us  [the longest x1 12.6 us: on_device(): tree_all = lax.all_gather(tree_input, 'blk', axis=0, tiled=True)]
    pmax x1 -> x0, blocking collectives: 24 us -> none  [on_device(): max_all = lax.pmax(request_max, 'blk')]
    ppermute x0 -> x20, starting transfers between devices: none -> 14.2 us  [the longest x17 11.6 us: swap(): return lax.ppermute(values, axis, [(i, i ^ bits) for i in range(size)])]
    scatter x2 -> x0, local copies, waits for them, and re-layouts: 13.5 us -> none  [the longest x1 6.86 us: on_device(): new_values = cache[0, 1].at[target].set(received[:, width:], mode='drop')]
  transfers between devices with their start and end apart: 6 -> 23, of which waited for: 4 -> 12; matrix products, arithmetic and copies ran while one was open for 32% -> 5% of each run, Pallas kernels for 0% -> 23%
where the time goes in v1:
time: 145 us; the launch traced here: 144 us
  Pallas kernels  39 us (27%)
  blocking collectives  38.6 us (27%)
  starting transfers between devices  24.7 us (17%)
  waiting for transfers between devices  24 us (17%)
  local copies, waits for them, and re-layouts  10.2 us (7%)
  other arithmetic  6.27 us (4%)
    pallas_call x1, Pallas kernels, attend(): pl.pallas_call(functools.partial(attend_body, pages, requests), out_shape...  16.9 us
    all_gather x1, blocking collectives, on_device(): query_all = lax.all_gather(projected[:, :width], 'blk', axis=0, tiled=True)  14.9 us
    all_gather x1, blocking collectives, on_device(): tree_all = lax.all_gather(tree_input, 'blk', axis=0, tiled=True)  12.6 us
    ppermute x17, waiting for transfers between devices, swap(): return lax.ppermute(values, axis, [(i, i ^ bits) for i in range(size)])  11.7 us
    ppermute x17, starting transfers between devices, swap(): return lax.ppermute(values, axis, [(i, i ^ bits) for i in range(size)])  11.6 us
    all_gather x1, blocking collectives, on_device(): rows_all = lax.all_gather(draft_rows, 'blk', axis=0, tiled=False)  11.1 us
    unnamed x46, local copies, waits for them, and re-layouts  8.63 us
    all_to_all x1, waiting for transfers between devices, on_device(): lax.all_to_all(parts, 'blk', split_axis=0, concat_axis=0, tiled=True)  4.48 us
  transfers between devices with their start and end apart: 23, of which 12 were waited for; matrix products, arithmetic and copies ran while one was open for 5% of the time, Pallas kernels for 23%

profile of v1, /device:TPU:0, one launch (start us, length us, event | category | flops | bytes accessed | tf_op | source)
XLA Modules:
  0.0 143.7 jit_solution(13547697591528144861)
XLA Ops:
  0.6 12.6 %all_gather.12.tree_ref = bf16[384,1280]{1,0:T(8,128)(2,1)S(1)} all-gather(bf16[48,1280]{1,0:T(8,128)(2,1)} %tree_ref.1), channel_id=1, replica_groups=mesh['req'=4,'blk'=8] {'blk'}, dimensions={0}, use_global_device_ids=true | all-gather | bytes 1105920 | tf_op jit(solution)/shard_map/all_gather | solution.py:694
  13.3 1.3 copy-done.3
  14.5 1.6 %project.1 = bf16[8,48,480]{2,1,0:T(8,128)(2,1)} custom-call(bf16[384,1280]{1,0:T(8,128)(2,1)S(1)} %all_gather.12.tree_ref, bf16[480,1280]{1,0:T(8,128)(2,1)S(1)} %bitcast.42), custom_call_target="tpu_custom_call" | custom-call | tf_op jit(solution)/shard_map/project/pallas_call | solution.py:277
  16.2 3.5 %all-to-all-start = ((bf16[8,48,480]{2,1,0:T(8,128)(2,1)}), bf16[8,48,480]{2,1,0:T(8,128)(2,1)S(1)}, u32[]{:S(2)}, u32[]{:S(2)}) async-start(bf16[8,48,480]{2,1,0:T(8,128)(2,1)} %project.1), calls=%async_computation | async-start | bytes 786432 | tf_op jit(solution)/shard_map/all_to_all | solution.py:702
  19.6 1.9 %collective-permute-start = (bf16[160,1280]{1,0:T(8,128)(2,1)}, bf16[160,1280]{1,0:T(8,128)(2,1)S(1)}, u32[]{:S(2)}, u32[]{:S(2)}) collective-permute-start(bf16[160,1280]{1,0:T(8,128)(2,1)} %bitcast.15.rest_0_), channel_id=1, source_target_pairs={{0,4},{1,5},{2,6},{3,7},{4,0},{5,1},{6,2},{7,3},{8,12},{9,13},{10,... | collective-permute-start | bytes 1228808 | tf_op jit(solution)/shard_map/ppermute | solution.py:667
  21.6 1.6 %collective-permute-start.13 = (bf16[320,1280]{1,0:T(8,128)(2,1)}, bf16[320,1280]{1,0:T(8,128)(2,1)}, u32[]{:S(2)}, u32[]{:S(2)}) collective-permute-start(bf16[320,1280]{1,0:T(8,128)(2,1)} %bitcast.28.rest_0_), channel_id=1, source_target_pairs={{0,8},{8,16},{16,24},{24,0},{1,9},{9,17},{17,25},{25,1},{2,10},{10... | collective-permute-start | bytes 2457608 | tf_op jit(solution)/shard_map/ppermute | solution.py:662
  24.2 3.7 %all-to-all-done = bf16[8,48,480]{2,1,0:T(8,128)(2,1)S(1)} async-done(((bf16[8,48,480]{2,1,0:T(8,128)(2,1)}), bf16[8,48,480]{2,1,0:T(8,128)(2,1)S(1)}, u32[]{:S(2)}, u32[]{:S(2)}) %all-to-all-start) | async-done | bytes 368672 | tf_op jit(solution)/shard_map/all_to_all | solution.py:702
  28.8 14.9 %all_gather.13.q_ref = bf16[384,1280]{1,0:T(8,128)(2,1)} all-gather(bf16[48,1280]{1,0:T(8,128)(2,1)S(1)} %slice.4), channel_id=1, replica_groups=mesh['req'=4,'blk'=8] {'blk'}, dimensions={0}, use_global_device_ids=true | all-gather | bytes 1105920 | tf_op jit(solution)/shard_map/all_gather | solution.py:704
  43.7 2.2 %pad_maximum_fusion = bf16[320,1280]{1,0:T(8,128)(2,1)} fusion(bf16[160,1280]{1,0:T(8,128)(2,1)S(1)} %collective-permute-done.rest_1_, bf16[160,1280]{1,0:T(8,128)(2,1)} %bitcast.15.rest_0_), kind=kLoop, calls=%fused_computation | loop fusion | flops 1638400 | bytes 1638400 | tf_op jit(solution)/shard_map/concatenate | solution.py:707
  46.9 1.8 %collective-permute-start.5 = (bf16[320,1280]{1,0:T(8,128)(2,1)S(1)}, bf16[320,1280]{1,0:T(8,128)(2,1)S(1)}, u32[]{:S(2)}, u32[]{:S(2)}) collective-permute-start(bf16[320,1280]{1,0:T(8,128)(2,1)S(1)} %pad_maximum_fusion.1.rest_0_), channel_id=1, source_target_pairs={{0,4},{1,5},{2,6},{3,7},{4,0},{5,1},{6,2},{7,3},{8,12},{9,13},{10,... | collective-permute-start | bytes 2457608 | tf_op jit(solution)/shard_map/ppermute | solution.py:667
  48.7 16.9 %attend.1 = (bf16[8,48,1408]{2,1,0:T(8,128)(2,1)}, bf16[2,2048,1280]{2,1,0:T(8,128)(2,1)}) custom-call(s32[48]{0:T(128)} %pad_add_fusion.info, bf16[384,1280]{1,0:T(8,128)(2,1)} %all_gather.13.q_ref, bf16[2,2048,1280]{2,1,0:T(8,128)(2,1)} %bitcast.43), custom_call_target="tpu_custom_call" | custom-call | flops 1610612736 | bytes 26214400 | tf_op jit(solution)/shard_map/attend/pallas_call | solution.py:232
  65.6 3.6 %all-to-all-start.1 = ((bf16[8,48,1408]{2,1,0:T(8,128)(2,1)}), bf16[8,48,1408]{2,1,0:T(8,128)(2,1)S(1)}, u32[]{:S(2)}, u32[]{:S(2)}) async-start(bf16[8,48,1408]{2,1,0:T(8,128)(2,1)} %get-tuple-element.29), calls=%async_computation.1 | async-start | bytes 2162688 | tf_op jit(solution)/shard_map/all_to_all | solution.py:743
  69.9 1.6 %tree.1 = (f32[48,1408]{1,0:T(8,128)S(1)}, bf16[16,1280]{1,0:T(8,128)(2,1)S(1)}) custom-call(s32[1]{0:T(128)} %bitcast.18.info, bf16[48,3840]{1,0:T(8,128)(2,1)S(1)} %reshape.188.qkv_ref, f32[48,48]{1,0:T(8,128)S(1)} %fusion.parent_ref), custom_call_target="tpu_custom_call" | custom-call | tf_op jit(solution)/shard_map/tree/pallas_call | solution.py:337
  74.3 3.5 %collective-permute-done.2.rest_3_ = bf16[160,1280]{1,0:T(8,128)(2,1)S(1)} collective-permute-done((bf16[160,1280]{1,0:T(8,128)(2,1)}, bf16[160,1280]{1,0:T(8,128)(2,1)S(1)}, u32[]{:S(2)}, u32[]{:S(2)}) %collective-permute-start.2) | collective-permute-done | bytes 409632 | tf_op jit(solution)/shard_map/ppermute | solution.py:667
  79.1 1.3 convert_reduce_fusion.2
  80.4 4.5 %all-to-all-done.1.part_ref = bf16[8,48,1408]{2,1,0:T(8,128)(2,1)S(1)} async-done(((bf16[8,48,1408]{2,1,0:T(8,128)(2,1)}), bf16[8,48,1408]{2,1,0:T(8,128)(2,1)S(1)}, u32[]{:S(2)}, u32[]{:S(2)}) %all-to-all-start.1) | async-done | bytes 1081376 | tf_op jit(solution)/shard_map/all_to_all | solution.py:743
  84.9 1.0 copy-done.1
  88.7 3.7 %mix.1 = (bf16[48,1280]{1,0:T(8,128)(2,1)S(1)}, bf16[48,1280]{1,0:T(8,128)(2,1)S(1)}) custom-call(s32[8]{0:T(128)S(1)} %stack.50.info, bf16[8,48,1408]{2,1,0:T(8,128)(2,1)S(1)} %all-to-all-done.1.part_ref, f32[48,1408]{1,0:T(8,128)S(1)} %copy-done.9, bf16[48,1280]{1,0:T(8,128)(2,1)S(1)} %copy-done.5, bf16[160,1280]{1,0:T(8,128)(2,1)} %bitcast.15.rest_0_, ...), custom_call_target="tpu_custom_call" | custom-call | tf_op jit(solution)/shard_map/mix/pallas_call | solution.py:420
  93.1 4.3 %collective-permute-done.8.normed_ref = bf16[48,1280]{1,0:T(8,128)(2,1)S(1)} collective-permute-done((bf16[48,1280]{1,0:T(8,128)(2,1)S(1)}, bf16[48,1280]{1,0:T(8,128)(2,1)S(1)}, u32[]{:S(2)}, u32[]{:S(2)}) %collective-permute-start.8) | collective-permute-done | bytes 122912 | tf_op jit(solution)/shard_map/ppermute | solution.py:667
  97.4 2.1 %feed.3 = bf16[48,1280]{1,0:T(8,128)(2,1)S(1)} custom-call(bf16[48,1280]{1,0:T(8,128)(2,1)S(1)} %collective-permute-done.8.normed_ref, bf16[320,1280]{1,0:T(8,128)(2,1)S(1)} %pad_maximum_fusion.1.rest_0_, bf16[320,1280]{1,0:T(8,128)(2,1)S(1)} %collective-permute-done.5.rest_1_, bf16[320,1280]{1,0:T(8,128)(2,1)S(1)} %collective-permute-done.6.rest_2_, ...), custom_call_target="tpu_custom_call" | custom-call | tf_op jit(solution)/shard_map/feed/pallas_call | solution.py:447
  100.7 2.2 %feed.2.rest_0_ = f32[48,1280]{1,0:T(8,128)S(1)} custom-call(bf16[48,1280]{1,0:T(8,128)(2,1)S(1)} %get-tuple-element.36.normed_ref, bf16[320,1280]{1,0:T(8,128)(2,1)S(1)} %pad_maximum_fusion.1.rest_0_, bf16[320,1280]{1,0:T(8,128)(2,1)S(1)} %collective-permute-done.5.rest_1_, bf16[320,1280]{1,0:T(8,128)(2,1)S(1)} %collective-permute-done.6.rest_2_, ...), custom_call_target="tpu_custom_call" | custom-call | tf_op jit(solution)/shard_map/feed/pallas_call | solution.py:447
  103.5 1.0 collective-permute-done.9.rest_1_
  105.2 1.9 %finish.1 = (bf16[48,1280]{1,0:T(8,128)(2,1)}, bf16[48,1280]{1,0:T(8,128)(2,1)}) custom-call(bf16[48,1280]{1,0:T(8,128)(2,1)} %copy-done.11, f32[48,1280]{1,0:T(8,128)} %copy-done.4, bf16[48,1280]{1,0:T(8,128)(2,1)} %copy-done.16), custom_call_target="tpu_custom_call" | custom-call | tf_op jit(solution)/shard_map/finish/pallas_call | solution.py:470
  107.7 1.0 collective-permute-start.10
  108.9 2.2 %collective-permute-start.12 = (bf16[16,1280]{1,0:T(8,128)(2,1)S(1)}, bf16[16,1280]{1,0:T(8,128)(2,1)S(1)}, u32[]{:S(2)}, u32[]{:S(2)}) collective-permute-start(bf16[16,1280]{1,0:T(8,128)(2,1)S(1)} %copy-done.13), channel_id=1, source_target_pairs={{0,6},{1,7},{2,4},{3,5},{4,2},{5,3},{6,0},{7,1},{8,14},{9,15},{10,... | collective-permute-start | bytes 122888 | tf_op jit(solution)/shard_map/ppermute | solution.py:667
  112.7 1.1 collective-permute-done.12.rest_3_
  113.8 11.1 %all-gather = bf16[384,1280]{1,0:T(8,128)(2,1)S(1)} all-gather(bf16[48,1280]{1,0:T(8,128)(2,1)} %get-tuple-element.42), channel_id=2, replica_groups=mesh['req'=4,'blk'=8] {'blk'}, dimensions={0}, use_global_device_ids=true | all-gather | bytes 1105920 | tf_op jit(solution)/shard_map/all_gather | solution.py:776
  124.9 1.8 %draft.1 = bf16[8,48,640]{2,1,0:T(8,128)(2,1)} custom-call(bf16[8,48,1280]{2,1,0:T(8,128)(2,1)S(1)} %bitcast.40, bf16[640,1280]{1,0:T(8,128)(2,1)S(1)} %bitcast.41), custom_call_target="tpu_custom_call" | custom-call | tf_op jit(solution)/shard_map/draft/pallas_call | solution.py:491
  126.7 3.5 %all-to-all-start.2 = ((bf16[8,48,640]{2,1,0:T(8,128)(2,1)}), bf16[8,48,640]{2,1,0:T(8,128)(2,1)S(1)}, u32[]{:S(2)}, u32[]{:S(2)}) async-start(bf16[8,48,640]{2,1,0:T(8,128)(2,1)} %draft.1), calls=%async_computation.2 | async-start | bytes 983040 | tf_op jit(solution)/shard_map/all_to_all | solution.py:779
  132.5 3.0 %append.1 = bf16[2,2048,1280]{2,1,0:T(8,128)(2,1)} custom-call(s32[48]{0:T(128)S(1)} %pad_add_fusion.2.info, bf16[16,1280]{1,0:T(8,128)(2,1)S(1)} %copy-done.13, bf16[16,1280]{1,0:T(8,128)(2,1)S(1)} %collective-permute-done.10.rest_1_, bf16[16,1280]{1,0:T(8,128)(2,1)S(1)} %collective-permute-done.11.rest_2_, ...), custom_call_target="tpu_custom_call", output_to_operand_aliasing={{}: (9, {})} | custom-call | tf_op jit(solution)/shard_map/append/pallas_call | solution.py:624
  135.5 4.0 %all-to-all-done.2.branch_ref = bf16[8,48,640]{2,1,0:T(8,128)(2,1)S(1)} async-done(((bf16[8,48,640]{2,1,0:T(8,128)(2,1)}), bf16[8,48,640]{2,1,0:T(8,128)(2,1)S(1)}, u32[]{:S(2)}, u32[]{:S(2)}) %all-to-all-start.2) | async-done | bytes 491552 | tf_op jit(solution)/shard_map/all_to_all | solution.py:779
  139.5 4.2 %patch.1 = bf16[4,48,1280]{2,1,0:T(8,128)(2,1)} custom-call(s32[4]{0:T(128)S(1)} %pad_add_fusion.1.info, bf16[8,48,640]{2,1,0:T(8,128)(2,1)S(1)} %all-to-all-done.2.branch_ref, bf16[48,1280]{1,0:T(8,128)(2,1)S(1)} %copy-done.10, bf16[320,1280]{1,0:T(8,128)(2,1)} %bitcast.28.rest_0_, bf16[320,1280]{1,0:T(8,128)(2,1)} %collective-permute-done.13.rest_1_, ...), custom_call_target="tpu_custom_call" | custom-call | tf_op jit(solution)/shard_map/patch/pallas_call | solution.py:538
  (111 shorter events, 18.2 us)
Async XLA Ops:
  14.5 8.6 %copy-start.17 = (s32[1,8]{1,0:T(1,128)S(1)}, s32[1,8]{1,0:T(1,128)}, u32[]{:S(2)}) copy-start(s32[1,8]{1,0:T(1,128)} %param.17) | copy-start | bytes 100
  14.5 8.7 %copy-start.19 = (s32[1,128]{1,0:T(1,128)S(1)}, s32[1,128]{1,0:T(1,128)}, u32[]{:S(2)}) copy-start(s32[1,128]{1,0:T(1,128)} %param.16) | copy-start | bytes 1540
  16.2 11.8 %all-to-all-start = ((bf16[8,48,480]{2,1,0:T(8,128)(2,1)}), bf16[8,48,480]{2,1,0:T(8,128)(2,1)S(1)}, u32[]{:S(2)}, u32[]{:S(2)}) async-start(bf16[8,48,480]{2,1,0:T(8,128)(2,1)} %project.1), calls=%async_computation | async-start | bytes 786432 | tf_op jit(solution)/shard_map/all_to_all | solution.py:702
  19.6 24.1 %collective-permute-start = (bf16[160,1280]{1,0:T(8,128)(2,1)}, bf16[160,1280]{1,0:T(8,128)(2,1)S(1)}, u32[]{:S(2)}, u32[]{:S(2)}) collective-permute-start(bf16[160,1280]{1,0:T(8,128)(2,1)} %bitcast.15.rest_0_), channel_id=1, source_target_pairs={{0,4},{1,5},{2,6},{3,7},{4,0},{5,1},{6,2},{7,3},{8,12},{9,13},{10,... | collective-permute-start | bytes 1228808 | tf_op jit(solution)/shard_map/ppermute | solution.py:667
  21.6 52.3 %collective-permute-start.13 = (bf16[320,1280]{1,0:T(8,128)(2,1)}, bf16[320,1280]{1,0:T(8,128)(2,1)}, u32[]{:S(2)}, u32[]{:S(2)}) collective-permute-start(bf16[320,1280]{1,0:T(8,128)(2,1)} %bitcast.28.rest_0_), channel_id=1, source_target_pairs={{0,8},{8,16},{16,24},{24,0},{1,9},{9,17},{17,25},{25,1},{2,10},{10... | collective-permute-start | bytes 2457608 | tf_op jit(solution)/shard_map/ppermute | solution.py:662
  28.8 18.1 %copy-start.14 = (bf16[160,1280]{1,0:T(8,128)(2,1)S(1)}, bf16[160,1280]{1,0:T(8,128)(2,1)}, u32[]{:S(2)}) copy-start(bf16[160,1280]{1,0:T(8,128)(2,1)} %param.23) | copy-start | bytes 1228804
  28.8 18.1 %copy-start.15 = (bf16[1280,160]{0,1:T(8,128)(2,1)S(1)}, bf16[1280,160]{0,1:T(8,128)(2,1)}, u32[]{:S(2)}) copy-start(bf16[1280,160]{0,1:T(8,128)(2,1)} %param.22) | copy-start | bytes 1228804
  45.9 27.0 %collective-permute-start.1 = (bf16[320,1280]{1,0:T(8,128)(2,1)}, bf16[320,1280]{1,0:T(8,128)(2,1)}, u32[]{:S(2)}, u32[]{:S(2)}) collective-permute-start(bf16[320,1280]{1,0:T(8,128)(2,1)} %pad_maximum_fusion), channel_id=1, source_target_pairs={{0,2},{1,3},{2,0},{3,1},{4,6},{5,7},{6,4},{7,5},{8,10},{9,11},{10,... | collective-permute-start | bytes 2457608 | tf_op jit(solution)/shard_map/ppermute | solution.py:667
  46.9 26.9 %collective-permute-start.5 = (bf16[320,1280]{1,0:T(8,128)(2,1)S(1)}, bf16[320,1280]{1,0:T(8,128)(2,1)S(1)}, u32[]{:S(2)}, u32[]{:S(2)}) collective-permute-start(bf16[320,1280]{1,0:T(8,128)(2,1)S(1)} %pad_maximum_fusion.1.rest_0_), channel_id=1, source_target_pairs={{0,4},{1,5},{2,6},{3,7},{4,0},{5,1},{6,2},{7,3},{8,12},{9,13},{10,... | collective-permute-start | bytes 2457608 | tf_op jit(solution)/shard_map/ppermute | solution.py:667
  65.6 19.3 %all-to-all-start.1 = ((bf16[8,48,1408]{2,1,0:T(8,128)(2,1)}), bf16[8,48,1408]{2,1,0:T(8,128)(2,1)S(1)}, u32[]{:S(2)}, u32[]{:S(2)}) async-start(bf16[8,48,1408]{2,1,0:T(8,128)(2,1)} %get-tuple-element.29), calls=%async_computation.1 | async-start | bytes 2162688 | tf_op jit(solution)/shard_map/all_to_all | solution.py:743
  72.9 12.0 %collective-permute-start.4 = (bf16[320,1280]{1,0:T(8,128)(2,1)}, bf16[320,1280]{1,0:T(8,128)(2,1)}, u32[]{:S(2)}, u32[]{:S(2)}) collective-permute-start(bf16[320,1280]{1,0:T(8,128)(2,1)} %collective-permute-done.1.rest_2_), channel_id=1, source_target_pairs={{0,1},{1,0},{2,3},{3,2},{4,5},{5,4},{6,7},{7,6},{8,9},{9,8},{10,11... | collective-permute-start | bytes 2457608 | tf_op jit(solution)/shard_map/ppermute | solution.py:667
  73.3 4.5 %collective-permute-start.2 = (bf16[160,1280]{1,0:T(8,128)(2,1)}, bf16[160,1280]{1,0:T(8,128)(2,1)S(1)}, u32[]{:S(2)}, u32[]{:S(2)}) collective-permute-start(bf16[160,1280]{1,0:T(8,128)(2,1)} %bitcast.15.rest_0_), channel_id=1, source_target_pairs={{0,1},{1,0},{2,3},{3,2},{4,5},{5,4},{6,7},{7,6},{8,9},{9,8},{10,11... | collective-permute-start | bytes 1228808 | tf_op jit(solution)/shard_map/ppermute | solution.py:667
  73.4 19.7 %collective-permute-start.6 = (bf16[320,1280]{1,0:T(8,128)(2,1)S(1)}, bf16[320,1280]{1,0:T(8,128)(2,1)S(1)}, u32[]{:S(2)}, u32[]{:S(2)}) collective-permute-start(bf16[320,1280]{1,0:T(8,128)(2,1)S(1)} %pad_maximum_fusion.1.rest_0_), channel_id=1, source_target_pairs={{0,1},{1,0},{2,3},{3,2},{4,5},{5,4},{6,7},{7,6},{8,9},{9,8},{10,11... | collective-permute-start | bytes 2457608 | tf_op jit(solution)/shard_map/ppermute | solution.py:667
  73.8 19.3 %collective-permute-start.7 = (bf16[320,1280]{1,0:T(8,128)(2,1)S(1)}, bf16[320,1280]{1,0:T(8,128)(2,1)}, u32[]{:S(2)}, u32[]{:S(2)}) collective-permute-start(bf16[320,1280]{1,0:T(8,128)(2,1)S(1)} %collective-permute-done.5.rest_1_), channel_id=1, source_target_pairs={{0,1},{1,0},{2,3},{3,2},{4,5},{5,4},{6,7},{7,6},{8,9},{9,8},{10,11... | collective-permute-start | bytes 2457608 | tf_op jit(solution)/shard_map/ppermute | solution.py:667
  73.9 11.0 %collective-permute-start.3 = (bf16[160,1280]{1,0:T(8,128)(2,1)}, bf16[160,1280]{1,0:T(8,128)(2,1)}, u32[]{:S(2)}, u32[]{:S(2)}) collective-permute-start(bf16[160,1280]{1,0:T(8,128)(2,1)} %copy-done), channel_id=1, source_target_pairs={{0,1},{1,0},{2,3},{3,2},{4,5},{5,4},{6,7},{7,6},{8,9},{9,8},{10,11... | collective-permute-start | bytes 1228808 | tf_op jit(solution)/shard_map/ppermute | solution.py:667
  78.5 28.6 %collective-permute-start.14 = (bf16[320,1280]{1,0:T(8,128)(2,1)}, bf16[320,1280]{1,0:T(8,128)(2,1)}, u32[]{:S(2)}, u32[]{:S(2)}) collective-permute-start(bf16[320,1280]{1,0:T(8,128)(2,1)} %collective-permute-done.13.rest_1_), channel_id=1, source_target_pairs={{0,8},{8,16},{16,24},{24,0},{1,9},{9,17},{17,25},{25,1},{2,10},{10... | collective-permute-start | bytes 2457608 | tf_op jit(solution)/shard_map/ppermute | solution.py:662
  92.5 7.1 %copy-start.11 = (bf16[48,1280]{1,0:T(8,128)(2,1)}, bf16[48,1280]{1,0:T(8,128)(2,1)S(1)}, u32[]{:S(2)}) copy-start(bf16[48,1280]{1,0:T(8,128)(2,1)S(1)} %get-tuple-element.35.mid_ref) | copy-start | bytes 368644
  92.5 4.9 %collective-permute-start.8 = (bf16[48,1280]{1,0:T(8,128)(2,1)S(1)}, bf16[48,1280]{1,0:T(8,128)(2,1)S(1)}, u32[]{:S(2)}, u32[]{:S(2)}) collective-permute-start(bf16[48,1280]{1,0:T(8,128)(2,1)S(1)} %get-tuple-element.36.normed_ref), channel_id=1, source_target_pairs={{0,2},{1,3},{2,0},{3,1},{4,6},{5,7},{6,4},{7,5},{8,10},{9,11},{10,... | collective-permute-start | bytes 368648 | tf_op jit(solution)/shard_map/ppermute | solution.py:667
  99.6 4.9 %collective-permute-start.9 = (bf16[48,1280]{1,0:T(8,128)(2,1)S(1)}, bf16[48,1280]{1,0:T(8,128)(2,1)S(1)}, u32[]{:S(2)}, u32[]{:S(2)}) collective-permute-start(bf16[48,1280]{1,0:T(8,128)(2,1)S(1)} %feed.3), channel_id=1, source_target_pairs={{0,2},{1,3},{2,0},{3,1},{4,6},{5,7},{6,4},{7,5},{8,10},{9,11},{10,... | collective-permute-start | bytes 368648 | tf_op jit(solution)/shard_map/ppermute | solution.py:667
  100.6 6.9 %copy-start.22 = (s32[8]{0:T(128)S(1)}, s32[8]{0:T(128)}, u32[]{:S(2)}) copy-start(s32[8]{0:T(128)} %constant.131.clone) | copy-start | bytes 100
  100.6 7.0 %copy-start.13 = (bf16[16,1280]{1,0:T(8,128)(2,1)S(1)}, bf16[16,1280]{1,0:T(8,128)(2,1)}, u32[]{:S(2)}) copy-start(bf16[16,1280]{1,0:T(8,128)(2,1)} %copy-done.12) | copy-start | bytes 122884
  103.5 21.4 %copy-start.2 = (bf16[4,1280,160]{1,2,0:T(8,128)(2,1)S(1)}, bf16[4,1280,160]{1,2,0:T(8,128)(2,1)}, u32[]{:S(2)}) copy-start(bf16[4,1280,160]{1,2,0:T(8,128)(2,1)} %param.24) | copy-start | bytes 4915204
  107.1 32.4 %collective-permute-start.15 = (bf16[320,1280]{1,0:T(8,128)(2,1)}, bf16[320,1280]{1,0:T(8,128)(2,1)S(1)}, u32[]{:S(2)}, u32[]{:S(2)}) collective-permute-start(bf16[320,1280]{1,0:T(8,128)(2,1)} %collective-permute-done.14.rest_2_), channel_id=1, source_target_pairs={{0,8},{8,16},{16,24},{24,0},{1,9},{9,17},{17,25},{25,1},{2,10},{10... | collective-permute-start | bytes 2457608 | tf_op jit(solution)/shard_map/ppermute | solution.py:662
  107.7 4.3 %collective-permute-start.10 = (bf16[16,1280]{1,0:T(8,128)(2,1)S(1)}, bf16[16,1280]{1,0:T(8,128)(2,1)S(1)}, u32[]{:S(2)}, u32[]{:S(2)}) collective-permute-start(bf16[16,1280]{1,0:T(8,128)(2,1)S(1)} %copy-done.13), channel_id=1, source_target_pairs={{0,2},{1,3},{2,0},{3,1},{4,6},{5,7},{6,4},{7,5},{8,10},{9,11},{10,... | collective-permute-start | bytes 122888 | tf_op jit(solution)/shard_map/ppermute | solution.py:667
  108.7 4.0 %collective-permute-start.11 = (bf16[16,1280]{1,0:T(8,128)(2,1)S(1)}, bf16[16,1280]{1,0:T(8,128)(2,1)S(1)}, u32[]{:S(2)}, u32[]{:S(2)}) collective-permute-start(bf16[16,1280]{1,0:T(8,128)(2,1)S(1)} %copy-done.13), channel_id=1, source_target_pairs={{0,4},{1,5},{2,6},{3,7},{4,0},{5,1},{6,2},{7,3},{8,12},{9,13},{10,... | collective-permute-start | bytes 122888 | tf_op jit(solution)/shard_map/ppermute | solution.py:667
  108.9 4.9 %collective-permute-start.12 = (bf16[16,1280]{1,0:T(8,128)(2,1)S(1)}, bf16[16,1280]{1,0:T(8,128)(2,1)S(1)}, u32[]{:S(2)}, u32[]{:S(2)}) collective-permute-start(bf16[16,1280]{1,0:T(8,128)(2,1)S(1)} %copy-done.13), channel_id=1, source_target_pairs={{0,6},{1,7},{2,4},{3,5},{4,2},{5,3},{6,0},{7,1},{8,14},{9,15},{10,... | collective-permute-start | bytes 122888 | tf_op jit(solution)/shard_map/ppermute | solution.py:667
  126.7 12.8 %all-to-all-start.2 = ((bf16[8,48,640]{2,1,0:T(8,128)(2,1)}), bf16[8,48,640]{2,1,0:T(8,128)(2,1)S(1)}, u32[]{:S(2)}, u32[]{:S(2)}) async-start(bf16[8,48,640]{2,1,0:T(8,128)(2,1)} %draft.1), calls=%async_computation.2 | async-start | bytes 983040 | tf_op jit(solution)/shard_map/all_to_all | solution.py:779
  130.3 1.3 collective-permute-start.16
  130.7 1.2 collective-permute-start.17
  130.8 1.3 collective-permute-start.18
  131.2 1.2 collective-permute-start.19
  132.5 7.0 %copy-start.10 = (bf16[48,1280]{1,0:T(8,128)(2,1)S(1)}, bf16[48,1280]{1,0:T(8,128)(2,1)}, u32[]{:S(2)}) copy-start(bf16[48,1280]{1,0:T(8,128)(2,1)} %get-tuple-element.24.layer_ref) | copy-start | bytes 368644
  (14 other events, 23.3 us)

commit v2 on v1

--- a/solution.py
+++ b/solution.py
@@ -23,7 +23,6 @@
 SLOTS = 4
 LOW = 16
 SIDE = 128
-SHARDS_AT = (0, 2, 4, 6, 1, 3, 5, 7)
 LIGHT = pl.CostEstimate(flops=0, bytes_accessed=0, transcendentals=0)
 HBM = pl.BlockSpec(memory_space=pltpu.HBM)
 
@@ -254,7 +253,7 @@
             pltpu.SemaphoreType.DMA((2, pages)),
             pltpu.SemaphoreType.DMA((2, pages)),
         ],
-        compiler_params=pltpu.CompilerParams(vmem_limit_bytes=60 * 1024 * 1024),
+        compiler_params=pltpu.CompilerParams(vmem_limit_bytes=52 * 1024 * 1024),
         cost_estimate=pl.CostEstimate(
             flops=4 * pages * PAGE * H * TREE * WIN,
             bytes_accessed=5 * cache.size,
@@ -349,22 +348,17 @@
     )(info, qkv, parent_hot)
 
 
-def mix_body(spots, info, part_ref, own_ref, tree_ref, *rest):
-    count = 1 + max(buffer for buffer, _ in spots)
+def mix_body(count, info, part_ref, own_ref, tree_ref, sent_ref, *rest):
     buffers = rest[:count]
     mid_ref, normed_ref, weights, sems = rest[count:]
     blocks = part_ref.shape[0]
     width = tree_ref.shape[1]
-    rows = width // len(spots)
     copies = []
-    for index, (buffer, row) in enumerate(spots):
+    for index, buffer in enumerate(buffers):
+        rows = buffer.shape[0]
         first = pl.multiple_of(info[index] * rows, 16)
         copies.append(
-            pltpu.make_async_copy(
-                buffers[buffer].at[pl.ds(row, rows)],
-                weights.at[pl.ds(first, rows)],
-                sems.at[index],
-            )
+            pltpu.make_async_copy(buffer, weights.at[pl.ds(first, rows)], sems.at[index])
         )
     for copy in copies:
         copy.start()
@@ -412,41 +406,44 @@
     proj = dot_t(attended, weights[...]).astype(jnp.bfloat16)
     mid = (tree_ref[...].astype(jnp.float32) + proj.astype(jnp.float32)).astype(jnp.bfloat16)
     mid_ref[...] = mid
-    normed_ref[...] = rms_rows(mid)
-
-
-def mix(info, parts, own, tree_input, buffers, spots):
+    normed_ref[:TREE] = rms_rows(mid)
+    normed_ref[TREE:] = sent_ref[...]
+
+
+def mix(info, parts, own, tree_input, sent, buffers):
     width = tree_input.shape[1]
     return pl.pallas_call(
-        functools.partial(mix_body, spots),
-        out_shape=(jax.ShapeDtypeStruct((TREE, width), jnp.bfloat16),) * 2,
+        functools.partial(mix_body, len(buffers)),
+        out_shape=(
+            jax.ShapeDtypeStruct((TREE, width), jnp.bfloat16),
+            jax.ShapeDtypeStruct((TREE + LOW, width), jnp.bfloat16),
+        ),
         in_specs=[pl.BlockSpec(memory_space=pltpu.SMEM)]
-        + [pl.BlockSpec(memory_space=pltpu.VMEM)] * 3
+        + [pl.BlockSpec(memory_space=pltpu.VMEM)] * 4
         + [HBM] * len(buffers),
         out_specs=(pl.BlockSpec(memory_space=pltpu.VMEM),) * 2,
         scratch_shapes=[
             pltpu.VMEM((width, width), jnp.bfloat16),
-            pltpu.SemaphoreType.DMA((len(spots),)),
+            pltpu.SemaphoreType.DMA((len(buffers),)),
         ],
-        compiler_params=pltpu.CompilerParams(vmem_limit_bytes=40 * 1024 * 1024),
+        compiler_params=pltpu.CompilerParams(vmem_limit_bytes=60 * 1024 * 1024),
         cost_estimate=LIGHT,
         name="mix",
-    )(info, parts, own, tree_input, *buffers)
+    )(info, parts, own, tree_input, sent, *buffers)
 
 
 def feed_body(count, normed_ref, *rest):
     buffers, out_ref = rest[:count], rest[count]
-    half = buffers[0].shape[0] // 2
-    up = jnp.concatenate([buffer[:half] for buffer in buffers], axis=0)
-    down = jnp.concatenate([buffer[half:] for buffer in buffers], axis=0)
-    hidden = jax.nn.gelu(dot_t(normed_ref[...], up)).astype(jnp.bfloat16)
+    up = jnp.concatenate([buffer[: buffer.shape[0] // 2] for buffer in buffers], axis=0)
+    down = jnp.concatenate([buffer[buffer.shape[0] // 2 :] for buffer in buffers], axis=0)
+    hidden = jax.nn.gelu(dot_t(normed_ref[:TREE], up)).astype(jnp.bfloat16)
     out_ref[...] = dot_n(hidden, down).astype(out_ref.dtype)
 
 
 def feed(normed, buffers, kind):
     return pl.pallas_call(
         functools.partial(feed_body, len(buffers)),
-        out_shape=jax.ShapeDtypeStruct(normed.shape, kind),
+        out_shape=jax.ShapeDtypeStruct((TREE, normed.shape[1]), kind),
         in_specs=[pl.BlockSpec(memory_space=pltpu.VMEM)] * (1 + len(buffers)),
         out_specs=pl.BlockSpec(memory_space=pltpu.VMEM),
         compiler_params=pltpu.CompilerParams(vmem_limit_bytes=24 * 1024 * 1024),
@@ -472,6 +469,7 @@
         out_shape=(jax.ShapeDtypeStruct(mid.shape, jnp.bfloat16),) * 2,
         in_specs=[pl.BlockSpec(memory_space=pltpu.VMEM)] * (1 + len(parts)),
         out_specs=(pl.BlockSpec(memory_space=pltpu.VMEM),) * 2,
+        compiler_params=pltpu.CompilerParams(vmem_limit_bytes=8 * 1024 * 1024),
         cost_estimate=LIGHT,
         name="finish",
     )(mid, *parts)
@@ -505,11 +503,13 @@
     blocks, _, columns = branch_ref.shape
     piece = columns // heads
     copies = []
+    half = buffers[-1].shape[0]
     for index, buffer in enumerate(buffers):
-        rows = buffer.shape[0]
-        first = pl.multiple_of(info[index] * rows, 16)
+        first = pl.multiple_of(info[index] * half, 16)
         copies.append(
-            pltpu.make_async_copy(buffer, weights.at[pl.ds(first, rows)], sems.at[index])
+            pltpu.make_async_copy(
+                buffer, weights.at[pl.ds(first, buffer.shape[0])], sems.at[index]
+            )
         )
     for copy in copies:
         copy.start()
@@ -578,13 +578,11 @@
         return carry
 
     def merge(index, carry):
-        entry = index // 2
-        request = info[5 * requests + entry]
-        index = 2 * request + index % 2
+        request = index // 2
 
         @pl.when(info[index] >= 0)
         def _():
-            fresh = rows[entry].astype(jnp.float32)
+            fresh = rows[pl.ds(pl.multiple_of(request * LOW, LOW), LOW)].astype(jnp.float32)
             step = (
                 lax.broadcasted_iota(jnp.int32, (LOW, fresh.shape[1]), 0)
                 + info[2 * requests + index]
@@ -610,10 +608,12 @@
         return carry
 
     lax.fori_loop(0, 2 * requests, fetch, 0)
-    each = requests // count
-    for index in range(count):
-        for entry in range(each):
-            rows[index * each + entry] = sent[index][entry * LOW : (entry + 1) * LOW]
+    entry = 0
+    for buffer in sent:
+        for first in range(0, buffer.shape[0], LOW):
+            place = pl.multiple_of(info[5 * requests + entry] * LOW, LOW)
+            rows[pl.ds(place, LOW)] = buffer[first : first + LOW]
+            entry += 1
     lax.fori_loop(0, 2 * requests, merge, 0)
     lax.fori_loop(0, 2 * requests, settle, 0)
 
@@ -630,7 +630,7 @@
         out_specs=HBM,
         input_output_aliases={1 + count: 0},
         scratch_shapes=[
-            pltpu.VMEM((requests, LOW, width), jnp.bfloat16),
+            pltpu.VMEM((requests * LOW, width), jnp.bfloat16),
             pltpu.VMEM((2 * requests, 2, LOW, width), jnp.bfloat16),
             pltpu.SemaphoreType.DMA((2 * requests, 2)),
             pltpu.SemaphoreType.DMA((2 * requests, 2)),
@@ -643,18 +643,6 @@
 
 def after(values, earlier):
     return lax.optimization_barrier((values, earlier))[0]
-
-
-def to_chips(shard):
-    if lax.axis_size("blk") != 8:
-        return [lax.all_gather(shard, "blk", axis=0, tiled=True)]
-    return [shard] + [swap(shard, "blk", bits) for bits in (2, 4, 6)]
-
-
-def to_cores(shards):
-    if lax.axis_size("blk") != 8:
-        return shards
-    return shards + [swap(shard, "blk", 1) for shard in shards]
 
 
 def pass_on(values, axis):
@@ -691,22 +679,6 @@
     heads = w_draft.shape[0]
     int32 = jnp.int32
 
-    tree_all = lax.all_gather(tree_input, "blk", axis=0, tiled=True)
-    projected = project(tree_all, w_qkv.T)
-    out_rows = w_out.T
-    feed_rows = jnp.concatenate([w_up.T, w_down])
-    if blocks == 8:
-        out_y = swap(after(out_rows, projected), "blk", 4)
-    ring = [after(w_patch.T, projected)]
-    ring.append(pass_on(ring[-1], "req"))
-    projected = lax.all_to_all(projected, "blk", split_axis=0, concat_axis=0, tiled=True)
-    projected = projected.transpose(1, 0, 2).reshape(tree_input.shape[0], -1)
-    query_all = lax.all_gather(projected[:, :width], "blk", axis=0, tiled=True)
-    if blocks == 8:
-        query_all, out_y = lax.optimization_barrier((query_all, out_y))
-        out_x = swap(jnp.concatenate([out_rows, out_y]), "blk", 2)
-        feed_y = swap(after(feed_rows, query_all), "blk", 4)
-
     page_row, length_row, leaf_row = page_table[0], lengths[0], accept_leaf[0]
     total_pages = page_row.shape[0]
     npages = (length_row + DEPTH + PAGE - 1) // PAGE
@@ -737,55 +709,20 @@
     begin = jnp.sum(jnp.where(each[None, :] < each[:, None], count[None, :], 0), axis=1)
     page_info = jnp.concatenate([order, limit_at, begin, count])
 
-    parts, cache_copy = attend(page_info, query_all, cache[0], requests)
-    ring.append(pass_on(after(ring[-1], parts), "req"))
-    projected = after(projected, parts)
-    parts = lax.all_to_all(parts, "blk", split_axis=0, concat_axis=0, tiled=True)
-
     nodes = jnp.arange(TREE, dtype=int32)
     parent_hot = (parents[0][:, None] == nodes[None, :]).astype(jnp.float32)
     my_leaf = jnp.sum(jnp.where(each == myself, leaf_row, 0))
-    own, sent = tree(my_leaf.astype(int32).reshape(1), projected, parent_hot)
+    leaf_info = my_leaf.astype(int32).reshape(1)
     if blocks == 8:
-        buffers = [out_rows, *after((out_y, out_x), own)]
-        buffers += [swap(buffer, "blk", 1) for buffer in buffers]
-        spots = ((0, 0), (1, 0), (2, 0), (2, out_rows.shape[0]))
-        spots += tuple((buffer + 3, row) for buffer, row in spots)
-        shards_at = [myself ^ bits for bits in (0, 4, 2, 6, 1, 5, 3, 7)]
-        feeds = [feed_rows, after(feed_y, own)]
-        feeds += [swap(buffer, "blk", 1) for buffer in feeds]
+        mix_info = myself ^ jnp.asarray((0, 4, 2, 6, 1, 5, 3, 7), int32)
+        sent_by = myself ^ jnp.asarray((0, 2, 4, 6, 1, 3, 5, 7), int32)
     else:
-        buffers = [lax.all_gather(out_rows, "blk", axis=0, tiled=True)]
-        spots = ((0, 0),)
-        shards_at = [jnp.zeros((), int32)]
-        halves = [lax.all_gather(one, "blk", axis=0, tiled=True) for one in (w_up.T, w_down)]
-        feeds = [jnp.concatenate(halves)]
-    mid, mid_normed = mix(
-        jnp.stack([at.astype(int32) for at in shards_at]), parts, own, tree_input, buffers, spots
-    )
-    if blocks == 8:
-        other = swap(mid_normed, "blk", 2)
-        sums = [feed(mid_normed, feeds, jnp.float32)]
-        sums.append(swap(feed(other, feeds, jnp.bfloat16), "blk", 2))
-    else:
-        sums = [feed(mid_normed, feeds, jnp.float32)]
-    layer_out, draft_rows = finish(mid, sums)
-    ring.append(pass_on(after(ring[-1], layer_out), "req"))
-    if blocks == 8:
-        draft_rows, *sent_near = lax.optimization_barrier((draft_rows, *to_chips(sent)))
-    rows_all = lax.all_gather(draft_rows, "blk", axis=0, tiled=False)
-
-    branch = draft(rows_all, w_draft.transpose(0, 2, 1).reshape(-1, width))
-    branch = lax.all_to_all(branch, "blk", split_axis=0, concat_axis=0, tiled=True)
-    patch_info = jnp.stack([(my_line + lines - step) % lines for step in range(lines)])
-    drafts = patch(patch_info.astype(int32), branch, layer_out, ring, heads)
-
-    if blocks == 8:
-        sent_all = to_cores(sent_near)
-        sent_by = myself ^ jnp.asarray(SHARDS_AT, int32)
-    else:
-        sent_all = [lax.all_gather(sent, "blk", axis=0, tiled=True)]
+        mix_info = jnp.zeros((1,), int32)
         sent_by = each
+    others = 2 * ((my_line + lines - jnp.arange(1, lines, dtype=int32)) % lines)
+    patch_info = jnp.concatenate(
+        [2 * my_line.reshape(1), others + myself % 2, others + (myself ^ 1) % 2]
+    )
     level_marks = jnp.asarray(LEVEL_START[1:-1], int32)
     accepted = 1 + jnp.sum((leaf_row[:, None] >= level_marks[None, :]).astype(int32), axis=1)
     block_at = (length_row // LOW * LOW)[:, None] + jnp.arange(2, dtype=int32)[None, :] * LOW
@@ -801,6 +738,85 @@
     )
     shift = block_at - length_row[:, None]
     append_info = jnp.concatenate([row.reshape(-1), shift.reshape(-1), accepted, sent_by])
+
+    tree_all = lax.all_gather(tree_input, "blk", axis=0, tiled=True)
+    projected = project(tree_all, w_qkv.T)
+    out_rows = w_out.T
+    feed_rows = jnp.concatenate([w_up.T, w_down])
+    if blocks == 8:
+        out_y = swap(after(out_rows, projected), "blk", 4)
+        out_x = swap(after(out_rows, projected), "blk", 2)
+        few = w_down.shape[0] // 2
+        feed_half = jnp.concatenate(
+            [
+                lax.dynamic_slice_in_dim(one, my_line % 2 * few, few, 0)
+                for one in (w_up.T, w_down)
+            ]
+        )
+    half_rows = w_patch.shape[1] // 2
+    my_half = lax.dynamic_slice_in_dim(w_patch.T, myself % 2 * half_rows, half_rows, 0)
+    ring = [pass_on(after(my_half, projected), "req")]
+    projected = lax.all_to_all(projected, "blk", split_axis=0, concat_axis=0, tiled=True)
+    projected, page_info, append_info, leaf_info, mix_info, patch_info, parent_hot = (
+        lax.optimization_barrier(
+            (projected, page_info, append_info, leaf_info, mix_info, patch_info, parent_hot)
+        )
+    )
+    projected = projected.transpose(1, 0, 2).reshape(tree_input.shape[0], -1)
+    query_all = lax.all_gather(projected[:, :width], "blk", axis=0, tiled=True)
+    query_all, ring[0] = lax.optimization_barrier((query_all, ring[0]))
+    if blocks == 8:
+        query_all, out_y, out_x = lax.optimization_barrier((query_all, out_y, out_x))
+        out_xy = swap(out_y, "blk", 2)
+        feed_y = swap(after(feed_half, query_all), "blk", 4)
+
+    parts, cache_copy = attend(page_info, query_all, cache[0], requests)
+    if blocks == 8:
+        parts, out_xy, feed_y = lax.optimization_barrier((parts, out_xy, feed_y))
+        feed_z = swap(feed_y, "req", 1)
+        buffers = [out_rows, out_y, out_x, out_xy]
+        buffers += [swap(buffer, "blk", 1) for buffer in after(tuple(buffers), parts)]
+    else:
+        buffers = [lax.all_gather(out_rows, "blk", axis=0, tiled=True)]
+    projected, *buffers = lax.optimization_barrier((projected, *buffers))
+    parts = lax.all_to_all(parts, "blk", split_axis=0, concat_axis=0, tiled=True)
+
+    own, sent = tree(leaf_info, projected, parent_hot)
+    ring.append(pass_on(after(ring[-1], own), "req"))
+    parts, own = lax.optimization_barrier((parts, own))
+    if blocks == 8:
+        feeds = [feed_rows, *after((feed_y, feed_z), own)]
+        feeds += [swap(buffer, "blk", 1) for buffer in feeds]
+    else:
+        halves = [lax.all_gather(one, "blk", axis=0, tiled=True) for one in (w_up.T, w_down)]
+        feeds = [jnp.concatenate(halves)]
+    mid, mid_normed = mix(mix_info, parts, own, tree_input, sent, buffers)
+    mid, ring[-1] = lax.optimization_barrier((mid, ring[-1]))
+    sums = [feed(mid_normed, feeds, jnp.float32)]
+    if blocks == 8:
+        other, sums[0] = lax.optimization_barrier((swap(mid_normed, "blk", 2), sums[0]))
+        sent_all = [jnp.concatenate([sent, other[TREE:]])]
+        other = feed(other, feeds, jnp.bfloat16)
+        sent_all.append(swap(after(sent_all[0], other), "blk", 4))
+        ring.append(pass_on(after(ring[-1], other), "req"))
+        sums.append(swap(other, "blk", 2))
+    else:
+        ring.append(pass_on(after(ring[-1], sums[0]), "req"))
+    layer_out, draft_rows = finish(mid, sums)
+    rows_all = lax.all_gather(draft_rows, "blk", axis=0, tiled=False)
+    if blocks == 8:
+        rows_all, ring[-1], sent_all[-1] = lax.optimization_barrier(
+            (rows_all, ring[-1], sent_all[-1])
+        )
+        sent_all += [swap(rows, "blk", 1) for rows in after(tuple(sent_all), rows_all)]
+    else:
+        sent_all = [lax.all_gather(sent, "blk", axis=0, tiled=True)]
+    ring += [swap(after(half, rows_all), "blk", 1) for half in ring]
+
+    branch = draft(rows_all, w_draft.transpose(0, 2, 1).reshape(-1, width))
+    branch = lax.all_to_all(branch, "blk", split_axis=0, concat_axis=0, tiled=True)
+    drafts = patch(patch_info, branch, layer_out, [w_patch.T, *ring], heads)
+
     cache_new = append(append_info, sent_all, cache_copy, requests)[None]
     return (layer_out, drafts, cache_new)
 

time: 145 us -> 129 us (0.89); the launches traced: 144 us -> 129 us
  local copies, waits for them, and re-layouts: 10.2 us -> 5.87 us
  other arithmetic: 6.27 us -> 2.99 us
  blocking collectives: 38.6 us -> 35.5 us
  Pallas kernels: 39 us -> 37.5 us
  waiting for transfers between devices: 24 us -> 22.5 us
    unnamed x46 -> x44, local copies, waits for them, and re-layouts: 8.63 us -> 3.61 us
    all_to_all x1, waiting for transfers between devices: 4.48 us -> 8.94 us  [on_device(): lax.all_to_all(parts, 'blk', split_axis=0, concat_axis=0, tiled=True)]
    all_to_all x1, waiting for transfers between devices: 3.75 us -> 0.01 us  [on_device(): lax.all_to_all(projected, 'blk', split_axis=0, concat_axis=0, tiled=True)]
    ppermute x17 -> x20, waiting for transfers between devices: 11.7 us -> 9.21 us  [swap(): return lax.ppermute(values, axis, [(i, i ^ bits) for i in range(size)])]
    concatenate x1 -> x3, other arithmetic: 2.16 us -> 0.11 us  [the longest x1 0.08 us: on_device(): jnp.concatenate([2 * my_line.reshape(1), others + myself % 2, others + (m...]
    all_gather x1, blocking collectives: 14.9 us -> 13 us  [on_device(): query_all = lax.all_gather(projected[:, :width], 'blk', axis=0, tiled=True)]
    pallas_call x1, Pallas kernels: 3.73 us -> 5.27 us  [mix(): pl.pallas_call(functools.partial(mix_body, len(buffers)), out_shape=(jax....]
    ppermute x17 -> x20, starting transfers between devices: 11.6 us -> 11 us  [swap(): return lax.ppermute(values, axis, [(i, i ^ bits) for i in range(size)])]
  transfers between devices with their start and end apart: 23 -> 26, of which waited for: 12 -> 11; matrix products, arithmetic and copies ran while one was open for 5% -> 4% of each run, Pallas kernels for 23% -> 22%
where the time goes in v2:
time: 129 us
  Pallas kernels  37.5 us (29%)
  blocking collectives  35.5 us (28%)
  starting transfers between devices  24 us (19%)
  waiting for transfers between devices  22.5 us (17%)
  local copies, waits for them, and re-layouts  5.87 us (5%)
  other arithmetic  2.99 us (2%)
    pallas_call x1, Pallas kernels, attend(): pl.pallas_call(functools.partial(attend_body, pages, requests), out_shape...  15.7 us
    all_gather x1, blocking collectives, on_device(): query_all = lax.all_gather(projected[:, :width], 'blk', axis=0, tiled=True)  13 us
    all_gather x1, blocking collectives, on_device(): tree_all = lax.all_gather(tree_input, 'blk', axis=0, tiled=True)  12.6 us
    ppermute x20, starting transfers between devices, swap(): return lax.ppermute(values, axis, [(i, i ^ bits) for i in range(size)])  11 us
    all_gather x1, blocking collectives, on_device(): rows_all = lax.all_gather(draft_rows, 'blk', axis=0, tiled=False)  9.86 us
    ppermute x20, waiting for transfers between devices, swap(): return lax.ppermute(values, axis, [(i, i ^ bits) for i in range(size)])  9.21 us
    all_to_all x1, waiting for transfers between devices, on_device(): lax.all_to_all(parts, 'blk', split_axis=0, concat_axis=0, tiled=True)  8.94 us
    pallas_call x1, Pallas kernels, mix(): pl.pallas_call(functools.partial(mix_body, len(buffers)), out_shape=(jax....  5.27 us
  transfers between devices with their start and end apart: 26, of which 11 were waited for; matrix products, arithmetic and copies ran while one was open for 4% of the time, Pallas kernels for 22%

profile of v2, /device:TPU:0, one launch (start us, length us, event | category | flops | bytes accessed | tf_op | source)
XLA Modules:
  0.0 129.3 jit_solution(7002252030654437228)
XLA Ops:
  0.6 12.6 %all_gather.12.tree_ref = bf16[384,1280]{1,0:T(8,128)(2,1)S(1)} all-gather(bf16[48,1280]{1,0:T(8,128)(2,1)} %tree_ref.1), channel_id=1, replica_groups=mesh['req'=4,'blk'=8] {'blk'}, dimensions={0}, use_global_device_ids=true | all-gather | bytes 1105920 | tf_op jit(solution)/shard_map/all_gather | solution.py:742
  13.3 1.3 copy-done.2
  14.6 1.6 %project.1 = bf16[8,48,480]{2,1,0:T(8,128)(2,1)} custom-call(bf16[384,1280]{1,0:T(8,128)(2,1)S(1)} %all_gather.12.tree_ref, bf16[480,1280]{1,0:T(8,128)(2,1)S(1)} %bitcast.36), custom_call_target="tpu_custom_call" | custom-call | tf_op jit(solution)/shard_map/project/pallas_call | solution.py:276
  16.2 3.6 %all-to-all-start = ((bf16[8,48,480]{2,1,0:T(8,128)(2,1)}), bf16[8,48,480]{2,1,0:T(8,128)(2,1)S(1)}, u32[]{:S(2)}, u32[]{:S(2)}) async-start(bf16[8,48,480]{2,1,0:T(8,128)(2,1)} %project.1), calls=%async_computation | async-start | bytes 786432 | tf_op jit(solution)/shard_map/all_to_all | solution.py:759
  19.8 1.9 %collective-permute-start.1 = (bf16[160,1280]{1,0:T(8,128)(2,1)}, bf16[160,1280]{1,0:T(8,128)(2,1)}, u32[]{:S(2)}, u32[]{:S(2)}) collective-permute-start(bf16[160,1280]{1,0:T(8,128)(2,1)} %bitcast.12.rest_0_), channel_id=1, source_target_pairs={{0,4},{1,5},{2,6},{3,7},{4,0},{5,1},{6,2},{7,3},{8,12},{9,13},{10,... | collective-permute-start | bytes 1228808 | tf_op jit(solution)/shard_map/ppermute | solution.py:655
  21.7 1.5 %collective-permute-start.2 = (bf16[160,1280]{1,0:T(8,128)(2,1)}, bf16[160,1280]{1,0:T(8,128)(2,1)}, u32[]{:S(2)}, u32[]{:S(2)}) collective-permute-start(bf16[160,1280]{1,0:T(8,128)(2,1)} %bitcast.12.rest_0_), channel_id=1, source_target_pairs={{0,2},{1,3},{2,0},{3,1},{4,6},{5,7},{6,4},{7,5},{8,10},{9,11},{10,... | collective-permute-start | bytes 1228808 | tf_op jit(solution)/shard_map/ppermute | solution.py:655
  23.2 0.8 dynamic-slice_bitcast_fusion
  24.0 1.6 %collective-permute-start = (bf16[160,1280]{1,0:T(8,128)(2,1)}, bf16[160,1280]{1,0:T(8,128)(2,1)}, u32[]{:S(2)}, u32[]{:S(2)}) collective-permute-start(bf16[160,1280]{1,0:T(8,128)(2,1)} %dynamic-slice_bitcast_fusion), channel_id=1, source_target_pairs={{0,8},{8,16},{16,24},{24,0},{1,9},{9,17},{17,25},{25,1},{2,10},{10... | collective-permute-start | bytes 1228808 | tf_op jit(solution)/shard_map/ppermute | solution.py:650
  28.2 1.1 fusion.10
  30.1 13.0 %all_gather.13.q_ref = bf16[384,1280]{1,0:T(8,128)(2,1)S(1)} all-gather(bf16[48,1280]{1,0:T(8,128)(2,1)S(1)} %slice.8), channel_id=1, replica_groups=mesh['req'=4,'blk'=8] {'blk'}, dimensions={0}, use_global_device_ids=true | all-gather | bytes 1105920 | tf_op jit(solution)/shard_map/all_gather | solution.py:766
  43.6 1.7 %collective-permute-start.4 = (bf16[160,1280]{1,0:T(8,128)(2,1)S(1)}, bf16[160,1280]{1,0:T(8,128)(2,1)S(1)}, u32[]{:S(2)}, u32[]{:S(2)}) collective-permute-start(bf16[160,1280]{1,0:T(8,128)(2,1)S(1)} %pad_maximum_fusion.1), channel_id=1, source_target_pairs={{0,4},{1,5},{2,6},{3,7},{4,0},{5,1},{6,2},{7,3},{8,12},{9,13},{10,... | collective-permute-start | bytes 1228808 | tf_op jit(solution)/shard_map/ppermute | solution.py:655
  45.3 15.7 %attend.1 = (bf16[8,48,1408]{2,1,0:T(8,128)(2,1)}, bf16[2,2048,1280]{2,1,0:T(8,128)(2,1)}) custom-call(s32[48]{0:T(128)S(1)} %pad_add_fusion.info, bf16[384,1280]{1,0:T(8,128)(2,1)S(1)} %all_gather.13.q_ref, bf16[2,2048,1280]{2,1,0:T(8,128)(2,1)} %bitcast.37), custom_call_target="tpu_custom_call" | custom-call | flops 1610612736 | bytes 26214400 | tf_op jit(solution)/shard_map/attend/pallas_call | solution.py:231
  61.0 4.3 %all-to-all-start.1 = ((bf16[8,48,1408]{2,1,0:T(8,128)(2,1)}), bf16[8,48,1408]{2,1,0:T(8,128)(2,1)}, u32[]{:S(2)}, u32[]{:S(2)}) async-start(bf16[8,48,1408]{2,1,0:T(8,128)(2,1)} %get-tuple-element.71), calls=%async_computation.1 | async-start | bytes 2162688 | tf_op jit(solution)/shard_map/all_to_all | solution.py:782
  66.4 0.9 collective-permute-done.5.rest_4_
  69.0 1.6 %tree.1 = (f32[48,1408]{1,0:T(8,128)S(1)}, bf16[16,1280]{1,0:T(8,128)(2,1)S(1)}) custom-call(s32[1]{0:T(128)} %bitcast.7.info, bf16[48,3840]{1,0:T(8,128)(2,1)S(1)} %reshape.192.qkv_ref, f32[48,48]{1,0:T(8,128)S(1)} %fusion.parent_ref), custom_call_target="tpu_custom_call" | custom-call | tf_op jit(solution)/shard_map/tree/pallas_call | solution.py:336
  70.7 0.7 copy-done.3
  72.1 8.9 %all-to-all-done.1.part_ref = bf16[8,48,1408]{2,1,0:T(8,128)(2,1)} async-done(((bf16[8,48,1408]{2,1,0:T(8,128)(2,1)}), bf16[8,48,1408]{2,1,0:T(8,128)(2,1)}, u32[]{:S(2)}, u32[]{:S(2)}) %all-to-all-start.1) | async-done | bytes 1081376 | tf_op jit(solution)/shard_map/all_to_all | solution.py:782
  81.6 5.3 %mix.1 = (bf16[48,1280]{1,0:T(8,128)(2,1)}, bf16[64,1280]{1,0:T(8,128)(2,1)}) custom-call(s32[8]{0:T(128)} %get-tuple-element.61.info, bf16[8,48,1408]{2,1,0:T(8,128)(2,1)} %all-to-all-done.1.part_ref, f32[48,1408]{1,0:T(8,128)} %copy-done.3, bf16[48,1280]{1,0:T(8,128)(2,1)} %tree_ref.1, bf16[16,1280]{1,0:T(8,128)(2,1)} %copy-done.4, ...), custom_call_target="tpu_custom_call" | custom-call | tf_op jit(solution)/shard_map/mix/pallas_call | solution.py:415
  87.4 1.0 collective-permute-done.9.rest_2_
  88.5 0.9 copy-done.6
  89.4 2.1 %feed.2.rest_0_ = f32[48,1280]{1,0:T(8,128)S(1)} custom-call(bf16[64,1280]{1,0:T(8,128)(2,1)S(1)} %copy-done.6, bf16[320,1280]{1,0:T(8,128)(2,1)S(1)} %pad_maximum_fusion.rest_0_, bf16[160,1280]{1,0:T(8,128)(2,1)S(1)} %collective-permute-done.4.rest_1_, bf16[160,1280]{1,0:T(8,128)(2,1)} %collective-permute-done.11.rest_2_, ...), custom_call_target="tpu_custom_call" | custom-call | tf_op jit(solution)/shard_map/feed/pallas_call | solution.py:444
  91.5 1.7 %collective-permute-done.10.normed_ref = bf16[64,1280]{1,0:T(8,128)(2,1)S(1)} collective-permute-done((bf16[64,1280]{1,0:T(8,128)(2,1)}, bf16[64,1280]{1,0:T(8,128)(2,1)S(1)}, u32[]{:S(2)}, u32[]{:S(2)}) %collective-permute-start.10) | collective-permute-done | bytes 163872 | tf_op jit(solution)/shard_map/ppermute | solution.py:655
  93.2 2.2 %feed.3 = bf16[48,1280]{1,0:T(8,128)(2,1)S(1)} custom-call(bf16[64,1280]{1,0:T(8,128)(2,1)S(1)} %collective-permute-done.10.normed_ref, bf16[320,1280]{1,0:T(8,128)(2,1)S(1)} %pad_maximum_fusion.rest_0_, bf16[160,1280]{1,0:T(8,128)(2,1)S(1)} %collective-permute-done.4.rest_1_, bf16[160,1280]{1,0:T(8,128)(2,1)} %collective-permute-done.11.rest_2_, ...), custom_call_target="tpu_custom_call" | custom-call | tf_op jit(solution)/shard_map/feed/pallas_call | solution.py:444
  96.1 0.9 collective-permute-start.17
  97.0 3.3 %collective-permute-done.15.rest_1_ = bf16[48,1280]{1,0:T(8,128)(2,1)S(1)} collective-permute-done((bf16[48,1280]{1,0:T(8,128)(2,1)S(1)}, bf16[48,1280]{1,0:T(8,128)(2,1)S(1)}, u32[]{:S(2)}, u32[]{:S(2)}) %collective-permute-start.15) | collective-permute-done | bytes 122912 | tf_op jit(solution)/shard_map/ppermute | solution.py:655
  101.0 9.9 %all-gather = bf16[384,1280]{1,0:T(8,128)(2,1)S(1)} all-gather(bf16[48,1280]{1,0:T(8,128)(2,1)S(1)} %get-tuple-element.105), channel_id=2, replica_groups=mesh['req'=4,'blk'=8] {'blk'}, dimensions={0}, use_global_device_ids=true | all-gather | bytes 1105920 | tf_op jit(solution)/shard_map/all_gather | solution.py:806
  110.9 1.8 %draft.1 = bf16[8,48,640]{2,1,0:T(8,128)(2,1)} custom-call(bf16[8,48,1280]{2,1,0:T(8,128)(2,1)S(1)} %bitcast.33, bf16[640,1280]{1,0:T(8,128)(2,1)S(1)} %bitcast.35), custom_call_target="tpu_custom_call" | custom-call | tf_op jit(solution)/shard_map/draft/pallas_call | solution.py:489
  112.7 3.5 %all-to-all-start.2 = ((bf16[8,48,640]{2,1,0:T(8,128)(2,1)}), bf16[8,48,640]{2,1,0:T(8,128)(2,1)S(1)}, u32[]{:S(2)}, u32[]{:S(2)}) async-start(bf16[8,48,640]{2,1,0:T(8,128)(2,1)} %draft.1), calls=%async_computation.2 | async-start | bytes 983040 | tf_op jit(solution)/shard_map/all_to_all | solution.py:817
  117.6 1.7 %collective-permute-done.21.rest_2_ = bf16[32,1280]{1,0:T(8,128)(2,1)S(1)} collective-permute-done((bf16[32,1280]{1,0:T(8,128)(2,1)S(1)}, bf16[32,1280]{1,0:T(8,128)(2,1)S(1)}, u32[]{:S(2)}, u32[]{:S(2)}) %collective-permute-start.21) | collective-permute-done | bytes 81952 | tf_op jit(solution)/shard_map/ppermute | solution.py:655
  119.4 2.8 %append.1 = bf16[2,2048,1280]{2,1,0:T(8,128)(2,1)} custom-call(s32[48]{0:T(128)S(1)} %pad_add_fusion.1.info, bf16[32,1280]{1,0:T(8,128)(2,1)S(1)} %pad_maximum_fusion.2.rest_0_, bf16[32,1280]{1,0:T(8,128)(2,1)S(1)} %collective-permute-done.17.rest_1_, bf16[32,1280]{1,0:T(8,128)(2,1)S(1)} %collective-permute-done.21.rest_2_, ...), custom_call_target="tpu_custom_call", output_to_operand_aliasing={{}: (5, {})} | custom-call | tf_op jit(solution)/shard_map/append/pallas_call | solution.py:624
  122.2 3.3 %all-to-all-done.2.branch_ref = bf16[8,48,640]{2,1,0:T(8,128)(2,1)S(1)} async-done(((bf16[8,48,640]{2,1,0:T(8,128)(2,1)}), bf16[8,48,640]{2,1,0:T(8,128)(2,1)S(1)}, u32[]{:S(2)}, u32[]{:S(2)}) %all-to-all-start.2) | async-done | bytes 491552 | tf_op jit(solution)/shard_map/all_to_all | solution.py:817
  125.5 3.8 %patch.1 = bf16[4,48,1280]{2,1,0:T(8,128)(2,1)} custom-call(s32[7]{0:T(128)S(1)} %pad_add_fusion.2.info, bf16[8,48,640]{2,1,0:T(8,128)(2,1)S(1)} %all-to-all-done.2.branch_ref, bf16[48,1280]{1,0:T(8,128)(2,1)S(1)} %copy-done.7, bf16[320,1280]{1,0:T(8,128)(2,1)S(1)} %bitcast.34, bf16[160,1280]{1,0:T(8,128)(2,1)} %collective-permute-done.rest_1_, ...), custom_call_target="tpu_custom_call" | custom-call | tf_op jit(solution)/shard_map/patch/pallas_call | solution.py:538
  (119 shorter events, 11.4 us)
Async XLA Ops:
  14.6 11.8 %copy-start.21 = (s32[4]{0:T(128)S(1)}, s32[4]{0:T(128)}, u32[]{:S(2)}) copy-start(s32[4]{0:T(128)} %constant.144.clone) | copy-start | bytes 52
  14.6 13.0 %copy-start.20 = (s32[8]{0:T(128)S(1)}, s32[8]{0:T(128)}, u32[]{:S(2)}) copy-start(s32[8]{0:T(128)} %constant.143.clone) | copy-start | bytes 100
  14.6 13.0 %copy-start.17 = (s32[1,48]{1,0:T(1,128)S(1)}, s32[1,48]{1,0:T(1,128)}, u32[]{:S(2)}) copy-start(s32[1,48]{1,0:T(1,128)} %param.19) | copy-start | bytes 580
  14.6 13.1 %copy-start.9 = (bf16[160,1280]{1,0:T(8,128)(2,1)S(1)}, bf16[160,1280]{1,0:T(8,128)(2,1)}, u32[]{:S(2)}) copy-start(bf16[160,1280]{1,0:T(8,128)(2,1)} %param.24) | copy-start | bytes 1228804
  16.2 12.0 %copy-start.19 = (s32[8]{0:T(128)S(1)}, s32[8]{0:T(128)}, u32[]{:S(2)}) copy-start(s32[8]{0:T(128)} %constant.142.clone) | copy-start | bytes 100
  16.2 13.1 %all-to-all-start = ((bf16[8,48,480]{2,1,0:T(8,128)(2,1)}), bf16[8,48,480]{2,1,0:T(8,128)(2,1)S(1)}, u32[]{:S(2)}, u32[]{:S(2)}) async-start(bf16[8,48,480]{2,1,0:T(8,128)(2,1)} %project.1), calls=%async_computation | async-start | bytes 786432 | tf_op jit(solution)/shard_map/all_to_all | solution.py:759
  19.8 23.4 %collective-permute-start.1 = (bf16[160,1280]{1,0:T(8,128)(2,1)}, bf16[160,1280]{1,0:T(8,128)(2,1)}, u32[]{:S(2)}, u32[]{:S(2)}) collective-permute-start(bf16[160,1280]{1,0:T(8,128)(2,1)} %bitcast.12.rest_0_), channel_id=1, source_target_pairs={{0,4},{1,5},{2,6},{3,7},{4,0},{5,1},{6,2},{7,3},{8,12},{9,13},{10,... | collective-permute-start | bytes 1228808 | tf_op jit(solution)/shard_map/ppermute | solution.py:655
  21.7 21.4 %collective-permute-start.2 = (bf16[160,1280]{1,0:T(8,128)(2,1)}, bf16[160,1280]{1,0:T(8,128)(2,1)}, u32[]{:S(2)}, u32[]{:S(2)}) collective-permute-start(bf16[160,1280]{1,0:T(8,128)(2,1)} %bitcast.12.rest_0_), channel_id=1, source_target_pairs={{0,2},{1,3},{2,0},{3,1},{4,6},{5,7},{6,4},{7,5},{8,10},{9,11},{10,... | collective-permute-start | bytes 1228808 | tf_op jit(solution)/shard_map/ppermute | solution.py:655
  24.0 19.2 %collective-permute-start = (bf16[160,1280]{1,0:T(8,128)(2,1)}, bf16[160,1280]{1,0:T(8,128)(2,1)}, u32[]{:S(2)}, u32[]{:S(2)}) collective-permute-start(bf16[160,1280]{1,0:T(8,128)(2,1)} %dynamic-slice_bitcast_fusion), channel_id=1, source_target_pairs={{0,8},{8,16},{16,24},{24,0},{1,9},{9,17},{17,25},{25,1},{2,10},{10... | collective-permute-start | bytes 1228808 | tf_op jit(solution)/shard_map/ppermute | solution.py:650
  43.2 17.8 %collective-permute-start.3 = (bf16[160,1280]{1,0:T(8,128)(2,1)}, bf16[160,1280]{1,0:T(8,128)(2,1)}, u32[]{:S(2)}, u32[]{:S(2)}) collective-permute-start(bf16[160,1280]{1,0:T(8,128)(2,1)} %collective-permute-done.1.rest_1_), channel_id=1, source_target_pairs={{0,2},{1,3},{2,0},{3,1},{4,6},{5,7},{6,4},{7,5},{8,10},{9,11},{10,... | collective-permute-start | bytes 1228808 | tf_op jit(solution)/shard_map/ppermute | solution.py:655
  43.6 17.4 %collective-permute-start.4 = (bf16[160,1280]{1,0:T(8,128)(2,1)S(1)}, bf16[160,1280]{1,0:T(8,128)(2,1)S(1)}, u32[]{:S(2)}, u32[]{:S(2)}) collective-permute-start(bf16[160,1280]{1,0:T(8,128)(2,1)S(1)} %pad_maximum_fusion.1), channel_id=1, source_target_pairs={{0,4},{1,5},{2,6},{3,7},{4,0},{5,1},{6,2},{7,3},{8,12},{9,13},{10,... | collective-permute-start | bytes 1228808 | tf_op jit(solution)/shard_map/ppermute | solution.py:655
  61.0 20.0 %all-to-all-start.1 = ((bf16[8,48,1408]{2,1,0:T(8,128)(2,1)}), bf16[8,48,1408]{2,1,0:T(8,128)(2,1)}, u32[]{:S(2)}, u32[]{:S(2)}) async-start(bf16[8,48,1408]{2,1,0:T(8,128)(2,1)} %get-tuple-element.71), calls=%async_computation.1 | async-start | bytes 2162688 | tf_op jit(solution)/shard_map/all_to_all | solution.py:782
  65.3 2.0 %collective-permute-start.5 = (bf16[160,1280]{1,0:T(8,128)(2,1)}, bf16[160,1280]{1,0:T(8,128)(2,1)S(1)}, u32[]{:S(2)}, u32[]{:S(2)}) collective-permute-start(bf16[160,1280]{1,0:T(8,128)(2,1)} %bitcast.12.rest_0_), channel_id=1, source_target_pairs={{0,1},{1,0},{2,3},{3,2},{4,5},{5,4},{6,7},{7,6},{8,9},{9,8},{10,11... | collective-permute-start | bytes 1228808 | tf_op jit(solution)/shard_map/ppermute | solution.py:655
  65.6 2.2 %collective-permute-start.6 = (bf16[160,1280]{1,0:T(8,128)(2,1)}, bf16[160,1280]{1,0:T(8,128)(2,1)S(1)}, u32[]{:S(2)}, u32[]{:S(2)}) collective-permute-start(bf16[160,1280]{1,0:T(8,128)(2,1)} %collective-permute-done.1.rest_1_), channel_id=1, source_target_pairs={{0,1},{1,0},{2,3},{3,2},{4,5},{5,4},{6,7},{7,6},{8,9},{9,8},{10,11... | collective-permute-start | bytes 1228808 | tf_op jit(solution)/shard_map/ppermute | solution.py:655
  65.8 2.6 %collective-permute-start.7 = (bf16[160,1280]{1,0:T(8,128)(2,1)}, bf16[160,1280]{1,0:T(8,128)(2,1)S(1)}, u32[]{:S(2)}, u32[]{:S(2)}) collective-permute-start(bf16[160,1280]{1,0:T(8,128)(2,1)} %collective-permute-done.2.rest_2_), channel_id=1, source_target_pairs={{0,1},{1,0},{2,3},{3,2},{4,5},{5,4},{6,7},{7,6},{8,9},{9,8},{10,11... | collective-permute-start | bytes 1228808 | tf_op jit(solution)/shard_map/ppermute | solution.py:655
  66.2 2.9 %collective-permute-start.8 = (bf16[160,1280]{1,0:T(8,128)(2,1)}, bf16[160,1280]{1,0:T(8,128)(2,1)S(1)}, u32[]{:S(2)}, u32[]{:S(2)}) collective-permute-start(bf16[160,1280]{1,0:T(8,128)(2,1)} %collective-permute-done.3.rest_3_), channel_id=1, source_target_pairs={{0,1},{1,0},{2,3},{3,2},{4,5},{5,4},{6,7},{7,6},{8,9},{9,8},{10,11... | collective-permute-start | bytes 1228808 | tf_op jit(solution)/shard_map/ppermute | solution.py:655
  66.4 14.7 %collective-permute-start.11 = (bf16[160,1280]{1,0:T(8,128)(2,1)S(1)}, bf16[160,1280]{1,0:T(8,128)(2,1)}, u32[]{:S(2)}, u32[]{:S(2)}) collective-permute-start(bf16[160,1280]{1,0:T(8,128)(2,1)S(1)} %collective-permute-done.4.rest_1_), channel_id=1, source_target_pairs={{0,8},{8,0},{16,24},{24,16},{1,9},{9,1},{17,25},{25,17},{2,10},{10... | collective-permute-start | bytes 1228808 | tf_op jit(solution)/shard_map/ppermute | solution.py:655
  67.3 21.1 %collective-permute-start.12 = (bf16[320,1280]{1,0:T(8,128)(2,1)S(1)}, bf16[320,1280]{1,0:T(8,128)(2,1)S(1)}, u32[]{:S(2)}, u32[]{:S(2)}) collective-permute-start(bf16[320,1280]{1,0:T(8,128)(2,1)S(1)} %pad_maximum_fusion.rest_0_), channel_id=1, source_target_pairs={{0,1},{1,0},{2,3},{3,2},{4,5},{5,4},{6,7},{7,6},{8,9},{9,8},{10,11... | collective-permute-start | bytes 2457608 | tf_op jit(solution)/shard_map/ppermute | solution.py:655
  72.0 16.4 %collective-permute-start.9 = (bf16[160,1280]{1,0:T(8,128)(2,1)}, bf16[160,1280]{1,0:T(8,128)(2,1)}, u32[]{:S(2)}, u32[]{:S(2)}) collective-permute-start(bf16[160,1280]{1,0:T(8,128)(2,1)} %collective-permute-done.rest_1_), channel_id=1, source_target_pairs={{0,8},{8,16},{16,24},{24,0},{1,9},{9,17},{17,25},{25,1},{2,10},{10... | collective-permute-start | bytes 1228808 | tf_op jit(solution)/shard_map/ppermute | solution.py:650
  81.0 7.4 %collective-permute-start.13 = (bf16[160,1280]{1,0:T(8,128)(2,1)S(1)}, bf16[160,1280]{1,0:T(8,128)(2,1)S(1)}, u32[]{:S(2)}, u32[]{:S(2)}) collective-permute-start(bf16[160,1280]{1,0:T(8,128)(2,1)S(1)} %collective-permute-done.4.rest_1_), channel_id=1, source_target_pairs={{0,1},{1,0},{2,3},{3,2},{4,5},{5,4},{6,7},{7,6},{8,9},{9,8},{10,11... | collective-permute-start | bytes 1228808 | tf_op jit(solution)/shard_map/ppermute | solution.py:655
  81.0 7.4 %collective-permute-start.14 = (bf16[160,1280]{1,0:T(8,128)(2,1)}, bf16[160,1280]{1,0:T(8,128)(2,1)}, u32[]{:S(2)}, u32[]{:S(2)}) collective-permute-start(bf16[160,1280]{1,0:T(8,128)(2,1)} %collective-permute-done.11.rest_2_), channel_id=1, source_target_pairs={{0,1},{1,0},{2,3},{3,2},{4,5},{5,4},{6,7},{7,6},{8,9},{9,8},{10,11... | collective-permute-start | bytes 1228808 | tf_op jit(solution)/shard_map/ppermute | solution.py:655
  86.8 6.4 %collective-permute-start.10 = (bf16[64,1280]{1,0:T(8,128)(2,1)}, bf16[64,1280]{1,0:T(8,128)(2,1)S(1)}, u32[]{:S(2)}, u32[]{:S(2)}) collective-permute-start(bf16[64,1280]{1,0:T(8,128)(2,1)} %get-tuple-element.97.normed_ref), channel_id=1, source_target_pairs={{0,2},{1,3},{2,0},{3,1},{4,6},{5,7},{6,4},{7,5},{8,10},{9,11},{10,... | collective-permute-start | bytes 491528 | tf_op jit(solution)/shard_map/ppermute | solution.py:655
  95.4 15.5 %copy-start.1 = (bf16[4,1280,160]{1,2,0:T(8,128)(2,1)S(1)}, bf16[4,1280,160]{1,2,0:T(8,128)(2,1)}, u32[]{:S(2)}) copy-start(bf16[4,1280,160]{1,2,0:T(8,128)(2,1)} %param.25) | copy-start | bytes 4915204
  95.4 4.9 %collective-permute-start.15 = (bf16[48,1280]{1,0:T(8,128)(2,1)S(1)}, bf16[48,1280]{1,0:T(8,128)(2,1)S(1)}, u32[]{:S(2)}, u32[]{:S(2)}) collective-permute-start(bf16[48,1280]{1,0:T(8,128)(2,1)S(1)} %feed.3), channel_id=1, source_target_pairs={{0,2},{1,3},{2,0},{3,1},{4,6},{5,7},{6,4},{7,5},{8,10},{9,11},{10,... | collective-permute-start | bytes 368648 | tf_op jit(solution)/shard_map/ppermute | solution.py:655
  96.0 14.9 %collective-permute-start.16 = (bf16[160,1280]{1,0:T(8,128)(2,1)}, bf16[160,1280]{1,0:T(8,128)(2,1)S(1)}, u32[]{:S(2)}, u32[]{:S(2)}) collective-permute-start(bf16[160,1280]{1,0:T(8,128)(2,1)} %collective-permute-done.9.rest_2_), channel_id=1, source_target_pairs={{0,8},{8,16},{16,24},{24,0},{1,9},{9,17},{17,25},{25,1},{2,10},{10... | collective-permute-start | bytes 1228808 | tf_op jit(solution)/shard_map/ppermute | solution.py:650
  96.1 14.9 %collective-permute-start.17 = (bf16[32,1280]{1,0:T(8,128)(2,1)S(1)}, bf16[32,1280]{1,0:T(8,128)(2,1)S(1)}, u32[]{:S(2)}, u32[]{:S(2)}) collective-permute-start(bf16[32,1280]{1,0:T(8,128)(2,1)S(1)} %pad_maximum_fusion.2.rest_0_), channel_id=1, source_target_pairs={{0,4},{1,5},{2,6},{3,7},{4,0},{5,1},{6,2},{7,3},{8,12},{9,13},{10,... | collective-permute-start | bytes 245768 | tf_op jit(solution)/shard_map/ppermute | solution.py:655
  112.7 12.8 %all-to-all-start.2 = ((bf16[8,48,640]{2,1,0:T(8,128)(2,1)}), bf16[8,48,640]{2,1,0:T(8,128)(2,1)S(1)}, u32[]{:S(2)}, u32[]{:S(2)}) async-start(bf16[8,48,640]{2,1,0:T(8,128)(2,1)} %draft.1), calls=%async_computation.2 | async-start | bytes 983040 | tf_op jit(solution)/shard_map/all_to_all | solution.py:817
  116.2 6.0 %collective-permute-start.18 = (bf16[160,1280]{1,0:T(8,128)(2,1)}, bf16[160,1280]{1,0:T(8,128)(2,1)S(1)}, u32[]{:S(2)}, u32[]{:S(2)}) collective-permute-start(bf16[160,1280]{1,0:T(8,128)(2,1)} %collective-permute-done.rest_1_), channel_id=1, source_target_pairs={{0,1},{1,0},{2,3},{3,2},{4,5},{5,4},{6,7},{7,6},{8,9},{9,8},{10,11... | collective-permute-start | bytes 1228808 | tf_op jit(solution)/shard_map/ppermute | solution.py:655
  116.6 5.6 %collective-permute-start.19 = (bf16[160,1280]{1,0:T(8,128)(2,1)}, bf16[160,1280]{1,0:T(8,128)(2,1)S(1)}, u32[]{:S(2)}, u32[]{:S(2)}) collective-permute-start(bf16[160,1280]{1,0:T(8,128)(2,1)} %collective-permute-done.9.rest_2_), channel_id=1, source_target_pairs={{0,1},{1,0},{2,3},{3,2},{4,5},{5,4},{6,7},{7,6},{8,9},{9,8},{10,11... | collective-permute-start | bytes 1228808 | tf_op jit(solution)/shard_map/ppermute | solution.py:655
  116.7 5.5 %collective-permute-start.20 = (bf16[160,1280]{1,0:T(8,128)(2,1)S(1)}, bf16[160,1280]{1,0:T(8,128)(2,1)S(1)}, u32[]{:S(2)}, u32[]{:S(2)}) collective-permute-start(bf16[160,1280]{1,0:T(8,128)(2,1)S(1)} %collective-permute-done.16.rest_3_), channel_id=1, source_target_pairs={{0,1},{1,0},{2,3},{3,2},{4,5},{5,4},{6,7},{7,6},{8,9},{9,8},{10,11... | collective-permute-start | bytes 1228808 | tf_op jit(solution)/shard_map/ppermute | solution.py:655
  117.1 2.2 %collective-permute-start.21 = (bf16[32,1280]{1,0:T(8,128)(2,1)S(1)}, bf16[32,1280]{1,0:T(8,128)(2,1)S(1)}, u32[]{:S(2)}, u32[]{:S(2)}) collective-permute-start(bf16[32,1280]{1,0:T(8,128)(2,1)S(1)} %pad_maximum_fusion.2.rest_0_), channel_id=1, source_target_pairs={{0,1},{1,0},{2,3},{3,2},{4,5},{5,4},{6,7},{7,6},{8,9},{9,8},{10,11... | collective-permute-start | bytes 245768 | tf_op jit(solution)/shard_map/ppermute | solution.py:655
  117.3 2.1 %collective-permute-start.22 = (bf16[32,1280]{1,0:T(8,128)(2,1)S(1)}, bf16[32,1280]{1,0:T(8,128)(2,1)S(1)}, u32[]{:S(2)}, u32[]{:S(2)}) collective-permute-start(bf16[32,1280]{1,0:T(8,128)(2,1)S(1)} %collective-permute-done.17.rest_1_), channel_id=1, source_target_pairs={{0,1},{1,0},{2,3},{3,2},{4,5},{5,4},{6,7},{7,6},{8,9},{9,8},{10,11... | collective-permute-start | bytes 245768 | tf_op jit(solution)/shard_map/ppermute | solution.py:655
  (16 other events, 87.9 us)

commit v3 on v2

--- a/solution.py
+++ b/solution.py
@@ -17,6 +17,7 @@
 NEG = -1e30
 LEVEL_START = (0, 1, 5, 15, 30, 48)
 SCALE = 1.0 / math.sqrt(HD)
+EXPONENT = SCALE * math.log2(math.e)
 
 WIN = 256
 WINDOWS = H * HD // WIN
@@ -87,6 +88,22 @@
     for head in range(H):
         total = jnp.where(lane == head, column[head * TREE : (head + 1) * TREE], total)
     return total
+
+
+def split_heads(shares):
+    lane = lax.broadcasted_iota(jnp.int32, shares.shape, 1)
+    high = shares.astype(jnp.bfloat16).astype(jnp.float32)
+    split = jnp.where(lane < LOW, high, jnp.where(lane < 2 * LOW, shares - high, 0.0))
+    return split.astype(jnp.bfloat16)
+
+
+def head_columns(window):
+    head = lax.broadcasted_iota(jnp.int32, (SIDE, WIN), 0)
+    column = lax.broadcasted_iota(jnp.int32, (SIDE, WIN), 1) + window * WIN
+    first = (head & (H - 1)) * HD
+    return jnp.where(
+        (head < 2 * LOW) & (column >= first) & (column < first + HD), 1.0, 0.0
+    ).astype(jnp.bfloat16)
 
 
 def three_parts(wide):
@@ -100,23 +117,9 @@
     ).astype(jnp.bfloat16)
 
 
-def attend_body(
-    pages,
-    requests,
-    info,
-    q_ref,
-    cache_ref,
-    part_ref,
-    copy_ref,
-    held,
-    scores,
-    queries,
-    top,
-    total,
-    numer,
-    load_sem,
-    save_sem,
-):
+def attend_body(pages, requests, cores, info, q_ref, cache_ref, *rest):
+    part_refs, copy_ref, *rest = rest[:cores], *rest[cores:]
+    held, scores, queries, top, total, numer, expand, load_sem, save_sem = rest
     width = q_ref.shape[1]
 
     def place(page):
@@ -132,9 +135,90 @@
             held.at[side, page], copy_ref.at[side, place(page)], save_sem.at[side, page]
         )
 
+    core = info[2 * pages + 2 * requests]
+
     for side in range(2):
         for page in range(pages):
             load(side, page).start()
+    for window in range(WINDOWS):
+        expand[window] = head_columns(window)
+    ones = jnp.ones((2 * SIDE, SIDE), jnp.bfloat16)
+
+    def score(page, many, fresh):
+        for one in range(many):
+            load(0, page + one).wait()
+            save(0, page + one).start()
+        lane = lax.broadcasted_iota(jnp.int32, (TREE, PAGE), 1)
+        products = []
+        for window in range(WINDOWS):
+            keys = held[0, pl.ds(page, many), :, window * WIN : (window + 1) * WIN]
+            products.append(dot_t(queries[window], keys.reshape(many * PAGE, WIN)))
+        keep = [lane < info[pages + page + one] for one in range(many)]
+        for head, piece in enumerate(by_head(products)):
+            span = pl.ds(head * TREE, TREE)
+            largest = None if fresh else top[span]
+            for one in range(many):
+                masked = jnp.where(keep[one], piece[:, one * PAGE : (one + 1) * PAGE], NEG)
+                scores[page + one, span] = masked
+                largest = masked if largest is None else jnp.maximum(largest, masked)
+            top[span] = largest
+
+    def weigh(page, many, fresh):
+        for one in range(many):
+            load(1, page + one).wait()
+            save(1, page + one).start()
+        largest = top[...]
+        weights = [
+            jnp.exp2((scores[page + one] - largest) * EXPONENT) for one in range(many)
+        ]
+        added = functools.reduce(jnp.add, weights)
+        total[...] = added if fresh else total[...] + added
+        low = jnp.concatenate([one.astype(jnp.bfloat16) for one in weights], axis=1)
+        for window in range(WINDOWS):
+            first = 3 * window * TREE
+            values = held[1, pl.ds(page, many), :, window * WIN : (window + 1) * WIN]
+            product = dot_n(low[first : first + SLOTS * TREE], values.reshape(many * PAGE, WIN))
+            numer[window] = product if fresh else numer[window] + product
+
+    def over(step, begin, count):
+        odd = count % 2
+
+        @pl.when(odd == 1)
+        def _():
+            step(begin, 1, True)
+
+        @pl.when(odd == 0)
+        def _():
+            step(begin, 2, True)
+
+        def pair(i, carry):
+            step(begin + 2 * i - odd, 2, False)
+            return carry
+
+        lax.fori_loop(1, (count + odd) // 2, pair, 0)
+
+    def give(part):
+        high = total[...].astype(jnp.bfloat16)
+        rest = (total[...] - high.astype(jnp.float32)).astype(jnp.bfloat16)
+        total[...] = dot_n(jnp.concatenate([high, rest], axis=1), ones)
+        denom = heads_to_lanes(total)
+        inverse = split_heads(1.0 / denom)
+        for window in range(WINDOWS):
+            part[:, window * WIN : (window + 1) * WIN] = (
+                own_lanes(numer[window], window) * dot_n(inverse, expand[window])
+            ).astype(jnp.bfloat16)
+        part[:, width:] = three_parts(heads_to_lanes(top) * SCALE + jnp.log(denom))
+
+    def give_none(part):
+        part[:, :width] = jnp.zeros((TREE, width), jnp.bfloat16)
+        part[:, width:] = three_parts(jnp.full((TREE, SIDE), NEG, jnp.float32))
+
+    def to_output(r, act):
+        for index, part_ref in enumerate(part_refs):
+
+            @pl.when((r + core) % cores == index)
+            def _():
+                act(part_ref.at[r // cores])
 
     def request(r, carry):
         begin = info[2 * pages + r]
@@ -142,67 +226,18 @@
 
         @pl.when(count == 0)
         def _():
-            part_ref[r, :, :width] = jnp.zeros((TREE, width), jnp.bfloat16)
-            part_ref[r, :, width:] = three_parts(jnp.full((TREE, SIDE), NEG, jnp.float32))
+            to_output(r, give_none)
 
         @pl.when(count > 0)
         def _():
             rows = q_ref[pl.ds(pl.multiple_of(r * TREE, 16), TREE), :]
             for window in range(WINDOWS):
                 queries[window] = masked_queries(rows, window)
-            top[...] = jnp.full(top.shape, NEG, jnp.float32)
-
-            def score(i, carry):
-                page = begin + i
-                load(0, page).wait()
-                save(0, page).start()
-                keep = lax.broadcasted_iota(jnp.int32, (TREE, PAGE), 1) < info[pages + page]
-                products = [
-                    dot_t(
-                        queries[window], held[0, page, :, window * WIN : (window + 1) * WIN]
-                    )
-                    for window in range(WINDOWS)
-                ]
-                for head, piece in enumerate(by_head(products)):
-                    span = pl.ds(head * TREE, TREE)
-                    masked = jnp.where(keep, piece * SCALE, NEG)
-                    scores[page, span] = masked
-                    top[span] = jnp.maximum(top[span], masked)
-                return carry
-
-            lax.fori_loop(0, count, score, 0)
+            over(score, begin, count)
             largest = jnp.max(top[...], axis=1, keepdims=True)
             top[...] = jnp.broadcast_to(largest, top.shape)
-            total[...] = jnp.zeros(total.shape, jnp.float32)
-            numer[...] = jnp.zeros(numer.shape, jnp.float32)
-
-            def weigh(i, carry):
-                page = begin + i
-                load(1, page).wait()
-                save(1, page).start()
-                weights = jnp.exp(scores[page] - top[...])
-                total[...] += weights
-                low = weights.astype(jnp.bfloat16)
-                for window in range(WINDOWS):
-                    first = 3 * window * TREE
-                    numer[window] += dot_n(
-                        low[first : first + SLOTS * TREE],
-                        held[1, page, :, window * WIN : (window + 1) * WIN],
-                    )
-                return carry
-
-            lax.fori_loop(0, count, weigh, 0)
-            denom = jnp.sum(total[...], axis=1, keepdims=True)
-            inverse = 1.0 / denom
-            for window in range(WINDOWS):
-                first = 3 * window * TREE
-                scaled = numer[window] * inverse[first : first + SLOTS * TREE]
-                part_ref[r, :, window * WIN : (window + 1) * WIN] = own_lanes(
-                    scaled, window
-                ).astype(jnp.bfloat16)
-            part_ref[r, :, width:] = three_parts(
-                heads_to_lanes(top[:, :1] + jnp.log(denom))
-            )
+            over(weigh, begin, count)
+            to_output(r, give)
 
         return carry
 
@@ -225,24 +260,19 @@
     lax.fori_loop(0, pages, settle, 0)
 
 
-def attend(info, query_all, cache, requests):
+def attend(info, query_all, cache, requests, cores):
     pages = cache.shape[1] // PAGE
     width = query_all.shape[1]
-    return pl.pallas_call(
-        functools.partial(attend_body, pages, requests),
-        out_shape=(
-            jax.ShapeDtypeStruct((requests, TREE, width + SIDE), jnp.bfloat16),
-            jax.ShapeDtypeStruct(cache.shape, cache.dtype),
-        ),
+    parts = jax.ShapeDtypeStruct((requests // cores, TREE, width + SIDE), jnp.bfloat16)
+    return pl.pallas_call(
+        functools.partial(attend_body, pages, requests, cores),
+        out_shape=(parts,) * cores + (jax.ShapeDtypeStruct(cache.shape, cache.dtype),),
         in_specs=[
             pl.BlockSpec(memory_space=pltpu.SMEM),
             pl.BlockSpec(memory_space=pltpu.VMEM),
             HBM,
         ],
-        out_specs=(
-            pl.BlockSpec(memory_space=pltpu.VMEM),
-            HBM,
-        ),
+        out_specs=(pl.BlockSpec(memory_space=pltpu.VMEM),) * cores + (HBM,),
         scratch_shapes=[
             pltpu.VMEM((2, pages, PAGE, width), jnp.bfloat16),
             pltpu.VMEM((pages, H * TREE, PAGE), jnp.float32),
@@ -250,10 +280,11 @@
             pltpu.VMEM((H * TREE, PAGE), jnp.float32),
             pltpu.VMEM((H * TREE, PAGE), jnp.float32),
             pltpu.VMEM((WINDOWS, SLOTS * TREE, WIN), jnp.float32),
+            pltpu.VMEM((WINDOWS, SIDE, WIN), jnp.bfloat16),
             pltpu.SemaphoreType.DMA((2, pages)),
             pltpu.SemaphoreType.DMA((2, pages)),
         ],
-        compiler_params=pltpu.CompilerParams(vmem_limit_bytes=52 * 1024 * 1024),
+        compiler_params=pltpu.CompilerParams(vmem_limit_bytes=51 * 1024 * 1024),
         cost_estimate=pl.CostEstimate(
             flops=4 * pages * PAGE * H * TREE * WIN,
             bytes_accessed=5 * cache.size,
@@ -261,6 +292,49 @@
         ),
         name="attend",
     )(info, query_all, cache)
+
+
+def whole_log(packed):
+    wide = packed.astype(jnp.float32)
+    return wide + (pltpu.roll(wide, SIDE - 32, 1) + pltpu.roll(wide, SIDE - 64, 1))
+
+
+def merge_body(kept_ref, got_ref, out_ref):
+    chips = out_ref.shape[0]
+    width = out_ref.shape[2] - SIDE
+    lane = lax.broadcasted_iota(jnp.int32, (TREE, SIDE), 1)
+    shares = []
+    for chip in range(chips):
+        logs = [whole_log(ref[chip, :, width:]) for ref in (kept_ref, got_ref)]
+        largest = jnp.maximum(*logs)
+        terms = [jnp.exp(one - largest) for one in logs]
+        whole = terms[0] + terms[1]
+        shares += [term / whole for term in terms]
+        joined = jnp.where(lane < 32, largest + jnp.log(whole), 0.0)
+        joined = joined + pltpu.roll(joined, 32, 1) + pltpu.roll(joined, 64, 1)
+        out_ref[chip, :, width:] = three_parts(joined)
+    shares = split_heads(jnp.concatenate(shares, axis=0))
+    for window in range(WINDOWS):
+        span = slice(window * WIN, (window + 1) * WIN)
+        spread = dot_n(shares, head_columns(window))
+        for chip in range(chips):
+            total = 0.0
+            for one, ref in enumerate((kept_ref, got_ref)):
+                first = (2 * chip + one) * TREE
+                total += spread[first : first + TREE] * ref[chip, :, span].astype(jnp.float32)
+            out_ref[chip, :, span] = total.astype(jnp.bfloat16)
+
+
+def merge(kept, got):
+    return pl.pallas_call(
+        merge_body,
+        out_shape=jax.ShapeDtypeStruct(kept.shape, jnp.bfloat16),
+        in_specs=[pl.BlockSpec(memory_space=pltpu.VMEM)] * 2,
+        out_specs=pl.BlockSpec(memory_space=pltpu.VMEM),
+        compiler_params=pltpu.CompilerParams(vmem_limit_bytes=16 * 1024 * 1024),
+        cost_estimate=LIGHT,
+        name="merge",
+    )(kept, got)
 
 
 def project_body(tree_ref, w_ref, out_ref):
@@ -285,6 +359,7 @@
 
 
 def tree_body(info, qkv_ref, parent_ref, part_ref, send_ref):
+    mine = info[info[info.shape[0] - 1]]
     width = qkv_ref.shape[1] // 3
     node_row = lax.broadcasted_iota(jnp.int32, (TREE, TREE), 0)
     node_col = lax.broadcasted_iota(jnp.int32, (TREE, TREE), 1)
@@ -317,7 +392,7 @@
     part_ref[:, width:] = heads_to_lanes(top + jnp.log(denom))
 
     leaf = jnp.where(
-        lax.broadcasted_iota(jnp.int32, (LOW, TREE), 1) == info[0], 1.0, 0.0
+        lax.broadcasted_iota(jnp.int32, (LOW, TREE), 1) == mine, 1.0, 0.0
     ).astype(jnp.bfloat16)
     chosen = dot_n(leaf, steps.astype(jnp.bfloat16))
     earlier = jnp.where(node_row <= node_col, 1.0, 0.0).astype(jnp.bfloat16)
@@ -349,9 +424,9 @@
 
 
 def mix_body(count, info, part_ref, own_ref, tree_ref, sent_ref, *rest):
+    parts = [part_ref.at[block] for block in range(part_ref.shape[0])]
     buffers = rest[:count]
     mid_ref, normed_ref, weights, sems = rest[count:]
-    blocks = part_ref.shape[0]
     width = tree_ref.shape[1]
     copies = []
     for index, buffer in enumerate(buffers):
@@ -363,41 +438,18 @@
     for copy in copies:
         copy.start()
 
-    lane = lax.broadcasted_iota(jnp.int32, (TREE, SIDE), 1)
-    logs = []
-    for block in range(blocks):
-        packed = part_ref[block, :, width:].astype(jnp.float32)
-        logs.append(
-            packed + (pltpu.roll(packed, SIDE - 32, 1) + pltpu.roll(packed, SIDE - 64, 1))
-        )
-    logs.append(own_ref[:, width:])
+    logs = [whole_log(part[:, width:]) for part in parts] + [own_ref[:, width:]]
     largest = functools.reduce(jnp.maximum, logs)
-    shares = [jnp.exp(one - largest) for one in logs]
-    whole = functools.reduce(jnp.add, shares)
-    spread_rows = []
-    for share in shares:
-        share = share / whole
-        high = share.astype(jnp.bfloat16).astype(jnp.float32)
-        spread_rows.append(
-            jnp.where(
-                lane < LOW, high, jnp.where(lane < 2 * LOW, share - high, 0.0)
-            ).astype(jnp.bfloat16)
-        )
-    spread_rows = jnp.concatenate(spread_rows, axis=0)
+    terms = [jnp.exp(one - largest) for one in logs]
+    whole = functools.reduce(jnp.add, terms)
+    shares = split_heads(jnp.concatenate([term / whole for term in terms], axis=0))
     for window in range(WINDOWS):
         span = slice(window * WIN, (window + 1) * WIN)
-        head = lax.broadcasted_iota(jnp.int32, (SIDE, WIN), 0)
-        column = lax.broadcasted_iota(jnp.int32, (SIDE, WIN), 1) + window * WIN
-        first = (head & (H - 1)) * HD
-        expand = jnp.where(
-            (head < 2 * LOW) & (column >= first) & (column < first + HD), 1.0, 0.0
-        ).astype(jnp.bfloat16)
-        spread = dot_n(spread_rows, expand)
-        mixed = spread[blocks * TREE :] * own_ref[:, span]
-        for block in range(blocks):
-            mixed = mixed + spread[block * TREE : (block + 1) * TREE] * part_ref[
-                block, :, span
-            ].astype(jnp.float32)
+        spread = dot_n(shares, head_columns(window))
+        mixed = spread[len(parts) * TREE :] * own_ref[:, span]
+        for index, part in enumerate(parts):
+            first = index * TREE
+            mixed += spread[first : first + TREE] * part[:, span].astype(jnp.float32)
         mid_ref[:, span] = mixed.astype(jnp.bfloat16)
 
     attended = mid_ref[...]
@@ -434,8 +486,9 @@
 
 def feed_body(count, normed_ref, *rest):
     buffers, out_ref = rest[:count], rest[count]
-    up = jnp.concatenate([buffer[: buffer.shape[0] // 2] for buffer in buffers], axis=0)
-    down = jnp.concatenate([buffer[buffer.shape[0] // 2 :] for buffer in buffers], axis=0)
+    half = buffers[0].shape[0] // 2
+    up = jnp.concatenate([buffer[:half] for buffer in buffers], axis=0)
+    down = jnp.concatenate([buffer[half:] for buffer in buffers], axis=0)
     hidden = jax.nn.gelu(dot_t(normed_ref[:TREE], up)).astype(jnp.bfloat16)
     out_ref[...] = dot_n(hidden, down).astype(out_ref.dtype)
 
@@ -499,20 +552,13 @@
 
 def patch_body(heads, count, info, branch_ref, layer_ref, *rest):
     buffers = rest[:count]
-    out_ref, weights, sems = rest[count:]
+    out_ref, weights = rest[count:]
     blocks, _, columns = branch_ref.shape
     piece = columns // heads
-    copies = []
     half = buffers[-1].shape[0]
     for index, buffer in enumerate(buffers):
         first = pl.multiple_of(info[index] * half, 16)
-        copies.append(
-            pltpu.make_async_copy(
-                buffer, weights.at[pl.ds(first, buffer.shape[0])], sems.at[index]
-            )
-        )
-    for copy in copies:
-        copy.start()
+        weights[pl.ds(first, buffer.shape[0])] = buffer[...]
     layer = layer_ref[...].astype(jnp.float32)
     drafted = []
     for head in range(heads):
@@ -524,8 +570,6 @@
             axis=1,
         )
         drafted.append((layer + branch).astype(jnp.bfloat16))
-    for copy in copies:
-        copy.wait()
     product = dot_t(jnp.concatenate(drafted, axis=0), weights[...]).astype(jnp.bfloat16)
     for head in range(heads):
         out_ref[head] = product[head * TREE : (head + 1) * TREE]
@@ -539,14 +583,10 @@
         functools.partial(patch_body, heads, count),
         out_shape=jax.ShapeDtypeStruct((heads, TREE, outputs), jnp.bfloat16),
         in_specs=[pl.BlockSpec(memory_space=pltpu.SMEM)]
-        + [pl.BlockSpec(memory_space=pltpu.VMEM)] * 2
-        + [HBM] * count,
+        + [pl.BlockSpec(memory_space=pltpu.VMEM)] * (2 + count),
         out_specs=pl.BlockSpec(memory_space=pltpu.VMEM),
-        scratch_shapes=[
-            pltpu.VMEM((outputs, width), jnp.bfloat16),
-            pltpu.SemaphoreType.DMA((count,)),
-        ],
-        compiler_params=pltpu.CompilerParams(vmem_limit_bytes=16 * 1024 * 1024),
+        scratch_shapes=[pltpu.VMEM((outputs, width), jnp.bfloat16)],
+        compiler_params=pltpu.CompilerParams(vmem_limit_bytes=24 * 1024 * 1024),
         cost_estimate=LIGHT,
         name="patch",
     )(info, branches, layer_out, *buffers)
@@ -707,12 +747,12 @@
     holds = (owner_hot & used[:, None]).astype(int32)
     count = jnp.sum(holds, axis=0)
     begin = jnp.sum(jnp.where(each[None, :] < each[:, None], count[None, :], 0), axis=1)
-    page_info = jnp.concatenate([order, limit_at, begin, count])
+    my_core = myself % 2 if blocks == 8 else jnp.zeros((), int32)
+    page_info = jnp.concatenate([order, limit_at, begin, count, my_core.reshape(1)])
 
     nodes = jnp.arange(TREE, dtype=int32)
     parent_hot = (parents[0][:, None] == nodes[None, :]).astype(jnp.float32)
-    my_leaf = jnp.sum(jnp.where(each == myself, leaf_row, 0))
-    leaf_info = my_leaf.astype(int32).reshape(1)
+    leaf_info = jnp.concatenate([leaf_row, myself.reshape(1)])
     if blocks == 8:
         mix_info = myself ^ jnp.asarray((0, 4, 2, 6, 1, 5, 3, 7), int32)
         sent_by = myself ^ jnp.asarray((0, 2, 4, 6, 1, 3, 5, 7), int32)
@@ -746,52 +786,55 @@
     if blocks == 8:
         out_y = swap(after(out_rows, projected), "blk", 4)
         out_x = swap(after(out_rows, projected), "blk", 2)
-        few = w_down.shape[0] // 2
-        feed_half = jnp.concatenate(
-            [
-                lax.dynamic_slice_in_dim(one, my_line % 2 * few, few, 0)
-                for one in (w_up.T, w_down)
-            ]
-        )
     half_rows = w_patch.shape[1] // 2
     my_half = lax.dynamic_slice_in_dim(w_patch.T, myself % 2 * half_rows, half_rows, 0)
     ring = [pass_on(after(my_half, projected), "req")]
     projected = lax.all_to_all(projected, "blk", split_axis=0, concat_axis=0, tiled=True)
-    projected, page_info, append_info, leaf_info, mix_info, patch_info, parent_hot = (
-        lax.optimization_barrier(
-            (projected, page_info, append_info, leaf_info, mix_info, patch_info, parent_hot)
-        )
-    )
+    projected, page_info, feed_rows = lax.optimization_barrier((projected, page_info, feed_rows))
     projected = projected.transpose(1, 0, 2).reshape(tree_input.shape[0], -1)
     query_all = lax.all_gather(projected[:, :width], "blk", axis=0, tiled=True)
     query_all, ring[0] = lax.optimization_barrier((query_all, ring[0]))
     if blocks == 8:
         query_all, out_y, out_x = lax.optimization_barrier((query_all, out_y, out_x))
         out_xy = swap(out_y, "blk", 2)
-        feed_y = swap(after(feed_half, query_all), "blk", 4)
-
-    parts, cache_copy = attend(page_info, query_all, cache[0], requests)
+        feed_y = swap(after(feed_rows, query_all), "blk", 4)
+
     if blocks == 8:
-        parts, out_xy, feed_y = lax.optimization_barrier((parts, out_xy, feed_y))
-        feed_z = swap(feed_y, "req", 1)
+        kept, given, cache_copy = attend(page_info, query_all, cache[0], requests, 2)
+        kept, given, out_xy = lax.optimization_barrier((kept, given, out_xy))
+        parts = merge(kept, swap(given, "blk", 1))
+        parts, feed_y = lax.optimization_barrier((parts, feed_y))
         buffers = [out_rows, out_y, out_x, out_xy]
-        buffers += [swap(buffer, "blk", 1) for buffer in after(tuple(buffers), parts)]
+        buffers += [swap(buffer, "blk", 1) for buffer in after(tuple(buffers), kept)]
+        feeds = [feed_rows, feed_y]
+        feeds.append(swap(after(feed_rows, kept), "blk", 1))
+        parts, *buffers = lax.optimization_barrier((parts, *buffers))
+        projected = after(projected, parts)
+        parts = lax.all_to_all(
+            parts,
+            "blk",
+            split_axis=0,
+            concat_axis=0,
+            tiled=True,
+            axis_index_groups=[list(range(core, blocks, 2)) for core in range(2)],
+        )
     else:
+        parts, cache_copy = attend(page_info, query_all, cache[0], requests, 1)
+        parts = lax.all_to_all(parts, "blk", split_axis=0, concat_axis=0, tiled=True)
         buffers = [lax.all_gather(out_rows, "blk", axis=0, tiled=True)]
-    projected, *buffers = lax.optimization_barrier((projected, *buffers))
-    parts = lax.all_to_all(parts, "blk", split_axis=0, concat_axis=0, tiled=True)
+        projected = after(projected, parts[0])
 
     own, sent = tree(leaf_info, projected, parent_hot)
     ring.append(pass_on(after(ring[-1], own), "req"))
-    parts, own = lax.optimization_barrier((parts, own))
+    parts, own, append_info, mix_info, patch_info = lax.optimization_barrier(
+        (parts, own, append_info, mix_info, patch_info)
+    )
     if blocks == 8:
-        feeds = [feed_rows, *after((feed_y, feed_z), own)]
-        feeds += [swap(buffer, "blk", 1) for buffer in feeds]
+        feeds.append(swap(after(feed_y, own), "blk", 1))
     else:
         halves = [lax.all_gather(one, "blk", axis=0, tiled=True) for one in (w_up.T, w_down)]
         feeds = [jnp.concatenate(halves)]
     mid, mid_normed = mix(mix_info, parts, own, tree_input, sent, buffers)
-    mid, ring[-1] = lax.optimization_barrier((mid, ring[-1]))
     sums = [feed(mid_normed, feeds, jnp.float32)]
     if blocks == 8:
         other, sums[0] = lax.optimization_barrier((swap(mid_normed, "blk", 2), sums[0]))

time: 129 us -> 127 us (0.984); the launches traced: 129 us -> 126 us
  Pallas kernels: 37.5 us -> 31.5 us
  waiting for transfers between devices: 22.5 us -> 18.4 us
  starting transfers between devices: 24 us -> 26.8 us
  blocking collectives: 35.5 us -> 37.4 us
  local copies, waits for them, and re-layouts: 5.87 us -> 7.63 us
    all_to_all x1, waiting for transfers between devices: 8.94 us -> 4.77 us  [on_device(): lax.all_to_all(parts, 'blk', split_axis=0, concat_axis=0, tiled=True, axi...]
    pallas_call x1 -> x2, Pallas kernels: 15.7 us -> 13.1 us  [the longest x1 11.8 us: attend(): pl.pallas_call(functools.partial(attend_body, pages, requests, cores), ou...]
    pallas_call x2, Pallas kernels: 4.26 us -> 1.99 us  [feed(): pl.pallas_call(functools.partial(feed_body, len(buffers)), out_shape=jax....]
    ppermute x3, starting transfers between devices: 1.64 us -> 3.65 us  [pass_on(): lax.ppermute(values, axis, [(i, (i + 1) % size) for i in range(size)])]
    unnamed x44 -> x46, local copies, waits for them, and re-layouts: 3.61 us -> 5.32 us
    ppermute x20 -> x19, starting transfers between devices: 11 us -> 12.7 us  [swap(): return lax.ppermute(values, axis, [(i, i ^ bits) for i in range(size)])]
    ppermute x20 -> x19, waiting for transfers between devices: 9.21 us -> 8.39 us  [swap(): return lax.ppermute(values, axis, [(i, i ^ bits) for i in range(size)])]
  transfers between devices with their start and end apart: 26 -> 25, of which waited for: 11 -> 9; matrix products, arithmetic and copies ran while one was open for 4% -> 4% of each run, Pallas kernels for 22% -> 20%
where the time goes in v3:
time: 127 us; the launch traced here: 126 us
  blocking collectives  37.4 us (29%)
  Pallas kernels  31.5 us (25%)
  starting transfers between devices  26.8 us (21%)
  waiting for transfers between devices  18.4 us (14%)
  local copies, waits for them, and re-layouts  7.63 us (6%)
  other arithmetic  3.31 us (3%)
    all_gather x1, blocking collectives, on_device(): query_all = lax.all_gather(projected[:, :width], 'blk', axis=0, tiled=True)  13.8 us
    ppermute x19, starting transfers between devices, swap(): return lax.ppermute(values, axis, [(i, i ^ bits) for i in range(size)])  12.7 us
    all_gather x1, blocking collectives, on_device(): tree_all = lax.all_gather(tree_input, 'blk', axis=0, tiled=True)  12.6 us
    pallas_call x1, Pallas kernels, attend(): pl.pallas_call(functools.partial(attend_body, pages, requests, cores), ou...  11.8 us
    all_gather x1, blocking collectives, on_device(): rows_all = lax.all_gather(draft_rows, 'blk', axis=0, tiled=False)  10.9 us
    ppermute x19, waiting for transfers between devices, swap(): return lax.ppermute(values, axis, [(i, i ^ bits) for i in range(size)])  8.39 us
    unnamed x46, local copies, waits for them, and re-layouts  5.32 us
    pallas_call x1, Pallas kernels, mix(): pl.pallas_call(functools.partial(mix_body, len(buffers)), out_shape=(jax....  4.95 us
  transfers between devices with their start and end apart: 25, of which 9 were waited for; matrix products, arithmetic and copies ran while one was open for 4% of the time, Pallas kernels for 20%

profile of v3, /device:TPU:0, one launch (start us, length us, event | category | flops | bytes accessed | tf_op | source)
XLA Modules:
  0.0 125.8 jit_solution(2731806026977612911)
XLA Ops:
  0.6 12.6 %all_gather.12.tree_ref = bf16[384,1280]{1,0:T(8,128)(2,1)S(1)} all-gather(bf16[48,1280]{1,0:T(8,128)(2,1)} %tree_ref.1), channel_id=1, replica_groups=mesh['req'=4,'blk'=8] {'blk'}, dimensions={0}, use_global_device_ids=true | all-gather | bytes 1105920 | tf_op jit(solution)/shard_map/all_gather | solution.py:782
  13.3 1.3 %copy-done.3 = bf16[1280,480]{0,1:T(8,128)(2,1)S(1)} copy-done((bf16[1280,480]{0,1:T(8,128)(2,1)S(1)}, bf16[1280,480]{0,1:T(8,128)(2,1)}, u32[]{:S(2)}) %copy-start.3) | copy-done | bytes 1228824
  14.6 1.6 %project.1 = bf16[8,48,480]{2,1,0:T(8,128)(2,1)} custom-call(bf16[384,1280]{1,0:T(8,128)(2,1)S(1)} %all_gather.12.tree_ref, bf16[480,1280]{1,0:T(8,128)(2,1)S(1)} %bitcast.34), custom_call_target="tpu_custom_call" | custom-call | tf_op jit(solution)/shard_map/project/pallas_call | solution.py:350
  16.2 3.5 %all-to-all-start = ((bf16[8,48,480]{2,1,0:T(8,128)(2,1)}), bf16[8,48,480]{2,1,0:T(8,128)(2,1)S(1)}, u32[]{:S(2)}, u32[]{:S(2)}) async-start(bf16[8,48,480]{2,1,0:T(8,128)(2,1)} %project.1), calls=%async_computation | async-start | bytes 786432 | tf_op jit(solution)/shard_map/all_to_all | solution.py:792
  19.7 1.9 %collective-permute-start.1 = (bf16[160,1280]{1,0:T(8,128)(2,1)S(1)}, bf16[160,1280]{1,0:T(8,128)(2,1)S(1)}, u32[]{:S(2)}, u32[]{:S(2)}) collective-permute-start(bf16[160,1280]{1,0:T(8,128)(2,1)S(1)} %bitcast.40), channel_id=1, source_target_pairs={{0,4},{1,5},{2,6},{3,7},{4,0},{5,1},{6,2},{7,3},{8,12},{9,13},{10,... | collective-permute-start | bytes 1228808 | tf_op jit(solution)/shard_map/ppermute | solution.py:695
  21.6 1.5 %collective-permute-start.2 = (bf16[160,1280]{1,0:T(8,128)(2,1)S(1)}, bf16[160,1280]{1,0:T(8,128)(2,1)}, u32[]{:S(2)}, u32[]{:S(2)}) collective-permute-start(bf16[160,1280]{1,0:T(8,128)(2,1)S(1)} %bitcast.41), channel_id=1, source_target_pairs={{0,2},{1,3},{2,0},{3,1},{4,6},{5,7},{6,4},{7,5},{8,10},{9,11},{10,... | collective-permute-start | bytes 1228808 | tf_op jit(solution)/shard_map/ppermute | solution.py:695
  23.9 1.6 %collective-permute-start = (bf16[160,1280]{1,0:T(8,128)(2,1)}, bf16[160,1280]{1,0:T(8,128)(2,1)}, u32[]{:S(2)}, u32[]{:S(2)}) collective-permute-start(bf16[160,1280]{1,0:T(8,128)(2,1)} %dynamic-slice_bitcast_fusion), channel_id=1, source_target_pairs={{0,8},{8,16},{16,24},{24,0},{1,9},{9,17},{17,25},{25,1},{2,10},{10... | collective-permute-start | bytes 1228808 | tf_op jit(solution)/shard_map/ppermute | solution.py:690
  26.7 1.1 pad_maximum_fusion.rest_0_
  29.2 13.8 %all_gather.13.q_ref = bf16[384,1280]{1,0:T(8,128)(2,1)S(1)} all-gather(bf16[48,1280]{1,0:T(8,128)(2,1)S(1)} %slice.8), channel_id=1, replica_groups=mesh['req'=4,'blk'=8] {'blk'}, dimensions={0}, use_global_device_ids=true | all-gather | bytes 1105920 | tf_op jit(solution)/shard_map/all_gather | solution.py:795
  43.5 1.8 %collective-permute-start.5 = (bf16[320,1280]{1,0:T(8,128)(2,1)S(1)}, bf16[320,1280]{1,0:T(8,128)(2,1)S(1)}, u32[]{:S(2)}, u32[]{:S(2)}) collective-permute-start(bf16[320,1280]{1,0:T(8,128)(2,1)S(1)} %pad_maximum_fusion.rest_0_), channel_id=1, source_target_pairs={{0,4},{1,5},{2,6},{3,7},{4,0},{5,1},{6,2},{7,3},{8,12},{9,13},{10,... | collective-permute-start | bytes 2457608 | tf_op jit(solution)/shard_map/ppermute | solution.py:695
  45.2 11.8 %attend.1 = (bf16[4,48,1408]{2,1,0:T(8,128)(2,1)S(1)}, bf16[4,48,1408]{2,1,0:T(8,128)(2,1)}, bf16[2,2048,1280]{2,1,0:T(8,128)(2,1)}) custom-call(s32[49]{0:T(128)S(1)} %concatenate.18.info, bf16[384,1280]{1,0:T(8,128)(2,1)S(1)} %all_gather.13.q_ref, bf16[2,2048,1280]{2,1,0:T(8,128)(2,1)} %bitcast.35), custom_call_target="tpu_custom_call" | custom-call | flops 1610612736 | bytes 26214400 | tf_op jit(solution)/shard_map/attend/pallas_call | solution.py:267
  59.9 1.4 %merge.1 = bf16[4,48,1408]{2,1,0:T(8,128)(2,1)} custom-call(bf16[4,48,1408]{2,1,0:T(8,128)(2,1)S(1)} %get-tuple-element.71.kept_ref, bf16[4,48,1408]{2,1,0:T(8,128)(2,1)S(1)} %collective-permute-done.4.got_ref), custom_call_target="tpu_custom_call" | custom-call | tf_op jit(solution)/shard_map/merge/pallas_call | solution.py:329
  61.3 2.5 %collective-permute-done.5.rest_1_ = bf16[320,1280]{1,0:T(8,128)(2,1)S(1)} collective-permute-done((bf16[320,1280]{1,0:T(8,128)(2,1)S(1)}, bf16[320,1280]{1,0:T(8,128)(2,1)S(1)}, u32[]{:S(2)}, u32[]{:S(2)}) %collective-permute-start.5) | collective-permute-done | bytes 819232 | tf_op jit(solution)/shard_map/ppermute | solution.py:695
  63.8 3.5 %all-to-all-start.1 = ((bf16[4,48,1408]{2,1,0:T(8,128)(2,1)}), bf16[4,48,1408]{2,1,0:T(8,128)(2,1)S(1)}, u32[]{:S(2)}, u32[]{:S(2)}) async-start(bf16[4,48,1408]{2,1,0:T(8,128)(2,1)} %merge.1), calls=%async_computation.1 | async-start | bytes 1081344 | tf_op jit(solution)/shard_map/all_to_all | solution.py:813
  67.5 1.5 %tree.1 = (f32[48,1408]{1,0:T(8,128)S(1)}, bf16[16,1280]{1,0:T(8,128)(2,1)S(1)}) custom-call(s32[9]{0:T(128)S(1)} %pad_add_fusion.info, bf16[48,3840]{1,0:T(8,128)(2,1)S(1)} %reshape.195.qkv_ref, f32[48,48]{1,0:T(8,128)S(1)} %fusion.parent_ref), custom_call_target="tpu_custom_call" | custom-call | tf_op jit(solution)/shard_map/tree/pallas_call | solution.py:411
  70.4 4.8 %all-to-all-done.1.part_ref = bf16[4,48,1408]{2,1,0:T(8,128)(2,1)S(1)} async-done(((bf16[4,48,1408]{2,1,0:T(8,128)(2,1)}), bf16[4,48,1408]{2,1,0:T(8,128)(2,1)S(1)}, u32[]{:S(2)}, u32[]{:S(2)}) %all-to-all-start.1) | async-done | bytes 540704 | tf_op jit(solution)/shard_map/all_to_all | solution.py:813
  76.0 1.9 %collective-permute-start.14 = (bf16[160,1280]{1,0:T(8,128)(2,1)}, bf16[160,1280]{1,0:T(8,128)(2,1)S(1)}, u32[]{:S(2)}, u32[]{:S(2)}) collective-permute-start(bf16[160,1280]{1,0:T(8,128)(2,1)} %collective-permute-done.rest_1_), channel_id=1, source_target_pairs={{0,8},{8,16},{16,24},{24,0},{1,9},{9,17},{17,25},{25,1},{2,10},{10... | collective-permute-start | bytes 1228808 | tf_op jit(solution)/shard_map/ppermute | solution.py:690
  77.9 5.0 %mix.1 = (bf16[48,1280]{1,0:T(8,128)(2,1)}, bf16[64,1280]{1,0:T(8,128)(2,1)}) custom-call(s32[8]{0:T(128)} %get-tuple-element.85.info, bf16[4,48,1408]{2,1,0:T(8,128)(2,1)} %copy-done.12, f32[48,1408]{1,0:T(8,128)} %copy-done.6, bf16[48,1280]{1,0:T(8,128)(2,1)} %tree_ref.1, bf16[16,1280]{1,0:T(8,128)(2,1)} %copy-done.7, bf16[160,1280]{1,0:T(8,128)(2,1)} %bitcast.39, ...), custom_call_target="tpu_custom_call" | custom-call | tf_op jit(solution)/shard_map/mix/pallas_call | solution.py:467
  82.9 1.5 %collective-permute-start.10 = (bf16[64,1280]{1,0:T(8,128)(2,1)}, bf16[64,1280]{1,0:T(8,128)(2,1)S(1)}, u32[]{:S(2)}, u32[]{:S(2)}) collective-permute-start(bf16[64,1280]{1,0:T(8,128)(2,1)} %get-tuple-element.98.normed_ref), channel_id=1, source_target_pairs={{0,2},{1,3},{2,0},{3,1},{4,6},{5,7},{6,4},{7,5},{8,10},{9,11},{10,... | collective-permute-start | bytes 491528 | tf_op jit(solution)/shard_map/ppermute | solution.py:695
  85.3 1.0 feed.2.rest_0_
  86.3 3.2 %collective-permute-done.10.normed_ref = bf16[64,1280]{1,0:T(8,128)(2,1)S(1)} collective-permute-done((bf16[64,1280]{1,0:T(8,128)(2,1)}, bf16[64,1280]{1,0:T(8,128)(2,1)S(1)}, u32[]{:S(2)}, u32[]{:S(2)}) %collective-permute-start.10) | collective-permute-done | bytes 163872 | tf_op jit(solution)/shard_map/ppermute | solution.py:695
  89.5 1.0 feed.3
  90.5 1.5 %collective-permute-start.13 = (bf16[48,1280]{1,0:T(8,128)(2,1)S(1)}, bf16[48,1280]{1,0:T(8,128)(2,1)S(1)}, u32[]{:S(2)}, u32[]{:S(2)}) collective-permute-start(bf16[48,1280]{1,0:T(8,128)(2,1)S(1)} %feed.3), channel_id=1, source_target_pairs={{0,2},{1,3},{2,0},{3,1},{4,6},{5,7},{6,4},{7,5},{8,10},{9,11},{10,... | collective-permute-start | bytes 368648 | tf_op jit(solution)/shard_map/ppermute | solution.py:695
  92.0 1.0 collective-permute-done.14.rest_2_
  93.2 1.4 %collective-permute-start.16 = (bf16[32,1280]{1,0:T(8,128)(2,1)S(1)}, bf16[32,1280]{1,0:T(8,128)(2,1)S(1)}, u32[]{:S(2)}, u32[]{:S(2)}) collective-permute-start(bf16[32,1280]{1,0:T(8,128)(2,1)S(1)} %pad_maximum_fusion.1.rest_0_), channel_id=1, source_target_pairs={{0,4},{1,5},{2,6},{3,7},{4,0},{5,1},{6,2},{7,3},{8,12},{9,13},{10,... | collective-permute-start | bytes 245768 | tf_op jit(solution)/shard_map/ppermute | solution.py:695
  96.2 10.9 %all-gather = bf16[384,1280]{1,0:T(8,128)(2,1)S(1)} all-gather(bf16[48,1280]{1,0:T(8,128)(2,1)S(1)} %get-tuple-element.106), channel_id=2, replica_groups=mesh['req'=4,'blk'=8] {'blk'}, dimensions={0}, use_global_device_ids=true | all-gather | bytes 1105920 | tf_op jit(solution)/shard_map/all_gather | solution.py:849
  107.1 1.7 %draft.1 = bf16[8,48,640]{2,1,0:T(8,128)(2,1)} custom-call(bf16[8,48,1280]{2,1,0:T(8,128)(2,1)S(1)} %bitcast.31, bf16[640,1280]{1,0:T(8,128)(2,1)S(1)} %bitcast.33), custom_call_target="tpu_custom_call" | custom-call | tf_op jit(solution)/shard_map/draft/pallas_call | solution.py:542
  108.9 3.5 %all-to-all-start.2 = ((bf16[8,48,640]{2,1,0:T(8,128)(2,1)}), bf16[8,48,640]{2,1,0:T(8,128)(2,1)S(1)}, u32[]{:S(2)}, u32[]{:S(2)}) async-start(bf16[8,48,640]{2,1,0:T(8,128)(2,1)} %draft.1), calls=%async_computation.2 | async-start | bytes 983040 | tf_op jit(solution)/shard_map/all_to_all | solution.py:860
  113.8 1.7 %collective-permute-done.20.rest_2_ = bf16[32,1280]{1,0:T(8,128)(2,1)S(1)} collective-permute-done((bf16[32,1280]{1,0:T(8,128)(2,1)S(1)}, bf16[32,1280]{1,0:T(8,128)(2,1)S(1)}, u32[]{:S(2)}, u32[]{:S(2)}) %collective-permute-start.20) | collective-permute-done | bytes 81952 | tf_op jit(solution)/shard_map/ppermute | solution.py:695
  115.6 2.6 %append.1 = bf16[2,2048,1280]{2,1,0:T(8,128)(2,1)} custom-call(s32[48]{0:T(128)S(1)} %pad_add_fusion.1.info, bf16[32,1280]{1,0:T(8,128)(2,1)S(1)} %pad_maximum_fusion.1.rest_0_, bf16[32,1280]{1,0:T(8,128)(2,1)S(1)} %collective-permute-done.16.rest_1_, bf16[32,1280]{1,0:T(8,128)(2,1)S(1)} %collective-permute-done.20.rest_2_, ...), custom_call_target="tpu_custom_call", output_to_operand_aliasing={{}: (5, {})} | custom-call | tf_op jit(solution)/shard_map/append/pallas_call | solution.py:664
  118.2 3.5 %all-to-all-done.2.branch_ref = bf16[8,48,640]{2,1,0:T(8,128)(2,1)S(1)} async-done(((bf16[8,48,640]{2,1,0:T(8,128)(2,1)}), bf16[8,48,640]{2,1,0:T(8,128)(2,1)S(1)}, u32[]{:S(2)}, u32[]{:S(2)}) %all-to-all-start.2) | async-done | bytes 491552 | tf_op jit(solution)/shard_map/all_to_all | solution.py:860
  122.6 3.2 %patch.1 = bf16[4,48,1280]{2,1,0:T(8,128)(2,1)} custom-call(s32[7]{0:T(128)S(1)} %pad_add_fusion.2.info, bf16[8,48,640]{2,1,0:T(8,128)(2,1)S(1)} %all-to-all-done.2.branch_ref, bf16[48,1280]{1,0:T(8,128)(2,1)S(1)} %copy-done.10, bf16[320,1280]{1,0:T(8,128)(2,1)S(1)} %bitcast.32, bf16[160,1280]{1,0:T(8,128)(2,1)} %collective-permute-done.rest_1_, ...), custom_call_target="tpu_custom_call" | custom-call | tf_op jit(solution)/shard_map/patch/pallas_call | solution.py:582
  (118 shorter events, 14.3 us)
Async XLA Ops:
  14.6 12.0 %copy-start.21 = (s32[1,8]{1,0:T(1,128)S(1)}, s32[1,8]{1,0:T(1,128)}, u32[]{:S(2)}) copy-start(s32[1,8]{1,0:T(1,128)} %param.20) | copy-start | bytes 100
  14.6 12.0 %copy-start.22 = (s32[4]{0:T(128)S(1)}, s32[4]{0:T(128)}, u32[]{:S(2)}) copy-start(s32[4]{0:T(128)} %constant.138.clone) | copy-start | bytes 52
  14.6 12.1 %copy-start.15 = (bf16[160,1280]{1,0:T(8,128)(2,1)S(1)}, bf16[160,1280]{1,0:T(8,128)(2,1)}, u32[]{:S(2)}) copy-start(bf16[160,1280]{1,0:T(8,128)(2,1)} %param.24) | copy-start | bytes 1228804
  16.2 12.2 %all-to-all-start = ((bf16[8,48,480]{2,1,0:T(8,128)(2,1)}), bf16[8,48,480]{2,1,0:T(8,128)(2,1)S(1)}, u32[]{:S(2)}, u32[]{:S(2)}) async-start(bf16[8,48,480]{2,1,0:T(8,128)(2,1)} %project.1), calls=%async_computation | async-start | bytes 786432 | tf_op jit(solution)/shard_map/all_to_all | solution.py:792
  19.7 23.4 %collective-permute-start.1 = (bf16[160,1280]{1,0:T(8,128)(2,1)S(1)}, bf16[160,1280]{1,0:T(8,128)(2,1)S(1)}, u32[]{:S(2)}, u32[]{:S(2)}) collective-permute-start(bf16[160,1280]{1,0:T(8,128)(2,1)S(1)} %bitcast.40), channel_id=1, source_target_pairs={{0,4},{1,5},{2,6},{3,7},{4,0},{5,1},{6,2},{7,3},{8,12},{9,13},{10,... | collective-permute-start | bytes 1228808 | tf_op jit(solution)/shard_map/ppermute | solution.py:695
  21.6 21.4 %collective-permute-start.2 = (bf16[160,1280]{1,0:T(8,128)(2,1)S(1)}, bf16[160,1280]{1,0:T(8,128)(2,1)}, u32[]{:S(2)}, u32[]{:S(2)}) collective-permute-start(bf16[160,1280]{1,0:T(8,128)(2,1)S(1)} %bitcast.41), channel_id=1, source_target_pairs={{0,2},{1,3},{2,0},{3,1},{4,6},{5,7},{6,4},{7,5},{8,10},{9,11},{10,... | collective-permute-start | bytes 1228808 | tf_op jit(solution)/shard_map/ppermute | solution.py:695
  23.9 19.2 %collective-permute-start = (bf16[160,1280]{1,0:T(8,128)(2,1)}, bf16[160,1280]{1,0:T(8,128)(2,1)}, u32[]{:S(2)}, u32[]{:S(2)}) collective-permute-start(bf16[160,1280]{1,0:T(8,128)(2,1)} %dynamic-slice_bitcast_fusion), channel_id=1, source_target_pairs={{0,8},{8,16},{16,24},{24,0},{1,9},{9,17},{17,25},{25,1},{2,10},{10... | collective-permute-start | bytes 1228808 | tf_op jit(solution)/shard_map/ppermute | solution.py:690
  43.0 14.0 %copy-start.14 = (bf16[160,1280]{1,0:T(8,128)(2,1)}, bf16[160,1280]{1,0:T(8,128)(2,1)S(1)}, u32[]{:S(2)}) copy-start(bf16[160,1280]{1,0:T(8,128)(2,1)S(1)} %collective-permute-done.1.rest_1_) | copy-start | bytes 1228804
  43.0 14.0 %collective-permute-start.3 = (bf16[160,1280]{1,0:T(8,128)(2,1)S(1)}, bf16[160,1280]{1,0:T(8,128)(2,1)}, u32[]{:S(2)}, u32[]{:S(2)}) collective-permute-start(bf16[160,1280]{1,0:T(8,128)(2,1)S(1)} %collective-permute-done.1.rest_1_), channel_id=1, source_target_pairs={{0,2},{1,3},{2,0},{3,1},{4,6},{5,7},{6,4},{7,5},{8,10},{9,11},{10,... | collective-permute-start | bytes 1228808 | tf_op jit(solution)/shard_map/ppermute | solution.py:695
  43.5 20.3 %collective-permute-start.5 = (bf16[320,1280]{1,0:T(8,128)(2,1)S(1)}, bf16[320,1280]{1,0:T(8,128)(2,1)S(1)}, u32[]{:S(2)}, u32[]{:S(2)}) collective-permute-start(bf16[320,1280]{1,0:T(8,128)(2,1)S(1)} %pad_maximum_fusion.rest_0_), channel_id=1, source_target_pairs={{0,4},{1,5},{2,6},{3,7},{4,0},{5,1},{6,2},{7,3},{8,12},{9,13},{10,... | collective-permute-start | bytes 2457608 | tf_op jit(solution)/shard_map/ppermute | solution.py:695
  45.2 14.2 %copy-start.19 = (s32[8]{0:T(128)S(1)}, s32[8]{0:T(128)}, u32[]{:S(2)}) copy-start(s32[8]{0:T(128)} %constant.136.clone) | copy-start | bytes 100
  45.2 14.2 %copy-start.20 = (s32[8]{0:T(128)S(1)}, s32[8]{0:T(128)}, u32[]{:S(2)}) copy-start(s32[8]{0:T(128)} %constant.137.clone) | copy-start | bytes 100
  57.0 2.2 %collective-permute-start.4 = (bf16[4,48,1408]{2,1,0:T(8,128)(2,1)}, bf16[4,48,1408]{2,1,0:T(8,128)(2,1)S(1)}, u32[]{:S(2)}, u32[]{:S(2)}) collective-permute-start(bf16[4,48,1408]{2,1,0:T(8,128)(2,1)} %get-tuple-element.72), channel_id=1, source_target_pairs={{0,1},{1,0},{2,3},{3,2},{4,5},{5,4},{6,7},{7,6},{8,9},{9,8},{10,11... | collective-permute-start | bytes 1622024 | tf_op jit(solution)/shard_map/ppermute | solution.py:695
  58.2 5.6 %collective-permute-start.6 = (bf16[160,1280]{1,0:T(8,128)(2,1)}, bf16[160,1280]{1,0:T(8,128)(2,1)}, u32[]{:S(2)}, u32[]{:S(2)}) collective-permute-start(bf16[160,1280]{1,0:T(8,128)(2,1)} %bitcast.38), channel_id=1, source_target_pairs={{0,1},{1,0},{2,3},{3,2},{4,5},{5,4},{6,7},{7,6},{8,9},{9,8},{10,11... | collective-permute-start | bytes 1228808 | tf_op jit(solution)/shard_map/ppermute | solution.py:695
  58.7 5.1 %collective-permute-start.7 = (bf16[160,1280]{1,0:T(8,128)(2,1)}, bf16[160,1280]{1,0:T(8,128)(2,1)}, u32[]{:S(2)}, u32[]{:S(2)}) collective-permute-start(bf16[160,1280]{1,0:T(8,128)(2,1)} %copy-done.14), channel_id=1, source_target_pairs={{0,1},{1,0},{2,3},{3,2},{4,5},{5,4},{6,7},{7,6},{8,9},{9,8},{10,11... | collective-permute-start | bytes 1228808 | tf_op jit(solution)/shard_map/ppermute | solution.py:695
  58.8 5.0 %collective-permute-start.8 = (bf16[160,1280]{1,0:T(8,128)(2,1)}, bf16[160,1280]{1,0:T(8,128)(2,1)}, u32[]{:S(2)}, u32[]{:S(2)}) collective-permute-start(bf16[160,1280]{1,0:T(8,128)(2,1)} %collective-permute-done.2.rest_2_), channel_id=1, source_target_pairs={{0,1},{1,0},{2,3},{3,2},{4,5},{5,4},{6,7},{7,6},{8,9},{9,8},{10,11... | collective-permute-start | bytes 1228808 | tf_op jit(solution)/shard_map/ppermute | solution.py:695
  59.3 4.5 %collective-permute-start.9 = (bf16[160,1280]{1,0:T(8,128)(2,1)}, bf16[160,1280]{1,0:T(8,128)(2,1)}, u32[]{:S(2)}, u32[]{:S(2)}) collective-permute-start(bf16[160,1280]{1,0:T(8,128)(2,1)} %collective-permute-done.3.rest_3_), channel_id=1, source_target_pairs={{0,1},{1,0},{2,3},{3,2},{4,5},{5,4},{6,7},{7,6},{8,9},{9,8},{10,11... | collective-permute-start | bytes 1228808 | tf_op jit(solution)/shard_map/ppermute | solution.py:695
  63.8 11.4 %all-to-all-start.1 = ((bf16[4,48,1408]{2,1,0:T(8,128)(2,1)}), bf16[4,48,1408]{2,1,0:T(8,128)(2,1)S(1)}, u32[]{:S(2)}, u32[]{:S(2)}) async-start(bf16[4,48,1408]{2,1,0:T(8,128)(2,1)} %merge.1), calls=%async_computation.1 | async-start | bytes 1081344 | tf_op jit(solution)/shard_map/all_to_all | solution.py:813
  67.5 16.9 %collective-permute-start.11 = (bf16[320,1280]{1,0:T(8,128)(2,1)S(1)}, bf16[320,1280]{1,0:T(8,128)(2,1)S(1)}, u32[]{:S(2)}, u32[]{:S(2)}) collective-permute-start(bf16[320,1280]{1,0:T(8,128)(2,1)S(1)} %pad_maximum_fusion.rest_0_), channel_id=1, source_target_pairs={{0,1},{1,0},{2,3},{3,2},{4,5},{5,4},{6,7},{7,6},{8,9},{9,8},{10,11... | collective-permute-start | bytes 2457608 | tf_op jit(solution)/shard_map/ppermute | solution.py:695
  76.0 8.4 %collective-permute-start.12 = (bf16[320,1280]{1,0:T(8,128)(2,1)S(1)}, bf16[320,1280]{1,0:T(8,128)(2,1)S(1)}, u32[]{:S(2)}, u32[]{:S(2)}) collective-permute-start(bf16[320,1280]{1,0:T(8,128)(2,1)S(1)} %collective-permute-done.5.rest_1_), channel_id=1, source_target_pairs={{0,1},{1,0},{2,3},{3,2},{4,5},{5,4},{6,7},{7,6},{8,9},{9,8},{10,11... | collective-permute-start | bytes 2457608 | tf_op jit(solution)/shard_map/ppermute | solution.py:695
  76.0 17.1 %collective-permute-start.14 = (bf16[160,1280]{1,0:T(8,128)(2,1)}, bf16[160,1280]{1,0:T(8,128)(2,1)S(1)}, u32[]{:S(2)}, u32[]{:S(2)}) collective-permute-start(bf16[160,1280]{1,0:T(8,128)(2,1)} %collective-permute-done.rest_1_), channel_id=1, source_target_pairs={{0,8},{8,16},{16,24},{24,0},{1,9},{9,17},{17,25},{25,1},{2,10},{10... | collective-permute-start | bytes 1228808 | tf_op jit(solution)/shard_map/ppermute | solution.py:690
  82.9 6.6 %collective-permute-start.10 = (bf16[64,1280]{1,0:T(8,128)(2,1)}, bf16[64,1280]{1,0:T(8,128)(2,1)S(1)}, u32[]{:S(2)}, u32[]{:S(2)}) collective-permute-start(bf16[64,1280]{1,0:T(8,128)(2,1)} %get-tuple-element.98.normed_ref), channel_id=1, source_target_pairs={{0,2},{1,3},{2,0},{3,1},{4,6},{5,7},{6,4},{7,5},{8,10},{9,11},{10,... | collective-permute-start | bytes 491528 | tf_op jit(solution)/shard_map/ppermute | solution.py:695
  90.5 16.6 %copy-start.2 = (bf16[4,1280,160]{1,2,0:T(8,128)(2,1)S(1)}, bf16[4,1280,160]{1,2,0:T(8,128)(2,1)}, u32[]{:S(2)}) copy-start(bf16[4,1280,160]{1,2,0:T(8,128)(2,1)} %param.25) | copy-start | bytes 4915204
  90.5 4.9 %collective-permute-start.13 = (bf16[48,1280]{1,0:T(8,128)(2,1)S(1)}, bf16[48,1280]{1,0:T(8,128)(2,1)S(1)}, u32[]{:S(2)}, u32[]{:S(2)}) collective-permute-start(bf16[48,1280]{1,0:T(8,128)(2,1)S(1)} %feed.3), channel_id=1, source_target_pairs={{0,2},{1,3},{2,0},{3,1},{4,6},{5,7},{6,4},{7,5},{8,10},{9,11},{10,... | collective-permute-start | bytes 368648 | tf_op jit(solution)/shard_map/ppermute | solution.py:695
  93.1 14.1 %collective-permute-start.15 = (bf16[160,1280]{1,0:T(8,128)(2,1)S(1)}, bf16[160,1280]{1,0:T(8,128)(2,1)S(1)}, u32[]{:S(2)}, u32[]{:S(2)}) collective-permute-start(bf16[160,1280]{1,0:T(8,128)(2,1)S(1)} %collective-permute-done.14.rest_2_), channel_id=1, source_target_pairs={{0,8},{8,16},{16,24},{24,0},{1,9},{9,17},{17,25},{25,1},{2,10},{10... | collective-permute-start | bytes 1228808 | tf_op jit(solution)/shard_map/ppermute | solution.py:690
  93.2 13.9 %collective-permute-start.16 = (bf16[32,1280]{1,0:T(8,128)(2,1)S(1)}, bf16[32,1280]{1,0:T(8,128)(2,1)S(1)}, u32[]{:S(2)}, u32[]{:S(2)}) collective-permute-start(bf16[32,1280]{1,0:T(8,128)(2,1)S(1)} %pad_maximum_fusion.1.rest_0_), channel_id=1, source_target_pairs={{0,4},{1,5},{2,6},{3,7},{4,0},{5,1},{6,2},{7,3},{8,12},{9,13},{10,... | collective-permute-start | bytes 245768 | tf_op jit(solution)/shard_map/ppermute | solution.py:695
  108.9 12.8 %all-to-all-start.2 = ((bf16[8,48,640]{2,1,0:T(8,128)(2,1)}), bf16[8,48,640]{2,1,0:T(8,128)(2,1)S(1)}, u32[]{:S(2)}, u32[]{:S(2)}) async-start(bf16[8,48,640]{2,1,0:T(8,128)(2,1)} %draft.1), calls=%async_computation.2 | async-start | bytes 983040 | tf_op jit(solution)/shard_map/all_to_all | solution.py:860
  112.4 5.8 %collective-permute-start.17 = (bf16[160,1280]{1,0:T(8,128)(2,1)}, bf16[160,1280]{1,0:T(8,128)(2,1)S(1)}, u32[]{:S(2)}, u32[]{:S(2)}) collective-permute-start(bf16[160,1280]{1,0:T(8,128)(2,1)} %collective-permute-done.rest_1_), channel_id=1, source_target_pairs={{0,1},{1,0},{2,3},{3,2},{4,5},{5,4},{6,7},{7,6},{8,9},{9,8},{10,11... | collective-permute-start | bytes 1228808 | tf_op jit(solution)/shard_map/ppermute | solution.py:695
  112.8 5.4 %collective-permute-start.18 = (bf16[160,1280]{1,0:T(8,128)(2,1)S(1)}, bf16[160,1280]{1,0:T(8,128)(2,1)S(1)}, u32[]{:S(2)}, u32[]{:S(2)}) collective-permute-start(bf16[160,1280]{1,0:T(8,128)(2,1)S(1)} %copy-done.5), channel_id=1, source_target_pairs={{0,1},{1,0},{2,3},{3,2},{4,5},{5,4},{6,7},{7,6},{8,9},{9,8},{10,11... | collective-permute-start | bytes 1228808 | tf_op jit(solution)/shard_map/ppermute | solution.py:695
  112.9 5.3 %collective-permute-start.19 = (bf16[160,1280]{1,0:T(8,128)(2,1)S(1)}, bf16[160,1280]{1,0:T(8,128)(2,1)S(1)}, u32[]{:S(2)}, u32[]{:S(2)}) collective-permute-start(bf16[160,1280]{1,0:T(8,128)(2,1)S(1)} %collective-permute-done.15.rest_3_), channel_id=1, source_target_pairs={{0,1},{1,0},{2,3},{3,2},{4,5},{5,4},{6,7},{7,6},{8,9},{9,8},{10,11... | collective-permute-start | bytes 1228808 | tf_op jit(solution)/shard_map/ppermute | solution.py:695
  113.3 2.2 %collective-permute-start.20 = (bf16[32,1280]{1,0:T(8,128)(2,1)S(1)}, bf16[32,1280]{1,0:T(8,128)(2,1)S(1)}, u32[]{:S(2)}, u32[]{:S(2)}) collective-permute-start(bf16[32,1280]{1,0:T(8,128)(2,1)S(1)} %pad_maximum_fusion.1.rest_0_), channel_id=1, source_target_pairs={{0,1},{1,0},{2,3},{3,2},{4,5},{5,4},{6,7},{7,6},{8,9},{9,8},{10,11... | collective-permute-start | bytes 245768 | tf_op jit(solution)/shard_map/ppermute | solution.py:695
  113.5 2.1 %collective-permute-start.21 = (bf16[32,1280]{1,0:T(8,128)(2,1)S(1)}, bf16[32,1280]{1,0:T(8,128)(2,1)S(1)}, u32[]{:S(2)}, u32[]{:S(2)}) collective-permute-start(bf16[32,1280]{1,0:T(8,128)(2,1)S(1)} %collective-permute-done.16.rest_1_), channel_id=1, source_target_pairs={{0,1},{1,0},{2,3},{3,2},{4,5},{5,4},{6,7},{7,6},{8,9},{9,8},{10,11... | collective-permute-start | bytes 245768 | tf_op jit(solution)/shard_map/ppermute | solution.py:695
  (16 other events, 75.8 us)
